TPU v7x, 256 devices: a whole 4x4x8 slice. The times are simulated.
256 devices in a mesh: win: 8 (over z_lo, x), tile: 32 (over y, z_hi, core).
Axes of the slice: x: 4, y: 4, z: 8 (z_hi: 4, z_lo: 2; z = z_hi * 2 + z_lo), core: 2. Of those that a mesh axis runs over, the one named last changes fastest.
Arguments:
- adjoint: float32 [8, 4, 32, 512, 320], P('win', None, None, 'tile'), may hold values from -6 to 6
- velocity: float32 [8, 2, 2, 32, 512, 320], P('win', None, None, None, 'tile'), may hold values from -0.5 to 0.5
- kappa: float32 [8, 2, 32, 512, 320], P('win', None, None, 'tile'), may hold values from 0.02 to 0.2
Outputs:
- result: float32 [8, 4, 32, 512, 320], P('win', None, None, 'tile')
All inputs are finite; a program needn't handle non-finite values.
Results may differ from a plain program's by a relative error of at most 0.00002.
Values sent between devices are 32-bit elements; how exact they have to be, the bound alone decides.
No kernel may reach another device: no remote copies, remote signals or barrier semaphores. Data moves between devices by JAX's collectives and lax.ppermute only.
A program may use at most 128 MiB of HBM per device.

v0:
```python
import jax
import jax.numpy as jnp
from jax import lax
from jax.sharding import PartitionSpec as P


def padded(block, sides, width):
    for axis, dim in sides:
        count = lax.axis_size(axis)
        forward = [(i, i + 1) for i in range(count - 1)]
        forward.append((count - 1, 0))
        backward = [(target, source) for source, target in forward]
        low = lax.ppermute(
            lax.slice_in_dim(block, block.shape[dim] - width, None, axis=dim), axis, forward
        )
        high = lax.ppermute(lax.slice_in_dim(block, 0, width, axis=dim), axis, backward)
        block = jnp.concatenate([low, block, high], axis=dim)
    return block


def passed_along(value, axis, steps):
    count = lax.axis_size(axis)
    initial, last = (max(0, -steps), min(count, count - steps))
    return lax.ppermute(value, axis, [(source, source + steps) for source in range(initial, last)])


def lat_pair(field):
    edge = jnp.zeros_like(field[..., :1])
    upper = jnp.concatenate([field[..., 1:], edge], axis=-1)
    lower = jnp.concatenate([edge, field[..., :-1]], axis=-1)
    return (upper, lower)


def combine(state, carried, spread, lateral, width):
    east = carried[..., 3 : width + 3, :]
    west = carried[..., 1 : width + 1, :]
    far_east = carried[..., 4 : width + 4, :]
    far_west = carried[..., 0:width, :]
    along = (8.0 * (east - west) - (far_east - far_west)) / 12.0
    centre = spread[..., 2 : width + 2, :]
    spread_up, spread_down = lat_pair(centre)
    diffuse = (
        spread[..., 3 : width + 3, :]
        + spread[..., 1 : width + 1, :]
        + spread_up
        + spread_down
        - 4.0 * centre
    )
    lat_up, lat_down = lat_pair(lateral)
    return state + along + 0.5 * (lat_up - lat_down) + diffuse


def run_model(state, velocity, kappa):
    sections = velocity.shape[0]
    width = state.shape[2]
    for section in range(sections - 1, -1, -1):
        carried = velocity[section, 0] * state
        spread = kappa[section] * state
        lateral = velocity[section, 1] * state
        rimmed = padded(jnp.stack([carried, spread]), (("tile", 3),), 2)
        state = combine(state, rimmed[0], rimmed[1], lateral, width)
    return state


def per_device(adjoint, velocity, kappa):
    own_state = adjoint[0]
    own_velocity = velocity[0]
    own_kappa = kappa[0]
    later = passed_along(run_model(own_state, own_velocity, own_kappa), "win", -1)
    return (own_state - later)[None]


def solution(mesh):
    return jax.shard_map(
        per_device,
        mesh=mesh,
        in_specs=(
            P("win", None, None, "tile", None),
            P("win", None, None, None, "tile", None),
            P("win", None, None, "tile", None),
        ),
        out_specs=P("win", None, None, "tile", None),
        check_vma=False,
    )
```

profile of v0, /device:TPU:6, one launch (start us, length us, event | category | flops | bytes accessed | tf_op | source)
XLA Modules:
  0.0 188.9 jit_solution(17991624390876638044)
XLA Ops:
  0.0 4.2 %slice_bitcast_fusion.5 = (f32[32,16,320]{2,1,0:T(8,128)}, f32[32,16,320]{2,1,0:T(8,128)}, f32[32,16,320]{2,1,0:T(8,128)S(1)}, f32[32,16,320]{2,1,0:T(8,128)S(1)...) fusion(f32[2,2,32,16,320]{4,3,2,1,0:T(8,128)} %bitcast.34, f32[1,2,32,16,320]{4,3,2,1,0:T(8,128)} %param.5), kind=kLoop, calls=%fused_computation.43 | loop fusion | bytes 7864320 | tf_op jit(solution)/shard_map/mul | solution.py:57
  4.2 0.0 copy-done.2
  4.2 0.6 broadcast_multiply_fusion.2
  4.8 0.8 pad_maximum_fusion.5
  5.6 0.1 collective-permute-start
  5.6 8.3 %collective-permute-start.1 = (f32[2,4,32,2,320]{4,3,2,1,0:T(2,128)S(1)}, f32[2,4,32,2,320]{4,3,2,1,0:T(2,128)S(1)}, u32[]{:S(2)}, u32[]{:S(2)}) collective-permute-start(f32[2,4,32,2,320]{4,3,2,1,0:T(2,128)S(1)} %get-tuple-element.14), channel_id=1, source_target_pairs={{1,0},{2,1},{3,2},{4,3},{5,4},{6,5},{7,6},{8,7},{9,8},{10,9},{11,1... | collective-permute-start | bytes 1966088 | tf_op jit(solution)/shard_map/ppermute | solution.py:16
  13.9 0.3 bitcast_multiply_fusion
  14.2 3.7 %fusion.23 = (f32[4,32,16,319]{3,2,1,0:T(8,128)}, f32[4,32,16,319]{3,2,1,0:T(8,128)}) fusion(f32[4,32,16,320]{3,2,1,0:T(8,128)S(1)} %bitcast_multiply_fusion), kind=kLoop, calls=%fused_computation.53 | loop fusion | bytes 10452992 | tf_op jit(solution)/shard_map/slice | solution.py:29
  17.9 8.5 %collective-permute-done = f32[2,4,32,2,320]{4,3,2,1,0:T(2,128)S(1)} collective-permute-done((f32[2,4,32,2,320]{4,3,2,1,0:T(2,128)S(1)}, f32[2,4,32,2,320]{4,3,2,1,0:T(2,128)S(1)}, u32[]{:S(2)}, u32[]{:S(2)}) %collective-permute-start) | collective-permute-done | bytes 655392 | tf_op jit(solution)/shard_map/ppermute | solution.py:13
  26.5 5.4 %collective-permute-done.1 = f32[2,4,32,2,320]{4,3,2,1,0:T(2,128)S(1)} collective-permute-done((f32[2,4,32,2,320]{4,3,2,1,0:T(2,128)S(1)}, f32[2,4,32,2,320]{4,3,2,1,0:T(2,128)S(1)}, u32[]{:S(2)}, u32[]{:S(2)}) %collective-permute-start.1) | collective-permute-done | bytes 655392 | tf_op jit(solution)/shard_map/ppermute | solution.py:16
  31.9 2.3 %pad_maximum_fusion = f32[2,4,32,20,320]{4,3,2,1,0:T(8,128)S(1)} fusion(f32[2,4,32,2,320]{4,3,2,1,0:T(2,128)S(1)} %collective-permute-done.1, f32[1,4,32,16,320]{4,3,2,1,0:T(8,128)S(1)} %get-tuple-element.30, f32[1,4,32,16,320]{4,3,2,1,0:T(8,128)S(1)} %get-tuple-element.29, f32[2,4,32,2,320]{4,3,2,1,0:T(2,128)S(1)} %collective-permute-done), kind=kLoop, calls=%fused_computation | loop fusion | flops 4915200 | bytes 13107200 | tf_op jit(solution)/shard_map/concatenate | solution.py:17
  34.2 2.7 %slice_bitcast_fusion.3 = (f32[4,32,20,320]{3,2,1,0:T(8,128)}, f32[4,32,20,320]{3,2,1,0:T(8,128)S(1)}) fusion(f32[2,4,32,20,320]{4,3,2,1,0:T(8,128)S(1)} %pad_maximum_fusion), kind=kLoop, calls=%fused_computation.5 | loop fusion | bytes 13107200 | tf_op jit(solution)/shard_map/squeeze | solution.py:61
  36.9 4.2 %fusion.21 = (f32[4,32,16,319]{3,2,1,0:T(8,128)}, f32[4,32,16,319]{3,2,1,0:T(8,128)}) fusion(f32[4,32,20,320]{3,2,1,0:T(8,128)S(1)} %get-tuple-element.10), kind=kLoop, calls=%fused_computation.51 | loop fusion | bytes 10452992 | tf_op jit(solution)/shard_map/slice | solution.py:29
  41.1 0.0 copy-done.1
  41.1 18.6 %broadcast_multiply_fusion = (f32[4,32,16,320]{3,2,1,0:T(8,128)}, f32[4,32,16,320]{3,2,1,0:T(8,128)}) fusion(f32[32,16,320]{2,1,0:T(8,128)} %get-tuple-element.24, f32[4,32,20,320]{3,2,1,0:T(8,128)} %copy-done.1, f32[4,32,16,319]{3,2,1,0:T(8,128)} %get-tuple-element.18, f32[4,32,16,319]{3,2,1,0:T(8,128)} %get-tuple-element.17, ...), kind=kLoop, calls=%fused_computation.37 | loop fusion | flops 10485760 | bytes 37322752 | tf_op jit(solution)/shard_map/mul | solution.py:59
  59.7 2.9 %multiply_bitcast_fusion.1 = (f32[1,4,32,16,320]{4,3,2,1,0:T(8,128)S(1)}, f32[1,4,32,16,320]{4,3,2,1,0:T(8,128)S(1)}) fusion(f32[4,32,16,320]{3,2,1,0:T(8,128)} %get-tuple-element.6, f32[32,16,320]{2,1,0:T(8,128)} %get-tuple-element.23, f32[32,16,320]{2,1,0:T(8,128)} %get-tuple-element.34), kind=kLoop, calls=%fused_computation.36 | loop fusion | flops 1310720 | bytes 9175040 | tf_op jit(solution)/shard_map/stack | solution.py:60
  62.6 0.0 copy-start.3
  62.6 0.8 pad_maximum_fusion.3
  63.4 0.1 collective-permute-start.2
  63.5 6.3 %collective-permute-start.3 = (f32[2,4,32,2,320]{4,3,2,1,0:T(2,128)S(1)}, f32[2,4,32,2,320]{4,3,2,1,0:T(2,128)S(1)}, u32[]{:S(2)}, u32[]{:S(2)}) collective-permute-start(f32[2,4,32,2,320]{4,3,2,1,0:T(2,128)S(1)} %get-tuple-element.12), channel_id=1, source_target_pairs={{1,0},{2,1},{3,2},{4,3},{5,4},{6,5},{7,6},{8,7},{9,8},{10,9},{11,1... | collective-permute-start | bytes 1966088 | tf_op jit(solution)/shard_map/ppermute | solution.py:16
  69.8 0.0 copy-done.3
  69.8 3.7 %fusion.22 = (f32[4,32,16,319]{3,2,1,0:T(8,128)}, f32[4,32,16,319]{3,2,1,0:T(8,128)}) fusion(f32[4,32,16,320]{3,2,1,0:T(8,128)S(1)} %copy-done.3), kind=kLoop, calls=%fused_computation.52 | loop fusion | bytes 10452992 | tf_op jit(solution)/shard_map/slice | solution.py:29
  73.5 13.4 %collective-permute-done.2 = f32[2,4,32,2,320]{4,3,2,1,0:T(2,128)S(1)} collective-permute-done((f32[2,4,32,2,320]{4,3,2,1,0:T(2,128)S(1)}, f32[2,4,32,2,320]{4,3,2,1,0:T(2,128)S(1)}, u32[]{:S(2)}, u32[]{:S(2)}) %collective-permute-start.2) | collective-permute-done | bytes 655392 | tf_op jit(solution)/shard_map/ppermute | solution.py:13
  86.9 0.0 collective-permute-done.3
  86.9 2.3 %pad_maximum_fusion.1 = f32[2,4,32,20,320]{4,3,2,1,0:T(8,128)S(1)} fusion(f32[2,4,32,2,320]{4,3,2,1,0:T(2,128)S(1)} %collective-permute-done.3, f32[1,4,32,16,320]{4,3,2,1,0:T(8,128)S(1)} %get-tuple-element.22, f32[1,4,32,16,320]{4,3,2,1,0:T(8,128)S(1)} %get-tuple-element.21, f32[2,4,32,2,320]{4,3,2,1,0:T(2,128)S(1)} %collective-permute-done.2), kind=kLoop, calls=%fused_computation.1 | loop fusion | flops 4915200 | bytes 13107200 | tf_op jit(solution)/shard_map/concatenate | solution.py:17
  89.2 2.7 %slice_bitcast_fusion.1 = (f32[4,32,20,320]{3,2,1,0:T(8,128)}, f32[4,32,20,320]{3,2,1,0:T(8,128)S(1)}) fusion(f32[2,4,32,20,320]{4,3,2,1,0:T(8,128)S(1)} %pad_maximum_fusion.1), kind=kLoop, calls=%fused_computation.3 | loop fusion | bytes 13107200 | tf_op jit(solution)/shard_map/squeeze | solution.py:61
  91.9 4.1 %fusion.20 = (f32[4,32,16,319]{3,2,1,0:T(8,128)}, f32[4,32,16,319]{3,2,1,0:T(8,128)}) fusion(f32[4,32,20,320]{3,2,1,0:T(8,128)S(1)} %get-tuple-element.8), kind=kLoop, calls=%fused_computation.50 | loop fusion | bytes 10452992 | tf_op jit(solution)/shard_map/slice | solution.py:29
  96.1 0.0 copy-done
  96.1 18.2 %fusion.1 = f32[4,32,16,320]{3,2,1,0:T(8,128)} fusion(f32[4,32,20,320]{3,2,1,0:T(8,128)} %copy-done, f32[4,32,16,320]{3,2,1,0:T(8,128)} %get-tuple-element.6, f32[4,32,20,320]{3,2,1,0:T(8,128)} %get-tuple-element.7, f32[4,32,16,319]{3,2,1,0:T(8,128)} %get-tuple-element.16, f32[4,32,16,319]{3,2,1,0:T(8,128)} %get-tuple-element.15, ...), kind=kLoop, calls=%fused_computation.8 | loop fusion | flops 9830400 | bytes 34045952 | tf_op jit(solution)/shard_map/add | solution.py:50
  114.3 2.7 %collective-permute-start.4 = (f32[4,32,16,320]{3,2,1,0:T(8,128)}, f32[4,32,16,320]{3,2,1,0:T(8,128)S(1)}, u32[]{:S(2)}, u32[]{:S(2)}) collective-permute-start(f32[4,32,16,320]{3,2,1,0:T(8,128)} %fusion.1), channel_id=1, source_target_pairs={{32,0},{64,32},{96,64},{128,96},{160,128},{192,160},{224,192},{33,... | collective-permute-start | bytes 7864328 | tf_op jit(solution)/shard_map/ppermute | solution.py:24
  117.0 69.9 %collective-permute-done.4 = f32[4,32,16,320]{3,2,1,0:T(8,128)S(1)} collective-permute-done((f32[4,32,16,320]{3,2,1,0:T(8,128)}, f32[4,32,16,320]{3,2,1,0:T(8,128)S(1)}, u32[]{:S(2)}, u32[]{:S(2)}) %collective-permute-start.4) | collective-permute-done | bytes 2621472 | tf_op jit(solution)/shard_map/ppermute | solution.py:24
  186.9 2.1 %fusion.18 = f32[1,4,32,16,320]{4,3,2,1,0:T(8,128)} fusion(f32[4,32,16,320]{3,2,1,0:T(8,128)S(1)} %collective-permute-done.4, f32[1,4,32,16,320]{4,3,2,1,0:T(8,128)S(1)} %copy-done.2), kind=kLoop, calls=%fused_computation.34 | loop fusion | flops 655360 | bytes 7864320 | tf_op jit(solution)/shard_map/broadcast_in_dim | solution.py:70
  (3 shorter events, 0.0 us)
Async XLA Ops:
  0.0 4.2 %copy-start.2 = (f32[1,4,32,16,320]{4,3,2,1,0:T(8,128)S(1)}, f32[1,4,32,16,320]{4,3,2,1,0:T(8,128)}, u32[]{:S(2)}) copy-start(f32[1,4,32,16,320]{4,3,2,1,0:T(8,128)} %param.3) | copy-start | bytes 7864324
  5.6 20.9 %collective-permute-start = (f32[2,4,32,2,320]{4,3,2,1,0:T(2,128)S(1)}, f32[2,4,32,2,320]{4,3,2,1,0:T(2,128)S(1)}, u32[]{:S(2)}, u32[]{:S(2)}) collective-permute-start(f32[2,4,32,2,320]{4,3,2,1,0:T(2,128)S(1)} %get-tuple-element.13), channel_id=1, source_target_pairs={{0,1},{1,2},{2,3},{3,4},{4,5},{5,6},{6,7},{7,8},{8,9},{9,10},{10,1... | collective-permute-start | bytes 1966088 | tf_op jit(solution)/shard_map/ppermute | solution.py:13
  5.6 26.2 %collective-permute-start.1 = (f32[2,4,32,2,320]{4,3,2,1,0:T(2,128)S(1)}, f32[2,4,32,2,320]{4,3,2,1,0:T(2,128)S(1)}, u32[]{:S(2)}, u32[]{:S(2)}) collective-permute-start(f32[2,4,32,2,320]{4,3,2,1,0:T(2,128)S(1)} %get-tuple-element.14), channel_id=1, source_target_pairs={{1,0},{2,1},{3,2},{4,3},{5,4},{6,5},{7,6},{8,7},{9,8},{10,9},{11,1... | collective-permute-start | bytes 1966088 | tf_op jit(solution)/shard_map/ppermute | solution.py:16
  36.9 4.2 %copy-start.1 = (f32[4,32,20,320]{3,2,1,0:T(8,128)}, f32[4,32,20,320]{3,2,1,0:T(8,128)S(1)}, u32[]{:S(2)}) copy-start(f32[4,32,20,320]{3,2,1,0:T(8,128)S(1)} %get-tuple-element.10) | copy-start | bytes 9830404
  62.6 7.2 %copy-start.3 = (f32[4,32,16,320]{3,2,1,0:T(8,128)S(1)}, f32[4,32,16,320]{3,2,1,0:T(8,128)}, u32[]{:S(2)}) copy-start(f32[4,32,16,320]{3,2,1,0:T(8,128)} %get-tuple-element.5) | copy-start | bytes 7864324
  63.4 23.5 %collective-permute-start.2 = (f32[2,4,32,2,320]{4,3,2,1,0:T(2,128)S(1)}, f32[2,4,32,2,320]{4,3,2,1,0:T(2,128)S(1)}, u32[]{:S(2)}, u32[]{:S(2)}) collective-permute-start(f32[2,4,32,2,320]{4,3,2,1,0:T(2,128)S(1)} %get-tuple-element.11), channel_id=1, source_target_pairs={{0,1},{1,2},{2,3},{3,4},{4,5},{5,6},{6,7},{7,8},{8,9},{9,10},{10,1... | collective-permute-start | bytes 1966088 | tf_op jit(solution)/shard_map/ppermute | solution.py:13
  63.5 23.5 %collective-permute-start.3 = (f32[2,4,32,2,320]{4,3,2,1,0:T(2,128)S(1)}, f32[2,4,32,2,320]{4,3,2,1,0:T(2,128)S(1)}, u32[]{:S(2)}, u32[]{:S(2)}) collective-permute-start(f32[2,4,32,2,320]{4,3,2,1,0:T(2,128)S(1)} %get-tuple-element.12), channel_id=1, source_target_pairs={{1,0},{2,1},{3,2},{4,3},{5,4},{6,5},{7,6},{8,7},{9,8},{10,9},{11,1... | collective-permute-start | bytes 1966088 | tf_op jit(solution)/shard_map/ppermute | solution.py:16
  91.9 4.1 %copy-start = (f32[4,32,20,320]{3,2,1,0:T(8,128)}, f32[4,32,20,320]{3,2,1,0:T(8,128)S(1)}, u32[]{:S(2)}) copy-start(f32[4,32,20,320]{3,2,1,0:T(8,128)S(1)} %get-tuple-element.8) | copy-start | bytes 9830404
  114.3 72.6 %collective-permute-start.4 = (f32[4,32,16,320]{3,2,1,0:T(8,128)}, f32[4,32,16,320]{3,2,1,0:T(8,128)S(1)}, u32[]{:S(2)}, u32[]{:S(2)}) collective-permute-start(f32[4,32,16,320]{3,2,1,0:T(8,128)} %fusion.1), channel_id=1, source_target_pairs={{32,0},{64,32},{96,64},{128,96},{160,128},{192,160},{224,192},{33,... | collective-permute-start | bytes 7864328 | tf_op jit(solution)/shard_map/ppermute | solution.py:24
where the time goes:
time: 189 us
  waiting for transfers between devices  97.2 us (51%)
  other arithmetic  48.8 us (26%)
  local copies, waits for them, and re-layouts  25.3 us (13%)
  starting transfers between devices  17.5 us (9%)
    ppermute x1, waiting for transfers between devices, passed_along(): lax.ppermute(value, axis, [(source, source + steps) for source in range(i...  69.9 us
    ppermute x2, waiting for transfers between devices, padded(): lax.ppermute(lax.slice_in_dim(block, block.shape[dim] - width, None, axis...  21.9 us
    mul x2, other arithmetic, run_model(): lateral = velocity[section, 1] * state  18.9 us
    add x1, other arithmetic, combine(): return state + along + 0.5 * (lat_up - lat_down) + diffuse  18.2 us
    slice x4, local copies, waits for them, and re-layouts, lat_pair(): upper = jnp.concatenate([field[..., 1:], edge], axis=-1)  15.7 us
    ppermute x2, starting transfers between devices, padded(): lax.ppermute(lax.slice_in_dim(block, 0, width, axis=dim), axis, backward)  14.6 us
    squeeze x2, local copies, waits for them, and re-layouts, run_model(): state = combine(state, rimmed[0], rimmed[1], lateral, width)  5.45 us
    ppermute x2, waiting for transfers between devices, padded(): lax.ppermute(lax.slice_in_dim(block, 0, width, axis=dim), axis, backward)  5.43 us
  transfers between devices with their start and end apart: 5, of which 4 were waited for; matrix products, arithmetic and copies ran while one was open for 4% of the time, Pallas kernels for 0%

commit v1 on v0

v1 whole, which is shorter than its diff:
```python
import functools

import jax
import jax.numpy as jnp
from jax import lax
from jax.experimental import pallas as pl
from jax.experimental.pallas import tpu as pltpu
from jax.sharding import PartitionSpec as P

FIELDS, LON, LAT = 4, 16, 320
WIDE = 384
BLOCK = 4
CHUNKS = ((0, 8), (8, 12), (20, 12))


def wide(x):
    return jnp.concatenate([x, jnp.zeros((x.shape[0], WIDE - LAT), x.dtype)], axis=1)


def ends(x):
    row = lax.broadcasted_iota(jnp.int32, (8, x.shape[1]), 0)
    return jnp.where(row < 4, x[0:8], x[8:16])


def middle(x):
    row = lax.broadcasted_iota(jnp.int32, (8, x.shape[1]), 0)
    return jnp.where(row < 4, x[8:16], x[0:8])


def rates(a, b, c):
    along = a * (2.0 / 3.0)
    across = b * 0.5
    return dict(
        centre=1.0 - 4.0 * c,
        down=c + along,
        up=c - along,
        far=a * (1.0 / 12.0),
        lat_down=c + across,
        lat_up=c - across,
    )


def rolled(x, shift, axis):
    size = x.shape[axis]
    return pltpu.roll(x, shift % size, axis)


def inside(r, first, last):
    row = lax.broadcasted_iota(jnp.int32, r["far"].shape, 0)
    return dict(
        centre=r["centre"],
        lat_down=r["lat_down"],
        lat_up=r["lat_up"],
        down=jnp.where(row > first, r["down"], 0.0),
        up=jnp.where(row < last, r["up"], 0.0),
        far_down=jnp.where(row > first + 1, r["far"], 0.0),
        far_up=jnp.where(row < last - 1, r["far"], 0.0),
    )


def step(w, r):
    out = r["centre"] * w
    out += rolled(r["down"] * w, -1, 0) + rolled(r["up"] * w, 1, 0)
    out += rolled(r["far_up"] * w, 2, 0) - rolled(r["far_down"] * w, -2, 0)
    out += rolled(r["lat_down"] * w, -1, 1) + rolled(r["lat_up"] * w, 1, 1)
    return out


def leaving_rates(r):
    row = lax.broadcasted_iota(jnp.int32, r["far"].shape, 0)
    return dict(
        down=jnp.where(row == 0, r["down"], 0.0),
        up=jnp.where(row == 7, r["up"], 0.0),
        far_down=jnp.where(row < 2, r["far"], 0.0),
        far_up=jnp.where(row >= 6, r["far"], 0.0),
    )


def leaving(ws, r):
    to_next = 0.0
    to_previous = 0.0
    for f, w in enumerate(ws):
        to_next += rolled(r["up"] * w, 2 * f + 1, 0) + rolled(r["far_up"] * w, 2 * f + 2, 0)
        to_previous += rolled(r["down"] * w, 2 * f + 1, 0) - rolled(r["far_down"] * w, 2 * f, 0)
    return to_next, to_previous


def arriving(from_previous, from_next, f):
    row = lax.broadcasted_iota(jnp.int32, from_next.shape, 0)
    low = jnp.where(row < 2, rolled(from_previous, -2 * f, 0), 0.0)
    return jnp.where(row >= 6, rolled(from_next, 6 - 2 * f, 0), low)


def put_packed(ref, l, pieces):
    lane = lax.broadcasted_iota(jnp.int32, (8, 128), 1)
    for pair in range(FIELDS // 2):
        first, second = pieces[2 * pair], pieces[2 * pair + 1]
        base = 40 * pair
        ref[l, base : base + 8] = first[:, 0:128]
        ref[l, base + 8 : base + 16] = first[:, 128:256]
        ref[l, base + 16 : base + 24] = second[:, 0:128]
        ref[l, base + 24 : base + 32] = second[:, 128:256]
        ref[l, base + 32 : base + 40] = jnp.where(
            lane < 64, first[:, 256:384], pltpu.roll(second[:, 256:384], 64, 1)
        )


def get_packed(ref, l, f, part):
    base = 40 * (f // 2)
    if part < 2:
        at = base + 16 * (f % 2) + 8 * part
        return ref[l, at : at + 8]
    last = ref[l, base + 32 : base + 40]
    return pltpu.roll(last, 64, 1) if f % 2 else last


def levels(body):
    pl.loop(0, BLOCK)(body)


def first_kernel(adj, vel, kap, mid, image, state, to_next, to_previous):
    @levels
    def _(l):
        ws = [wide(adj[f, l]) for f in range(FIELDS)]
        for s in (1, 0):
            r = rates(wide(vel[s, 0, l]), wide(vel[s, 1, l]), wide(kap[s, l]))
            if s == 1:
                out = leaving_rates({k: ends(v) for k, v in r.items() if k in ("down", "up", "far")})
                to_next[l], to_previous[l] = leaving([ends(w) for w in ws], out)
            r = inside(r, 0, LON - 1)
            ws = [step(w, r) for w in ws]
            if s == 1:
                for f, w in enumerate(ws):
                    state[l, f] = ends(w)
        put_packed(mid, l, [middle(w) for w in ws])
        for f, w in enumerate(ws):
            image[l, f] = ends(w)


def second_kernel(vel, kap, from_previous, from_next, state, image, image_out, to_next, to_previous):
    @levels
    def _(l):
        r = rates(wide(ends(vel[0, 0, l])), wide(ends(vel[0, 1, l])), wide(ends(kap[0, l])))
        low, high = from_previous[l], from_next[l]
        new = [arriving(low, high, f) for f in range(FIELDS)]
        to_next[l], to_previous[l] = leaving([state[l, f] + new[f] for f in range(FIELDS)], leaving_rates(r))
        r = inside(r, 0, 7)
        for f in range(FIELDS):
            image_out[l, f] = image[l, f] + step(new[f], r)


def third_kernel(from_previous, from_next, image, packed):
    @levels
    def _(l):
        low, high = from_previous[l], from_next[l]
        put_packed(packed, l, [image[l, f] + arriving(low, high, f) for f in range(FIELDS)])


def last_kernel(adj, mid, end, *refs):
    out = refs[-1]
    row = lax.broadcasted_iota(jnp.int32, (8, 128), 0)

    @levels
    def _(l):
        for f in range(FIELDS):
            for part in range(3):
                lanes = slice(128 * part, min(128 * part + 128, LAT))
                n = lanes.stop - lanes.start
                m, e = get_packed(mid, l, f, part), get_packed(end, l, f, part)
                out[f, l, 0:8, lanes] = adj[f, l, 0:8, lanes] - jnp.where(row < 4, e, m)[:, :n]
                out[f, l, 8:16, lanes] = adj[f, l, 8:16, lanes] - jnp.where(row < 4, m, e)[:, :n]


def spec(dims, at, first=0):
    block = tuple(BLOCK if i == at else d for i, d in enumerate(dims))
    return pl.BlockSpec(block, lambda i: tuple(first + i if k == at else 0 for k in range(len(dims))))


def f32(*dims):
    return jax.ShapeDtypeStruct(dims, jnp.float32)


def call(kernel, count, in_specs, out_specs, out_shape, name, cost, **kw):
    return pl.pallas_call(
        kernel,
        grid=(count // BLOCK,),
        in_specs=in_specs,
        out_specs=out_specs,
        out_shape=out_shape,
        name=name,
        cost_estimate=pl.CostEstimate(flops=cost * count, bytes_accessed=cost * count, transcendentals=0),
        compiler_params=pltpu.CompilerParams(vmem_limit_bytes=48 * 1024 * 1024),
        **kw,
    )


TILE = (0, 8, WIDE)
FIELD_TILES = (0, FIELDS, 8, WIDE)
PACKED = (0, 80, 128)


def sized(dims, n):
    return f32(n, *dims[1:])


def neighbours(to_next, to_previous):
    n = lax.axis_size("tile")
    ahead = [(i, (i + 1) % n) for i in range(n)]
    back = [(j, i) for i, j in ahead]
    return lax.ppermute(to_next, "tile", ahead), lax.ppermute(to_previous, "tile", back)


def to_preceding(x):
    n = lax.axis_size("win")
    return lax.ppermute(x, "win", [(k + 1, k) for k in range(n - 1)])


def per_device(adjoint, velocity, kappa):
    adj, vel, kap = adjoint[0], velocity[0], kappa[0]
    lev = adj.shape[1]
    adj_dims, vel_dims, kap_dims = adj.shape, vel.shape, kap.shape
    firsts = []
    for start, n in CHUNKS:
        b = start // BLOCK
        mid, image, state, to_next, to_previous = call(
            first_kernel, n,
            [spec(adj_dims, 1, b), spec(vel_dims, 2, b), spec(kap_dims, 1, b)],
            [spec(PACKED, 0), spec(FIELD_TILES, 0), spec(FIELD_TILES, 0), spec(TILE, 0), spec(TILE, 0)],
            [sized(PACKED, n), sized(FIELD_TILES, n), sized(FIELD_TILES, n), sized(TILE, n), sized(TILE, n)],
            "interior", 250000,
        )(adj, vel, kap)
        firsts.append((to_preceding(mid), image, state, neighbours(to_next, to_previous)))
    seconds = []
    for (start, n), (mid, image, state, (low, high)) in zip(CHUNKS, firsts):
        b = start // BLOCK
        image, to_next, to_previous = call(
            second_kernel, n,
            [spec(vel_dims, 2, b), spec(kap_dims, 1, b), spec(TILE, 0), spec(TILE, 0), spec(FIELD_TILES, 0), spec(FIELD_TILES, 0)],
            [spec(FIELD_TILES, 0), spec(TILE, 0), spec(TILE, 0)],
            [sized(FIELD_TILES, n), sized(TILE, n), sized(TILE, n)],
            "ends_first", 100000,
        )(vel, kap, low, high, state, image)
        seconds.append((mid, image, neighbours(to_next, to_previous)))
    thirds = []
    for (start, n), (mid, image, (low, high)) in zip(CHUNKS, seconds):
        end = call(
            third_kernel, n,
            [spec(TILE, 0), spec(TILE, 0), spec(FIELD_TILES, 0)],
            spec(PACKED, 0), sized(PACKED, n), "ends_second", 50000,
        )(low, high, image)
        thirds.append((mid, to_preceding(end)))
    out = None
    for (start, n), (mid, end) in zip(CHUNKS, thirds):
        b = start // BLOCK
        more = {} if out is None else dict(input_output_aliases={3: 0})
        args = () if out is None else (out,)
        out = call(
            last_kernel, n,
            [spec(adj_dims, 1, b), spec(PACKED, 0), spec(PACKED, 0)] + [pl.BlockSpec(memory_space=pl.ANY)] * len(args),
            spec(adj_dims, 1, b), f32(*adj_dims), "subtract", 80000, **more,
        )(adj, mid, end, *args)
    return out[None]


def solution(mesh):
    return jax.shard_map(
        per_device,
        mesh=mesh,
        in_specs=(
            P("win", None, None, "tile", None),
            P("win", None, None, None, "tile", None),
            P("win", None, None, "tile", None),
        ),
        out_specs=P("win", None, None, "tile", None),
        check_vma=False,
    )
```

time: 189 us -> 115 us (0.61)
  waiting for transfers between devices: 97.2 us -> 39.2 us
  other arithmetic: 48.8 us -> 0 us
  starting transfers between devices: 17.5 us -> 46.4 us
  Pallas kernels: 0 us -> 27.5 us
  local copies, waits for them, and re-layouts: 25.3 us -> 1.41 us
    ppermute x5 -> x18, waiting for transfers between devices: 97.2 us -> 39.2 us  [the longest x6 39.2 us: to_preceding(): return lax.ppermute(x, 'win', [(k + 1, k) for k in range(n - 1)])]
    ppermute x5 -> x18, starting transfers between devices: 17.5 us -> 46.4 us  [the longest x6 32.2 us: neighbours(): lax.ppermute(to_previous, 'tile', back)]
    pallas_call x0 -> x12, Pallas kernels: none -> 27.5 us  [the longest x3 11.6 us: per_device(): call(first_kernel, n, [spec(adj_dims, 1, b), spec(vel_dims, 2, b), spec(k...]
    mul x3 -> x0, other arithmetic: 19.5 us -> none  [the longest x2 18.9 us: run_model(): lateral = velocity[section, 1] * state]
    add x1 -> x0, other arithmetic: 18.2 us -> none  [combine(): return state + along + 0.5 * (lat_up - lat_down) + diffuse]
    slice x4 -> x0, local copies, waits for them, and re-layouts: 15.7 us -> none  [lat_pair(): upper = jnp.concatenate([field[..., 1:], edge], axis=-1)]
    squeeze x2 -> x0, local copies, waits for them, and re-layouts: 5.45 us -> none  [run_model(): state = combine(state, rimmed[0], rimmed[1], lateral, width)]
    concatenate x2 -> x0, other arithmetic: 4.59 us -> none  [padded(): block = jnp.concatenate([low, block, high], axis=dim)]
  transfers between devices with their start and end apart: 5 -> 18, of which waited for: 4 -> 1; matrix products, arithmetic and copies ran while one was open for 4% -> 0% of each run, Pallas kernels for 0% -> 18%
where the time goes in v1:
time: 115 us
  starting transfers between devices  46.4 us (40%)
  waiting for transfers between devices  39.2 us (34%)
  Pallas kernels  27.5 us (24%)
  local copies, waits for them, and re-layouts  1.41 us (1%)
    ppermute x6, waiting for transfers between devices, to_preceding(): return lax.ppermute(x, 'win', [(k + 1, k) for k in range(n - 1)])  39.2 us
    ppermute x6, starting transfers between devices, neighbours(): lax.ppermute(to_previous, 'tile', back)  32.2 us
    ppermute x6, starting transfers between devices, to_preceding(): return lax.ppermute(x, 'win', [(k + 1, k) for k in range(n - 1)])  13.3 us
    pallas_call x3, Pallas kernels, per_device(): call(first_kernel, n, [spec(adj_dims, 1, b), spec(vel_dims, 2, b), spec(k...  11.6 us
    pallas_call x3, Pallas kernels, per_device(): call(second_kernel, n, [spec(vel_dims, 2, b), spec(kap_dims, 1, b), spec(...  7.55 us
    pallas_call x3, Pallas kernels, per_device(): call(last_kernel, n, [spec(adj_dims, 1, b), spec(PACKED, 0), spec(PACKED,...  5.84 us
    pallas_call x3, Pallas kernels, per_device(): call(third_kernel, n, [spec(TILE, 0), spec(TILE, 0), spec(FIELD_TILES, 0)...  2.54 us
  transfers between devices with their start and end apart: 18, of which 1 were waited for; matrix products, arithmetic and copies ran while one was open for 0% of the time, Pallas kernels for 18%

profile of v1, /device:TPU:6, one launch (start us, length us, event | category | flops | bytes accessed | tf_op | source)
XLA Modules:
  0.0 114.7 jit_solution(18000610308571584735)
XLA Ops:
  0.0 1.4 %copy-done.1 = f32[1,2,32,16,320]{4,3,2,1,0:T(8,128)S(1)} copy-done((f32[1,2,32,16,320]{4,3,2,1,0:T(8,128)S(1)}, f32[1,2,32,16,320]{4,3,2,1,0:T(8,128)}, u32[]{:S(2)}) %copy-start.1) | copy-done | bytes 1310744
  1.4 4.3 %interior.4 = (f32[12,80,128]{2,1,0:T(8,128)S(1)}, f32[12,4,8,384]{3,2,1,0:T(8,128)S(1)}, f32[12,4,8,384]{3,2,1,0:T(8,128)S(1)}, f32[12,8,384]{2,1,0:T(8,128)S(1)}, f32[12,8,384]{2,1,0:T(8,128)S(1)}) custom-call(f32[4,32,16,320]{3,2,1,0:T(8,128)} %bitcast.4, f32[2,2,32,16,320]{4,3,2,1,0:T(8,128)} %bitcast.16, f32[2,32,16,320]{3,2,1,0:T(8,128)S(1)} %bitcast.10), custom_call_target="tpu_custom_call" | custom-call | flops 3000000 | bytes 3000000 | tf_op jit(solution)/shard_map/interior/pallas_call | solution.py:225
  5.7 0.1 collective-permute-start.7
  5.8 8.3 %collective-permute-start.8 = (f32[12,8,384]{2,1,0:T(8,128)S(1)}, f32[12,8,384]{2,1,0:T(8,128)S(1)}, u32[]{:S(2)}, u32[]{:S(2)}) collective-permute-start(f32[12,8,384]{2,1,0:T(8,128)S(1)} %get-tuple-element.39), channel_id=1, source_target_pairs={{1,0},{2,1},{3,2},{4,3},{5,4},{6,5},{7,6},{8,7},{9,8},{10,9},{11,1... | collective-permute-start | bytes 442376 | tf_op jit(solution)/shard_map/ppermute | solution.py:210
  14.0 4.3 %interior.3 = (f32[12,80,128]{2,1,0:T(8,128)S(1)}, f32[12,4,8,384]{3,2,1,0:T(8,128)S(1)}, f32[12,4,8,384]{3,2,1,0:T(8,128)S(1)}, f32[12,8,384]{2,1,0:T(8,128)S(1)}, f32[12,8,384]{2,1,0:T(8,128)S(1)}) custom-call(f32[4,32,16,320]{3,2,1,0:T(8,128)} %bitcast.5, f32[2,2,32,16,320]{4,3,2,1,0:T(8,128)} %bitcast.17, f32[2,32,16,320]{3,2,1,0:T(8,128)S(1)} %bitcast.11), custom_call_target="tpu_custom_call" | custom-call | flops 3000000 | bytes 3000000 | tf_op jit(solution)/shard_map/interior/pallas_call | solution.py:225
  18.3 0.1 collective-permute-start.1
  18.4 6.0 %collective-permute-start.2 = (f32[12,8,384]{2,1,0:T(8,128)S(1)}, f32[12,8,384]{2,1,0:T(8,128)S(1)}, u32[]{:S(2)}, u32[]{:S(2)}) collective-permute-start(f32[12,8,384]{2,1,0:T(8,128)S(1)} %get-tuple-element.31), channel_id=1, source_target_pairs={{1,0},{2,1},{3,2},{4,3},{5,4},{6,5},{7,6},{8,7},{9,8},{10,9},{11,1... | collective-permute-start | bytes 442376 | tf_op jit(solution)/shard_map/ppermute | solution.py:210
  24.4 3.1 %interior.5 = (f32[8,80,128]{2,1,0:T(8,128)S(1)}, f32[8,4,8,384]{3,2,1,0:T(8,128)S(1)}, f32[8,4,8,384]{3,2,1,0:T(8,128)S(1)}, f32[8,8,384]{2,1,0:T(8,128)S(1)}, f32[8,8,384]{2,1,0:T(8,128)S(1)}) custom-call(f32[4,32,16,320]{3,2,1,0:T(8,128)S(1)} %bitcast.6, f32[2,2,32,16,320]{4,3,2,1,0:T(8,128)} %bitcast.18, f32[2,32,16,320]{3,2,1,0:T(8,128)S(1)} %bitcast.12), custom_call_target="tpu_custom_call" | custom-call | flops 2000000 | bytes 2000000 | tf_op jit(solution)/shard_map/interior/pallas_call | solution.py:225
  27.4 0.1 collective-permute-start.13
  27.5 5.9 %collective-permute-start.14 = (f32[8,8,384]{2,1,0:T(8,128)S(1)}, f32[8,8,384]{2,1,0:T(8,128)S(1)}, u32[]{:S(2)}, u32[]{:S(2)}) collective-permute-start(f32[8,8,384]{2,1,0:T(8,128)S(1)} %get-tuple-element.47), channel_id=1, source_target_pairs={{1,0},{2,1},{3,2},{4,3},{5,4},{6,5},{7,6},{8,7},{9,8},{10,9},{11,1... | collective-permute-start | bytes 294920 | tf_op jit(solution)/shard_map/ppermute | solution.py:210
  33.5 2.8 %ends_first.4 = (f32[12,4,8,384]{3,2,1,0:T(8,128)S(1)}, f32[12,8,384]{2,1,0:T(8,128)S(1)}, f32[12,8,384]{2,1,0:T(8,128)S(1)}) custom-call(f32[2,2,32,16,320]{4,3,2,1,0:T(8,128)} %bitcast.19, f32[2,32,16,320]{3,2,1,0:T(8,128)S(1)} %bitcast.13, f32[12,8,384]{2,1,0:T(8,128)S(1)} %collective-permute-done.7.from_previous, ...), custom_call_target="tpu_custom_call" | custom-call | flops 1200000 | bytes 1200000 | tf_op jit(solution)/shard_map/ends_first/pallas_call | solution.py:236
  36.3 0.1 collective-permute-start.10
  36.4 0.5 collective-permute-start.9
  36.9 2.7 %collective-permute-start.12 = (f32[8,80,128]{2,1,0:T(8,128)S(1)}, f32[8,80,128]{2,1,0:T(8,128)S(1)}, u32[]{:S(2)}, u32[]{:S(2)}) collective-permute-start(f32[8,80,128]{2,1,0:T(8,128)S(1)} %get-tuple-element.45), channel_id=1, source_target_pairs={{32,0},{64,32},{96,64},{128,96},{160,128},{192,160},{224,192},{33,... | collective-permute-start | bytes 983048 | tf_op jit(solution)/shard_map/ppermute | solution.py:215
  39.7 2.9 %ends_first.3 = (f32[12,4,8,384]{3,2,1,0:T(8,128)S(1)}, f32[12,8,384]{2,1,0:T(8,128)S(1)}, f32[12,8,384]{2,1,0:T(8,128)S(1)}) custom-call(f32[2,2,32,16,320]{4,3,2,1,0:T(8,128)} %bitcast.20, f32[2,32,16,320]{3,2,1,0:T(8,128)S(1)} %bitcast.14, f32[12,8,384]{2,1,0:T(8,128)S(1)} %collective-permute-done.1.from_previous, ...), custom_call_target="tpu_custom_call" | custom-call | flops 1200000 | bytes 1200000 | tf_op jit(solution)/shard_map/ends_first/pallas_call | solution.py:236
  42.5 0.1 collective-permute-start.3
  42.6 5.9 %collective-permute-start.4 = (f32[12,8,384]{2,1,0:T(8,128)S(1)}, f32[12,8,384]{2,1,0:T(8,128)S(1)}, u32[]{:S(2)}, u32[]{:S(2)}) collective-permute-start(f32[12,8,384]{2,1,0:T(8,128)S(1)} %get-tuple-element.35), channel_id=1, source_target_pairs={{1,0},{2,1},{3,2},{4,3},{5,4},{6,5},{7,6},{8,7},{9,8},{10,9},{11,1... | collective-permute-start | bytes 442376 | tf_op jit(solution)/shard_map/ppermute | solution.py:210
  48.6 1.8 %ends_first.5 = (f32[8,4,8,384]{3,2,1,0:T(8,128)S(1)}, f32[8,8,384]{2,1,0:T(8,128)S(1)}, f32[8,8,384]{2,1,0:T(8,128)S(1)}) custom-call(f32[2,2,32,16,320]{4,3,2,1,0:T(8,128)} %bitcast.21, f32[2,32,16,320]{3,2,1,0:T(8,128)S(1)} %bitcast.15, f32[8,8,384]{2,1,0:T(8,128)S(1)} %collective-permute-done.13.from_previous, ...), custom_call_target="tpu_custom_call" | custom-call | flops 800000 | bytes 800000 | tf_op jit(solution)/shard_map/ends_first/pallas_call | solution.py:236
  50.5 0.1 collective-permute-start.15
  50.6 5.9 %collective-permute-start.16 = (f32[8,8,384]{2,1,0:T(8,128)S(1)}, f32[8,8,384]{2,1,0:T(8,128)S(1)}, u32[]{:S(2)}, u32[]{:S(2)}) collective-permute-start(f32[8,8,384]{2,1,0:T(8,128)S(1)} %get-tuple-element.51), channel_id=1, source_target_pairs={{1,0},{2,1},{3,2},{4,3},{5,4},{6,5},{7,6},{8,7},{9,8},{10,9},{11,1... | collective-permute-start | bytes 294920 | tf_op jit(solution)/shard_map/ppermute | solution.py:210
  56.5 0.9 ends_second.4
  57.4 2.4 %collective-permute-start.6 = (f32[12,80,128]{2,1,0:T(8,128)S(1)}, f32[12,80,128]{2,1,0:T(8,128)S(1)}, u32[]{:S(2)}, u32[]{:S(2)}) collective-permute-start(f32[12,80,128]{2,1,0:T(8,128)S(1)} %get-tuple-element.37), channel_id=1, source_target_pairs={{32,0},{64,32},{96,64},{128,96},{160,128},{192,160},{224,192},{33,... | collective-permute-start | bytes 1474568 | tf_op jit(solution)/shard_map/ppermute | solution.py:215
  59.9 2.4 %collective-permute-start.11 = (f32[12,80,128]{2,1,0:T(8,128)S(1)}, f32[12,80,128]{2,1,0:T(8,128)S(1)}, u32[]{:S(2)}, u32[]{:S(2)}) collective-permute-start(f32[12,80,128]{2,1,0:T(8,128)S(1)} %ends_second.4), channel_id=1, source_target_pairs={{32,0},{64,32},{96,64},{128,96},{160,128},{192,160},{224,192},{33,... | collective-permute-start | bytes 1474568 | tf_op jit(solution)/shard_map/ppermute | solution.py:215
  62.3 1.0 ends_second.3
  63.3 1.9 %collective-permute-start = (f32[12,80,128]{2,1,0:T(8,128)S(1)}, f32[12,80,128]{2,1,0:T(8,128)S(1)}, u32[]{:S(2)}, u32[]{:S(2)}) collective-permute-start(f32[12,80,128]{2,1,0:T(8,128)S(1)} %get-tuple-element.29), channel_id=1, source_target_pairs={{32,0},{64,32},{96,64},{128,96},{160,128},{192,160},{224,192},{33,... | collective-permute-start | bytes 1474568 | tf_op jit(solution)/shard_map/ppermute | solution.py:215
  65.2 1.9 %collective-permute-start.5 = (f32[12,80,128]{2,1,0:T(8,128)S(1)}, f32[12,80,128]{2,1,0:T(8,128)S(1)}, u32[]{:S(2)}, u32[]{:S(2)}) collective-permute-start(f32[12,80,128]{2,1,0:T(8,128)S(1)} %ends_second.3), channel_id=1, source_target_pairs={{32,0},{64,32},{96,64},{128,96},{160,128},{192,160},{224,192},{33,... | collective-permute-start | bytes 1474568 | tf_op jit(solution)/shard_map/ppermute | solution.py:215
  67.2 0.6 ends_second.5
  67.8 1.9 %collective-permute-start.17 = (f32[8,80,128]{2,1,0:T(8,128)S(1)}, f32[8,80,128]{2,1,0:T(8,128)S(1)}, u32[]{:S(2)}, u32[]{:S(2)}) collective-permute-start(f32[8,80,128]{2,1,0:T(8,128)S(1)} %ends_second.5), channel_id=1, source_target_pairs={{32,0},{64,32},{96,64},{128,96},{160,128},{192,160},{224,192},{33,... | collective-permute-start | bytes 983048 | tf_op jit(solution)/shard_map/ppermute | solution.py:215
  69.7 39.1 %collective-permute-done.17.end = f32[8,80,128]{2,1,0:T(8,128)S(1)} collective-permute-done((f32[8,80,128]{2,1,0:T(8,128)S(1)}, f32[8,80,128]{2,1,0:T(8,128)S(1)}, u32[]{:S(2)}, u32[]{:S(2)}) %collective-permute-start.17) | collective-permute-done | bytes 327712 | tf_op jit(solution)/shard_map/ppermute | solution.py:215
  108.9 1.4 %subtract.3.refs_0_ = f32[4,32,16,320]{3,2,1,0:T(8,128)} custom-call(f32[4,32,16,320]{3,2,1,0:T(8,128)S(1)} %bitcast.7, f32[8,80,128]{2,1,0:T(8,128)S(1)} %collective-permute-done.12.mid, f32[8,80,128]{2,1,0:T(8,128)S(1)} %collective-permute-done.17.end), custom_call_target="tpu_custom_call" | custom-call | flops 640000 | bytes 640000 | tf_op jit(solution)/shard_map/subtract/pallas_call | solution.py:257
  110.3 2.2 %subtract.4.refs_0_ = f32[4,32,16,320]{3,2,1,0:T(8,128)} custom-call(f32[4,32,16,320]{3,2,1,0:T(8,128)S(1)} %bitcast.8, f32[12,80,128]{2,1,0:T(8,128)S(1)} %collective-permute-done.6.mid, f32[12,80,128]{2,1,0:T(8,128)S(1)} %collective-permute-done.11.end, f32[4,32,16,320]{3,2,1,0:T(8,128)} %subtract.3.refs_0_), custom_call_target="tpu_custom_call", output_to_operand_aliasing={{}: (3, {})} | custom-call | flops 960000 | bytes 960000 | tf_op jit(solution)/shard_map/subtract/pallas_call | solution.py:257
  112.5 2.2 %subtract.5 = f32[4,32,16,320]{3,2,1,0:T(8,128)} custom-call(f32[4,32,16,320]{3,2,1,0:T(8,128)S(1)} %bitcast.9, f32[12,80,128]{2,1,0:T(8,128)S(1)} %collective-permute-done.mid, f32[12,80,128]{2,1,0:T(8,128)S(1)} %collective-permute-done.5.end, f32[4,32,16,320]{3,2,1,0:T(8,128)} %subtract.4.refs_0_), custom_call_target="tpu_custom_call", output_to_operand_aliasing={{}: (3, {})} | custom-call | flops 960000 | bytes 960000 | tf_op jit(solution)/shard_map/subtract/pallas_call | solution.py:257
  (20 shorter events, 0.1 us)
Async XLA Ops:
  0.0 1.4 %copy-start.1 = (f32[1,2,32,16,320]{4,3,2,1,0:T(8,128)S(1)}, f32[1,2,32,16,320]{4,3,2,1,0:T(8,128)}, u32[]{:S(2)}) copy-start(f32[1,2,32,16,320]{4,3,2,1,0:T(8,128)} %param.5) | copy-start | bytes 3932164
  5.7 21.8 %collective-permute-start.7 = (f32[12,8,384]{2,1,0:T(8,128)S(1)}, f32[12,8,384]{2,1,0:T(8,128)S(1)}, u32[]{:S(2)}, u32[]{:S(2)}) collective-permute-start(f32[12,8,384]{2,1,0:T(8,128)S(1)} %get-tuple-element.38), channel_id=1, source_target_pairs={{0,1},{1,2},{2,3},{3,4},{4,5},{5,6},{6,7},{7,8},{8,9},{9,10},{10,1... | collective-permute-start | bytes 442376 | tf_op jit(solution)/shard_map/ppermute | solution.py:210
  5.8 18.6 %copy-start = (f32[1,4,32,16,320]{4,3,2,1,0:T(8,128)S(1)}, f32[1,4,32,16,320]{4,3,2,1,0:T(8,128)}, u32[]{:S(2)}) copy-start(f32[1,4,32,16,320]{4,3,2,1,0:T(8,128)} %param.3) | copy-start | bytes 7864324
  5.8 27.7 %collective-permute-start.8 = (f32[12,8,384]{2,1,0:T(8,128)S(1)}, f32[12,8,384]{2,1,0:T(8,128)S(1)}, u32[]{:S(2)}, u32[]{:S(2)}) collective-permute-start(f32[12,8,384]{2,1,0:T(8,128)S(1)} %get-tuple-element.39), channel_id=1, source_target_pairs={{1,0},{2,1},{3,2},{4,3},{5,4},{6,5},{7,6},{8,7},{9,8},{10,9},{11,1... | collective-permute-start | bytes 442376 | tf_op jit(solution)/shard_map/ppermute | solution.py:210
  18.3 18.1 %collective-permute-start.1 = (f32[12,8,384]{2,1,0:T(8,128)S(1)}, f32[12,8,384]{2,1,0:T(8,128)S(1)}, u32[]{:S(2)}, u32[]{:S(2)}) collective-permute-start(f32[12,8,384]{2,1,0:T(8,128)S(1)} %get-tuple-element.30), channel_id=1, source_target_pairs={{0,1},{1,2},{2,3},{3,4},{4,5},{5,6},{6,7},{7,8},{8,9},{9,10},{10,1... | collective-permute-start | bytes 442376 | tf_op jit(solution)/shard_map/ppermute | solution.py:210
  18.4 18.5 %collective-permute-start.2 = (f32[12,8,384]{2,1,0:T(8,128)S(1)}, f32[12,8,384]{2,1,0:T(8,128)S(1)}, u32[]{:S(2)}, u32[]{:S(2)}) collective-permute-start(f32[12,8,384]{2,1,0:T(8,128)S(1)} %get-tuple-element.31), channel_id=1, source_target_pairs={{1,0},{2,1},{3,2},{4,3},{5,4},{6,5},{7,6},{8,7},{9,8},{10,9},{11,1... | collective-permute-start | bytes 442376 | tf_op jit(solution)/shard_map/ppermute | solution.py:210
  27.4 15.1 %collective-permute-start.13 = (f32[8,8,384]{2,1,0:T(8,128)S(1)}, f32[8,8,384]{2,1,0:T(8,128)S(1)}, u32[]{:S(2)}, u32[]{:S(2)}) collective-permute-start(f32[8,8,384]{2,1,0:T(8,128)S(1)} %get-tuple-element.46), channel_id=1, source_target_pairs={{0,1},{1,2},{2,3},{3,4},{4,5},{5,6},{6,7},{7,8},{8,9},{9,10},{10,1... | collective-permute-start | bytes 294920 | tf_op jit(solution)/shard_map/ppermute | solution.py:210
  27.5 15.1 %collective-permute-start.14 = (f32[8,8,384]{2,1,0:T(8,128)S(1)}, f32[8,8,384]{2,1,0:T(8,128)S(1)}, u32[]{:S(2)}, u32[]{:S(2)}) collective-permute-start(f32[8,8,384]{2,1,0:T(8,128)S(1)} %get-tuple-element.47), channel_id=1, source_target_pairs={{1,0},{2,1},{3,2},{4,3},{5,4},{6,5},{7,6},{8,7},{9,8},{10,9},{11,1... | collective-permute-start | bytes 294920 | tf_op jit(solution)/shard_map/ppermute | solution.py:210
  36.3 14.1 %collective-permute-start.10 = (f32[12,8,384]{2,1,0:T(8,128)S(1)}, f32[12,8,384]{2,1,0:T(8,128)S(1)}, u32[]{:S(2)}, u32[]{:S(2)}) collective-permute-start(f32[12,8,384]{2,1,0:T(8,128)S(1)} %get-tuple-element.43), channel_id=1, source_target_pairs={{1,0},{2,1},{3,2},{4,3},{5,4},{6,5},{7,6},{8,7},{9,8},{10,9},{11,1... | collective-permute-start | bytes 442376 | tf_op jit(solution)/shard_map/ppermute | solution.py:210
  36.4 14.1 %collective-permute-start.9 = (f32[12,8,384]{2,1,0:T(8,128)S(1)}, f32[12,8,384]{2,1,0:T(8,128)S(1)}, u32[]{:S(2)}, u32[]{:S(2)}) collective-permute-start(f32[12,8,384]{2,1,0:T(8,128)S(1)} %get-tuple-element.42), channel_id=1, source_target_pairs={{0,1},{1,2},{2,3},{3,4},{4,5},{5,6},{6,7},{7,8},{8,9},{9,10},{10,1... | collective-permute-start | bytes 442376 | tf_op jit(solution)/shard_map/ppermute | solution.py:210
  36.9 30.9 %collective-permute-start.12 = (f32[8,80,128]{2,1,0:T(8,128)S(1)}, f32[8,80,128]{2,1,0:T(8,128)S(1)}, u32[]{:S(2)}, u32[]{:S(2)}) collective-permute-start(f32[8,80,128]{2,1,0:T(8,128)S(1)} %get-tuple-element.45), channel_id=1, source_target_pairs={{32,0},{64,32},{96,64},{128,96},{160,128},{192,160},{224,192},{33,... | collective-permute-start | bytes 983048 | tf_op jit(solution)/shard_map/ppermute | solution.py:215
  42.5 14.9 %collective-permute-start.3 = (f32[12,8,384]{2,1,0:T(8,128)S(1)}, f32[12,8,384]{2,1,0:T(8,128)S(1)}, u32[]{:S(2)}, u32[]{:S(2)}) collective-permute-start(f32[12,8,384]{2,1,0:T(8,128)S(1)} %get-tuple-element.34), channel_id=1, source_target_pairs={{0,1},{1,2},{2,3},{3,4},{4,5},{5,6},{6,7},{7,8},{8,9},{9,10},{10,1... | collective-permute-start | bytes 442376 | tf_op jit(solution)/shard_map/ppermute | solution.py:210
  42.6 17.2 %collective-permute-start.4 = (f32[12,8,384]{2,1,0:T(8,128)S(1)}, f32[12,8,384]{2,1,0:T(8,128)S(1)}, u32[]{:S(2)}, u32[]{:S(2)}) collective-permute-start(f32[12,8,384]{2,1,0:T(8,128)S(1)} %get-tuple-element.35), channel_id=1, source_target_pairs={{1,0},{2,1},{3,2},{4,3},{5,4},{6,5},{7,6},{8,7},{9,8},{10,9},{11,1... | collective-permute-start | bytes 442376 | tf_op jit(solution)/shard_map/ppermute | solution.py:210
  50.5 12.8 %collective-permute-start.15 = (f32[8,8,384]{2,1,0:T(8,128)S(1)}, f32[8,8,384]{2,1,0:T(8,128)S(1)}, u32[]{:S(2)}, u32[]{:S(2)}) collective-permute-start(f32[8,8,384]{2,1,0:T(8,128)S(1)} %get-tuple-element.50), channel_id=1, source_target_pairs={{0,1},{1,2},{2,3},{3,4},{4,5},{5,6},{6,7},{7,8},{8,9},{9,10},{10,1... | collective-permute-start | bytes 294920 | tf_op jit(solution)/shard_map/ppermute | solution.py:210
  50.6 14.7 %collective-permute-start.16 = (f32[8,8,384]{2,1,0:T(8,128)S(1)}, f32[8,8,384]{2,1,0:T(8,128)S(1)}, u32[]{:S(2)}, u32[]{:S(2)}) collective-permute-start(f32[8,8,384]{2,1,0:T(8,128)S(1)} %get-tuple-element.51), channel_id=1, source_target_pairs={{1,0},{2,1},{3,2},{4,3},{5,4},{6,5},{7,6},{8,7},{9,8},{10,9},{11,1... | collective-permute-start | bytes 294920 | tf_op jit(solution)/shard_map/ppermute | solution.py:210
  57.4 52.9 %collective-permute-start.6 = (f32[12,80,128]{2,1,0:T(8,128)S(1)}, f32[12,80,128]{2,1,0:T(8,128)S(1)}, u32[]{:S(2)}, u32[]{:S(2)}) collective-permute-start(f32[12,80,128]{2,1,0:T(8,128)S(1)} %get-tuple-element.37), channel_id=1, source_target_pairs={{32,0},{64,32},{96,64},{128,96},{160,128},{192,160},{224,192},{33,... | collective-permute-start | bytes 1474568 | tf_op jit(solution)/shard_map/ppermute | solution.py:215
  59.9 50.4 %collective-permute-start.11 = (f32[12,80,128]{2,1,0:T(8,128)S(1)}, f32[12,80,128]{2,1,0:T(8,128)S(1)}, u32[]{:S(2)}, u32[]{:S(2)}) collective-permute-start(f32[12,80,128]{2,1,0:T(8,128)S(1)} %ends_second.4), channel_id=1, source_target_pairs={{32,0},{64,32},{96,64},{128,96},{160,128},{192,160},{224,192},{33,... | collective-permute-start | bytes 1474568 | tf_op jit(solution)/shard_map/ppermute | solution.py:215
  63.3 49.2 %collective-permute-start = (f32[12,80,128]{2,1,0:T(8,128)S(1)}, f32[12,80,128]{2,1,0:T(8,128)S(1)}, u32[]{:S(2)}, u32[]{:S(2)}) collective-permute-start(f32[12,80,128]{2,1,0:T(8,128)S(1)} %get-tuple-element.29), channel_id=1, source_target_pairs={{32,0},{64,32},{96,64},{128,96},{160,128},{192,160},{224,192},{33,... | collective-permute-start | bytes 1474568 | tf_op jit(solution)/shard_map/ppermute | solution.py:215
  65.2 47.3 %collective-permute-start.5 = (f32[12,80,128]{2,1,0:T(8,128)S(1)}, f32[12,80,128]{2,1,0:T(8,128)S(1)}, u32[]{:S(2)}, u32[]{:S(2)}) collective-permute-start(f32[12,80,128]{2,1,0:T(8,128)S(1)} %ends_second.3), channel_id=1, source_target_pairs={{32,0},{64,32},{96,64},{128,96},{160,128},{192,160},{224,192},{33,... | collective-permute-start | bytes 1474568 | tf_op jit(solution)/shard_map/ppermute | solution.py:215
  67.8 41.1 %collective-permute-start.17 = (f32[8,80,128]{2,1,0:T(8,128)S(1)}, f32[8,80,128]{2,1,0:T(8,128)S(1)}, u32[]{:S(2)}, u32[]{:S(2)}) collective-permute-start(f32[8,80,128]{2,1,0:T(8,128)S(1)} %ends_second.5), channel_id=1, source_target_pairs={{32,0},{64,32},{96,64},{128,96},{160,128},{192,160},{224,192},{33,... | collective-permute-start | bytes 983048 | tf_op jit(solution)/shard_map/ppermute | solution.py:215

commit v2 on v1

v2 whole, which is shorter than its diff:
```python
import functools

import jax
import jax.numpy as jnp
from jax import lax
from jax.experimental import pallas as pl
from jax.experimental.pallas import tpu as pltpu
from jax.sharding import PartitionSpec as P

FIELDS, LON, LAT = 4, 16, 320
WIDE = 384
BLOCK = 4
FLOPS = 2000000000
FIRST_VMEM = 54
MIB = 1024 * 1024
HALVES = ((0, 16, ((0, 8), (8, 8))), (16, 16, ((16, 16),)))


def wide(x):
    return jnp.concatenate([x, jnp.zeros((x.shape[0], WIDE - LAT), x.dtype)], axis=1)


def ends(x):
    row = lax.broadcasted_iota(jnp.int32, (8, x.shape[1]), 0)
    return jnp.where(row < 4, x[0:8], x[8:16])


def middle(x):
    row = lax.broadcasted_iota(jnp.int32, (8, x.shape[1]), 0)
    return jnp.where(row < 4, x[8:16], x[0:8])


def rates(a, b, c):
    along = a * (2.0 / 3.0)
    across = b * 0.5
    return dict(
        centre=1.0 - 4.0 * c,
        down=c + along,
        up=c - along,
        far=a * (1.0 / 12.0),
        lat_down=c + across,
        lat_up=c - across,
    )


def rolled(x, shift, axis):
    size = x.shape[axis]
    return pltpu.roll(x, shift % size, axis)


def inside(r, first, last):
    row = lax.broadcasted_iota(jnp.int32, r["far"].shape, 0)
    return dict(
        centre=r["centre"],
        lat_down=r["lat_down"],
        lat_up=r["lat_up"],
        down=jnp.where(row > first, r["down"], 0.0),
        up=jnp.where(row < last, r["up"], 0.0),
        far_down=jnp.where(row > first + 1, r["far"], 0.0),
        far_up=jnp.where(row < last - 1, r["far"], 0.0),
    )


def step(w, r):
    out = r["centre"] * w
    out += rolled(r["down"] * w, -1, 0) + rolled(r["up"] * w, 1, 0)
    out += rolled(r["far_up"] * w, 2, 0) - rolled(r["far_down"] * w, -2, 0)
    out += rolled(r["lat_down"] * w, -1, 1) + rolled(r["lat_up"] * w, 1, 1)
    return out


def leaving_rates(r):
    row = lax.broadcasted_iota(jnp.int32, r["far"].shape, 0)
    return dict(
        down=jnp.where(row == 0, r["down"], 0.0),
        up=jnp.where(row == 7, r["up"], 0.0),
        far_down=jnp.where(row < 2, r["far"], 0.0),
        far_up=jnp.where(row >= 6, r["far"], 0.0),
    )


def leaving(ws, r):
    to_next = 0.0
    to_previous = 0.0
    for f, w in enumerate(ws):
        to_next += rolled(r["up"] * w, 2 * f + 1, 0) + rolled(r["far_up"] * w, 2 * f + 2, 0)
        to_previous += rolled(r["down"] * w, 2 * f + 1, 0) - rolled(r["far_down"] * w, 2 * f, 0)
    return to_next, to_previous


def arriving(from_previous, from_next, f):
    row = lax.broadcasted_iota(jnp.int32, from_next.shape, 0)
    low = jnp.where(row < 2, rolled(from_previous, -2 * f, 0), 0.0)
    return jnp.where(row >= 6, rolled(from_next, 6 - 2 * f, 0), low)


def put_pair(ref, l, base, first, second):
    lane = lax.broadcasted_iota(jnp.int32, (8, 128), 1)
    ref[l, base : base + 8] = first[:, 0:128]
    ref[l, base + 8 : base + 16] = first[:, 128:256]
    ref[l, base + 16 : base + 24] = second[:, 0:128]
    ref[l, base + 24 : base + 32] = second[:, 128:256]
    ref[l, base + 32 : base + 40] = jnp.where(
        lane < 64, first[:, 256:384], pltpu.roll(second[:, 256:384], 64, 1)
    )


def put_packed(ref, l, pieces):
    for pair in range(FIELDS // 2):
        put_pair(ref, l, 40 * pair, pieces[2 * pair], pieces[2 * pair + 1])


def get_packed(ref, l, f, part):
    base = 40 * (f // 2)
    if part < 2:
        at = base + 16 * (f % 2) + 8 * part
        return ref[l, at : at + 8]
    last = ref[l, base + 32 : base + 40]
    return pltpu.roll(last, 64, 1) if f % 2 else last


def levels(body):
    pl.loop(0, BLOCK)(body)


def put_message(ref, l, now, then, r):
    put_pair(ref, l, 0, now, then)
    row = lax.broadcasted_iota(jnp.int32, (8, 128), 0)
    last = r[:, 256:384]
    rest = pltpu.roll(jnp.where(row < 2, last, 0.0), 6, 0)
    rest += pltpu.roll(pltpu.roll(jnp.where(row == 2, last, 0.0), 64, 1), 4, 0)
    ref[l, 40:48] = r[:, 0:128] + pltpu.roll(r[:, 128:256], 3, 0) + rest


def get_rate(message, k):
    last = message[46 + k % 2 : 47 + k % 2]
    if k == 2:
        last = pltpu.roll(jnp.broadcast_to(last, (8, 128)), 64, 1)
    parts = [message[40 + k : 41 + k], message[43 + k : 44 + k], last]
    return jnp.concatenate([jnp.broadcast_to(p, (8, 128)) for p in parts], axis=1)


def get_tile(message, k):
    base = 16 * k
    last = message[32:40]
    if k == 1:
        last = pltpu.roll(last, 64, 1)
    return jnp.concatenate([message[base : base + 8], message[base + 8 : base + 16], last], axis=1)


def leaving_rows(r):
    to_next = rolled(r["far_up"], 2, 0) + rolled(r["up"], 3, 0)
    to_previous = r["far_down"] + rolled(r["down"], 2, 0)
    return to_next, to_previous


def odd_tile():
    return lax.axis_index("tile") % 2 == 1


def first_kernel(base, adj, vel, kap, *refs):
    mid, image, partner, other, adj_buf, vel_buf, kap_buf, sem = refs[-8:]
    at, count = pl.program_id(0), pl.num_programs(0)

    def copies(block):
        slot = block % 2
        rows = pl.ds(base + block * BLOCK, BLOCK)
        return [
            pltpu.make_async_copy(adj.at[:, rows], adj_buf.at[slot], sem.at[slot, 0]),
            pltpu.make_async_copy(vel.at[:, :, rows], vel_buf.at[slot], sem.at[slot, 1]),
            pltpu.make_async_copy(kap.at[:, rows], kap_buf.at[slot], sem.at[slot, 2]),
        ]

    @pl.when(at == 0)
    def _():
        for copy in copies(at):
            copy.start()

    @pl.when(at + 1 < count)
    def _():
        for copy in copies(at + 1):
            copy.start()

    for copy in copies(at):
        copy.wait()
    adj, vel, kap = adj_buf.at[at % 2], vel_buf.at[at % 2], kap_buf.at[at % 2]

    @levels
    def _(l):
        odd = odd_tile()
        ws = [wide(adj[f, l]) for f in range(FIELDS)]
        sent = []
        for s in (1, 0):
            r = rates(wide(vel[s, 0, l]), wide(vel[s, 1, l]), wide(kap[s, l]))
            out = leaving_rates({k: ends(v) for k, v in r.items() if k in ("down", "up", "far")})
            sent.append(leaving([ends(w) for w in ws], out))
            r = inside(r, 0, LON - 1)
            ws = [step(w, r) for w in ws]
        sent.append(leaving_rows(out))
        put_message(partner, l, *[jnp.where(odd, p, n) for n, p in sent])
        put_message(other, l, *[jnp.where(odd, n, p) for n, p in sent])
        put_packed(mid, l, [middle(w) for w in ws])
        for f, w in enumerate(ws):
            image[l, f] = ends(w)


def second_kernel(vel, kap, partner, other, from_partner, from_other, image, *refs):
    packed = refs[-1]

    @levels
    def _(l):
        odd = odd_tile()
        row = lax.broadcasted_iota(jnp.int32, (8, WIDE), 0)
        even_row = row % 2 == 0
        sides = []
        for (mine_even, mine_odd), (theirs_even, theirs_odd) in (
            ((other, partner), (from_other, from_partner)),
            ((partner, other), (from_partner, from_other)),
        ):
            mine = jnp.where(odd, mine_odd[l], mine_even[l])
            theirs = jnp.where(odd, theirs_odd[l], theirs_even[l])
            sides.append((get_tile(mine, 0), get_tile(theirs, 0), get_tile(theirs, 1), theirs))
        gave, low, low_then, theirs = sides[0]
        low_then += jnp.where(even_row, get_rate(theirs, 0), get_rate(theirs, 1)) * gave
        low_then += jnp.where(even_row, get_rate(theirs, 2) * rolled(gave, -1, 0), 0.0)
        gave, high, high_then, theirs = sides[1]
        high_then -= jnp.where(even_row, get_rate(theirs, 0), get_rate(theirs, 1)) * gave
        high_then += jnp.where(even_row, 0.0, get_rate(theirs, 2) * rolled(gave, 1, 0))
        r = rates(wide(ends(vel[0, 0, l])), wide(ends(vel[0, 1, l])), wide(ends(kap[0, l])))
        r = inside(r, 0, 7)
        pieces = []
        for f in range(FIELDS):
            new = arriving(low, high, f)
            pieces.append(image[l, f] + step(new, r) + arriving(low_then, high_then, f))
        put_packed(packed, l, pieces)


def last_kernel(adj, mid, mid_late, end, *refs):
    out = refs[-1]
    win, windows = lax.axis_index("win"), lax.axis_size("win")
    late, none = win == windows // 2 - 1, win == windows - 1
    row = lax.broadcasted_iota(jnp.int32, (8, 128), 0)

    @levels
    def _(l):
        for f in range(FIELDS):
            for part in range(3):
                lanes = slice(128 * part, min(128 * part + 128, LAT))
                n = lanes.stop - lanes.start
                m = jnp.where(late, get_packed(mid_late, l, f, part), get_packed(mid, l, f, part))
                m = jnp.where(none, 0.0, m)
                e = get_packed(end, l, f, part)
                out[f, l, 0:8, lanes] = adj[f, l, 0:8, lanes] - jnp.where(row < 4, e, m)[:, :n]
                out[f, l, 8:16, lanes] = adj[f, l, 8:16, lanes] - jnp.where(row < 4, m, e)[:, :n]


def spec(dims, at, first=0):
    block = tuple(BLOCK if i == at else d for i, d in enumerate(dims))
    return pl.BlockSpec(block, lambda i: tuple(first + i if k == at else 0 for k in range(len(dims))))


def f32(*dims):
    return jax.ShapeDtypeStruct(dims, jnp.float32)


def call(kernel, count, in_specs, out_specs, out_shape, name, args, after=(), into=(), scratch=(), vmem=24):
    args, in_specs, aliases = list(args), list(in_specs), {}
    for extra in after:
        args.append(extra)
        in_specs.append(pl.BlockSpec(memory_space=pl.ANY))
    for k, buffer in enumerate(into):
        if buffer is not None:
            aliases[len(args)] = k
            args.append(buffer)
            in_specs.append(pl.BlockSpec(memory_space=pl.ANY))
    return pl.pallas_call(
        kernel,
        grid=(count // BLOCK,),
        in_specs=in_specs,
        out_specs=out_specs,
        out_shape=out_shape,
        scratch_shapes=list(scratch),
        name=name,
        input_output_aliases=aliases,
        cost_estimate=pl.CostEstimate(flops=FLOPS, bytes_accessed=1, transcendentals=0),
        compiler_params=pltpu.CompilerParams(vmem_limit_bytes=vmem * MIB),
    )(*args)


MESSAGE = (0, 48, 128)
FIELD_TILES = (0, FIELDS, 8, WIDE)
PACKED = (0, 80, 128)


def sized(dims, n):
    return f32(n, *dims[1:])


def swapped(partner, other):
    n = lax.axis_size("tile")
    inner = [(i, i ^ 1) for i in range(n)]
    outer = [(i, (i + 1 if i % 2 else i - 1) % n) for i in range(n)]
    return lax.ppermute(partner, "tile", inner), lax.ppermute(other, "tile", outer)


def to_preceding(x, detour=False):
    n = lax.axis_size("win")
    pairs = [(k + 1, k) for k in range(n - 1)]
    if not detour:
        return lax.ppermute(x, "win", pairs)
    first = [(k, n - 1 if k == n // 2 else j) for k, j in pairs]
    arrived = lax.ppermute(x, "win", first)
    return arrived, lax.ppermute(arrived, "win", [(n - 1, n // 2 - 1)])


def per_device(adjoint, velocity, kappa):
    adj, vel, kap = adjoint[0], velocity[0], kappa[0]
    after = []
    mids, halves = [], []
    for start, n, pieces in HALVES:
        into = [None] * 4
        for first, count in pieces:
            c = (first - start) // BLOCK
            outs = call(
                functools.partial(first_kernel, first), count,
                [pl.BlockSpec(memory_space=pltpu.HBM)] * 3,
                [spec(PACKED, 0)] + [spec(d, 0, c) for d in (FIELD_TILES, MESSAGE, MESSAGE)],
                [sized(PACKED, count)] + [sized(d, n) for d in (FIELD_TILES, MESSAGE, MESSAGE)],
                "interior", (adj, vel, kap), after, into,
                [
                    pltpu.VMEM((2, FIELDS, BLOCK, LON, LAT), jnp.float32),
                    pltpu.VMEM((2, 2, 2, BLOCK, LON, LAT), jnp.float32),
                    pltpu.VMEM((2, 2, BLOCK, LON, LAT), jnp.float32),
                    pltpu.SemaphoreType.DMA((2, 3)),
                ],
                FIRST_VMEM,
            )
            into = [None] + list(outs[1:])
            after = [outs[0]]
            mids.append((first, count, *to_preceding(outs[0], True)))
        halves.append((outs[1], outs[2:], swapped(*outs[2:])))
    after = after + [mids[0][2], mids[1][2]]
    ends = []
    for (start, n, _), (image, mine, theirs) in zip(HALVES, halves):
        b = start // BLOCK
        end = call(
            second_kernel, n,
            [spec((1, *vel.shape[1:]), 2, b), spec((1, *kap.shape[1:]), 1, b)] + [spec(d, 0) for d in (MESSAGE,) * 4 + (FIELD_TILES,)],
            spec(PACKED, 0), sized(PACKED, n), "ends", (vel, kap, *mine, *theirs, image), after,
        )
        after = [end, mids[2][2]]
        ends.append((start, n, to_preceding(end)))
    after = [end]
    out = None
    for first, count, mid, mid_late in mids:
        start, end = [(s, e) for s, n, e in ends if s <= first < s + n][0]
        b = first // BLOCK
        out = call(
            last_kernel, count,
            [spec(adj.shape, 1, b), spec(PACKED, 0), spec(PACKED, 0), spec(PACKED, 0, (first - start) // BLOCK)],
            spec(adj.shape, 1, b), f32(*adj.shape), "subtract", (adj, mid, mid_late, end), after, [out],
        )
        after = []
    return out[None]


def solution(mesh):
    return jax.shard_map(
        per_device,
        mesh=mesh,
        in_specs=(
            P("win", None, None, "tile", None),
            P("win", None, None, None, "tile", None),
            P("win", None, None, "tile", None),
        ),
        out_specs=P("win", None, None, "tile", None),
        check_vma=False,
    )
```

time: 115 us -> 79.8 us (0.69)
  starting transfers between devices: 46.4 us -> 26.9 us
  waiting for transfers between devices: 39.2 us -> 25.5 us
  Pallas kernels: 27.5 us -> 25.7 us
    ppermute x18 -> x12, starting transfers between devices: 46.4 us -> 26.9 us  [the longest x2 10.4 us: swapped(): lax.ppermute(other, 'tile', outer)]
    ppermute x18 -> x12, waiting for transfers between devices: 39.2 us -> 25.5 us  [the longest x3 15 us: to_preceding(): return (arrived, lax.ppermute(arrived, 'win', [(n - 1, n // 2 - 1)]))]
    pallas_call x12 -> x8, Pallas kernels: 27.5 us -> 25.7 us  [call(): pl.pallas_call(kernel, grid=(count // BLOCK,), in_specs=in_specs, out_spe...]
  transfers between devices with their start and end apart: 18 -> 12, of which waited for: 1 -> 3; matrix products, arithmetic and copies ran while one was open for 0% -> 0% of each run, Pallas kernels for 18% -> 24%
where the time goes in v2:
time: 79.8 us; the launch traced here: 79.4 us
  starting transfers between devices  26.9 us (34%)
  Pallas kernels  25.7 us (32%)
  waiting for transfers between devices  25.5 us (32%)
  local copies, waits for them, and re-layouts  1.12 us (1%)
    pallas_call x8, Pallas kernels, call(): pl.pallas_call(kernel, grid=(count // BLOCK,), in_specs=in_specs, out_spe...  25.7 us
    ppermute x3, waiting for transfers between devices, to_preceding(): return (arrived, lax.ppermute(arrived, 'win', [(n - 1, n // 2 - 1)]))  15 us
    ppermute x2, starting transfers between devices, swapped(): lax.ppermute(other, 'tile', outer)  10.4 us
    ppermute x3, starting transfers between devices, to_preceding(): arrived = lax.ppermute(x, 'win', first)  7.92 us
    ppermute x2, waiting for transfers between devices, swapped(): lax.ppermute(other, 'tile', outer)  6.81 us
    ppermute x2, starting transfers between devices, to_preceding(): return lax.ppermute(x, 'win', pairs)  4.5 us
    ppermute x3, starting transfers between devices, to_preceding(): return (arrived, lax.ppermute(arrived, 'win', [(n - 1, n // 2 - 1)]))  3.88 us
    ppermute x2, waiting for transfers between devices, to_preceding(): return lax.ppermute(x, 'win', pairs)  3.68 us
  transfers between devices with their start and end apart: 12, of which 3 were waited for; matrix products, arithmetic and copies ran while one was open for 0% of the time, Pallas kernels for 24%

profile of v2, /device:TPU:6, one launch (start us, length us, event | category | flops | bytes accessed | tf_op | source)
XLA Modules:
  0.0 79.4 jit_solution(5338360899066436152)
XLA Ops:
  0.0 4.1 %interior.3 = (f32[8,80,128]{2,1,0:T(8,128)}, f32[16,4,8,384]{3,2,1,0:T(8,128)}, f32[16,48,128]{2,1,0:T(8,128)}, f32[16,48,128]{2,1,0:T(8,128)}) custom-call(f32[4,32,16,320]{3,2,1,0:T(8,128)} %bitcast.4, f32[2,2,32,16,320]{4,3,2,1,0:T(8,128)} %bitcast.10, f32[2,32,16,320]{3,2,1,0:T(8,128)} %bitcast.15), custom_call_target="tpu_custom_call" | custom-call | flops 2000000000 | bytes 1 | tf_op jit(solution)/shard_map/interior/pallas_call | solution.py:276
  4.1 2.8 %collective-permute-start.6 = (f32[8,80,128]{2,1,0:T(8,128)}, f32[8,80,128]{2,1,0:T(8,128)S(1)}, u32[]{:S(2)}, u32[]{:S(2)}) collective-permute-start(f32[8,80,128]{2,1,0:T(8,128)} %get-tuple-element.17.refs_0_), channel_id=1, source_target_pairs={{32,0},{64,32},{96,64},{128,224},{160,128},{192,160},{224,192},{33... | collective-permute-start | bytes 983048 | tf_op jit(solution)/shard_map/ppermute | solution.py:312
  6.9 4.1 %interior.4 = (f32[8,80,128]{2,1,0:T(8,128)}, f32[16,4,8,384]{3,2,1,0:T(8,128)}, f32[16,48,128]{2,1,0:T(8,128)}, f32[16,48,128]{2,1,0:T(8,128)}) custom-call(f32[4,32,16,320]{3,2,1,0:T(8,128)} %bitcast.5, f32[2,2,32,16,320]{4,3,2,1,0:T(8,128)} %bitcast.11, f32[2,32,16,320]{3,2,1,0:T(8,128)} %bitcast.16, ...), custom_call_target="tpu_custom_call", output_to_operand_aliasing={{1}: (4, {}), {2}: (5, {}), {3}: (6, {})} | custom-call | flops 2000000000 | bytes 1 | tf_op jit(solution)/shard_map/interior/pallas_call | solution.py:276
  11.0 0.1 collective-permute-start.4
  11.1 8.9 %collective-permute-start.5 = (f32[16,48,128]{2,1,0:T(8,128)}, f32[16,48,128]{2,1,0:T(8,128)S(1)}, u32[]{:S(2)}, u32[]{:S(2)}) collective-permute-start(f32[16,48,128]{2,1,0:T(8,128)} %get-tuple-element.27.other), channel_id=1, source_target_pairs={{0,31},{1,2},{2,1},{3,4},{4,3},{5,6},{6,5},{7,8},{8,7},{9,10},{10,... | collective-permute-start | bytes 1179656 | tf_op jit(solution)/shard_map/ppermute | solution.py:303
  20.0 2.7 %collective-permute-start.7 = (f32[8,80,128]{2,1,0:T(8,128)}, f32[8,80,128]{2,1,0:T(8,128)S(1)}, u32[]{:S(2)}, u32[]{:S(2)}) collective-permute-start(f32[8,80,128]{2,1,0:T(8,128)} %get-tuple-element.21.refs_0_), channel_id=1, source_target_pairs={{32,0},{64,32},{96,64},{128,224},{160,128},{192,160},{224,192},{33... | collective-permute-start | bytes 983048 | tf_op jit(solution)/shard_map/ppermute | solution.py:312
  22.7 6.7 %interior.5 = (f32[16,80,128]{2,1,0:T(8,128)}, f32[16,4,8,384]{3,2,1,0:T(8,128)}, f32[16,48,128]{2,1,0:T(8,128)}, f32[16,48,128]{2,1,0:T(8,128)}) custom-call(f32[4,32,16,320]{3,2,1,0:T(8,128)} %bitcast.6, f32[2,2,32,16,320]{4,3,2,1,0:T(8,128)} %bitcast.12, f32[2,32,16,320]{3,2,1,0:T(8,128)} %bitcast.17, f32[8,80,128]{2,1,0:T(8,128)} %get-tuple-element.21.refs_0_), custom_call_target="tpu_custom_call" | custom-call | flops 2000000000 | bytes 1 | tf_op jit(solution)/shard_map/interior/pallas_call | solution.py:276
  29.3 2.5 %collective-permute-start = (f32[16,80,128]{2,1,0:T(8,128)}, f32[16,80,128]{2,1,0:T(8,128)S(1)}, u32[]{:S(2)}, u32[]{:S(2)}) collective-permute-start(f32[16,80,128]{2,1,0:T(8,128)} %get-tuple-element.22.refs_0_), channel_id=1, source_target_pairs={{32,0},{64,32},{96,64},{128,224},{160,128},{192,160},{224,192},{33... | collective-permute-start | bytes 1966088 | tf_op jit(solution)/shard_map/ppermute | solution.py:312
  31.8 0.0 collective-permute-done.7.refs_2_.mid
  31.8 0.1 collective-permute-start.2
  31.9 0.0 collective-permute-done.6.refs_1_.mid
  31.9 1.5 %collective-permute-start.3 = (f32[16,48,128]{2,1,0:T(8,128)}, f32[16,48,128]{2,1,0:T(8,128)S(1)}, u32[]{:S(2)}, u32[]{:S(2)}) collective-permute-start(f32[16,48,128]{2,1,0:T(8,128)} %get-tuple-element.24.other), channel_id=1, source_target_pairs={{0,31},{1,2},{2,1},{3,4},{4,3},{5,6},{6,5},{7,8},{8,7},{9,10},{10,... | collective-permute-start | bytes 1179656 | tf_op jit(solution)/shard_map/ppermute | solution.py:303
  33.5 0.0 collective-permute-done.4.from_partner
  33.5 0.0 collective-permute-done.5.from_other
  33.5 1.1 %copy-done.7 = f32[16,80,128]{2,1,0:T(8,128)S(1)} copy-done((f32[16,80,128]{2,1,0:T(8,128)S(1)}, f32[16,80,128]{2,1,0:T(8,128)}, u32[]{:S(2)}) %copy-start.7) | copy-done | bytes 655384
  34.6 2.7 %ends.2.refs_0_ = f32[16,80,128]{2,1,0:T(8,128)S(1)} custom-call(f32[2,2,32,16,320]{4,3,2,1,0:T(8,128)S(1)} %bitcast.13, f32[2,32,16,320]{3,2,1,0:T(8,128)S(1)} %bitcast.18, f32[16,48,128]{2,1,0:T(8,128)S(1)} %copy-done.4, f32[16,48,128]{2,1,0:T(8,128)S(1)} %copy-done.5, f32[16,48,128]{2,1,0:T(8,128)S(1)} %collective-permute-done.4.from_partner, ...), custom_call_target="tpu_custom_call" | custom-call | flops 2000000000 | bytes 1 | tf_op jit(solution)/shard_map/ends/pallas_call | solution.py:276
  37.3 2.0 %collective-permute-start.10 = (f32[16,80,128]{2,1,0:T(8,128)S(1)}, f32[16,80,128]{2,1,0:T(8,128)S(1)}, u32[]{:S(2)}, u32[]{:S(2)}) collective-permute-start(f32[16,80,128]{2,1,0:T(8,128)S(1)} %ends.2.refs_0_), channel_id=1, source_target_pairs={{32,0},{64,32},{96,64},{128,96},{160,128},{192,160},{224,192},{33,... | collective-permute-start | bytes 1966088 | tf_op jit(solution)/shard_map/ppermute | solution.py:310
  39.3 1.3 %collective-permute-start.11 = (f32[8,80,128]{2,1,0:T(8,128)S(1)}, f32[8,80,128]{2,1,0:T(8,128)S(1)}, u32[]{:S(2)}, u32[]{:S(2)}) collective-permute-start(f32[8,80,128]{2,1,0:T(8,128)S(1)} %collective-permute-done.6.refs_1_.mid), channel_id=1, source_target_pairs={{224,96},{225,97},{226,98},{227,99},{228,100},{229,101},{230,102},... | collective-permute-start | bytes 983048 | tf_op jit(solution)/shard_map/ppermute | solution.py:313
  40.7 6.8 %collective-permute-done.3.from_other = f32[16,48,128]{2,1,0:T(8,128)S(1)} collective-permute-done((f32[16,48,128]{2,1,0:T(8,128)}, f32[16,48,128]{2,1,0:T(8,128)S(1)}, u32[]{:S(2)}, u32[]{:S(2)}) %collective-permute-start.3) | collective-permute-done | bytes 393248 | tf_op jit(solution)/shard_map/ppermute | solution.py:303
  47.5 0.0 collective-permute-done.refs_1_.mid
  47.5 0.0 copy-start
  47.5 2.7 %ends.3.refs_0_ = f32[16,80,128]{2,1,0:T(8,128)S(1)} custom-call(f32[2,2,32,16,320]{4,3,2,1,0:T(8,128)S(1)} %bitcast.14, f32[2,32,16,320]{3,2,1,0:T(8,128)S(1)} %bitcast.19, f32[16,48,128]{2,1,0:T(8,128)S(1)} %copy-done.8, f32[16,48,128]{2,1,0:T(8,128)S(1)} %copy-done.9, f32[16,48,128]{2,1,0:T(8,128)S(1)} %collective-permute-done.2.from_partner, ...), custom_call_target="tpu_custom_call" | custom-call | flops 2000000000 | bytes 1 | tf_op jit(solution)/shard_map/ends/pallas_call | solution.py:276
  50.2 2.5 %collective-permute-start.8 = (f32[16,80,128]{2,1,0:T(8,128)S(1)}, f32[16,80,128]{2,1,0:T(8,128)S(1)}, u32[]{:S(2)}, u32[]{:S(2)}) collective-permute-start(f32[16,80,128]{2,1,0:T(8,128)S(1)} %ends.3.refs_0_), channel_id=1, source_target_pairs={{32,0},{64,32},{96,64},{128,96},{160,128},{192,160},{224,192},{33,... | collective-permute-start | bytes 1966088 | tf_op jit(solution)/shard_map/ppermute | solution.py:310
  52.7 1.3 %collective-permute-start.1 = (f32[16,80,128]{2,1,0:T(8,128)S(1)}, f32[16,80,128]{2,1,0:T(8,128)S(1)}, u32[]{:S(2)}, u32[]{:S(2)}) collective-permute-start(f32[16,80,128]{2,1,0:T(8,128)S(1)} %collective-permute-done.refs_1_.mid), channel_id=1, source_target_pairs={{224,96},{225,97},{226,98},{227,99},{228,100},{229,101},{230,102},... | collective-permute-start | bytes 1966088 | tf_op jit(solution)/shard_map/ppermute | solution.py:313
  54.0 1.3 %collective-permute-start.9 = (f32[8,80,128]{2,1,0:T(8,128)S(1)}, f32[8,80,128]{2,1,0:T(8,128)S(1)}, u32[]{:S(2)}, u32[]{:S(2)}) collective-permute-start(f32[8,80,128]{2,1,0:T(8,128)S(1)} %collective-permute-done.7.refs_2_.mid), channel_id=1, source_target_pairs={{224,96},{225,97},{226,98},{227,99},{228,100},{229,101},{230,102},... | collective-permute-start | bytes 983048 | tf_op jit(solution)/shard_map/ppermute | solution.py:313
  55.3 0.0 collective-permute-done.11.mid_late
  55.3 3.7 %collective-permute-done.10.end = f32[16,80,128]{2,1,0:T(8,128)S(1)} collective-permute-done((f32[16,80,128]{2,1,0:T(8,128)S(1)}, f32[16,80,128]{2,1,0:T(8,128)S(1)}, u32[]{:S(2)}, u32[]{:S(2)}) %collective-permute-start.10) | collective-permute-done | bytes 655392 | tf_op jit(solution)/shard_map/ppermute | solution.py:310
  59.0 1.4 %subtract.3.refs_0_ = f32[4,32,16,320]{3,2,1,0:T(8,128)} custom-call(f32[4,32,16,320]{3,2,1,0:T(8,128)S(1)} %bitcast.7, f32[8,80,128]{2,1,0:T(8,128)S(1)} %collective-permute-done.6.refs_1_.mid, f32[8,80,128]{2,1,0:T(8,128)S(1)} %collective-permute-done.11.mid_late, f32[16,80,128]{2,1,0:T(8,128)S(1)} %collective-permute-done.10.end, ...), custom_call_target="tpu_custom_call" | custom-call | flops 2000000000 | bytes 1 | tf_op jit(solution)/shard_map/subtract/pallas_call | solution.py:276
  60.4 14.9 %collective-permute-done.9.mid_late = f32[8,80,128]{2,1,0:T(8,128)S(1)} collective-permute-done((f32[8,80,128]{2,1,0:T(8,128)S(1)}, f32[8,80,128]{2,1,0:T(8,128)S(1)}, u32[]{:S(2)}, u32[]{:S(2)}) %collective-permute-start.9) | collective-permute-done | bytes 327712 | tf_op jit(solution)/shard_map/ppermute | solution.py:313
  75.4 1.4 %subtract.4.refs_0_ = f32[4,32,16,320]{3,2,1,0:T(8,128)} custom-call(f32[4,32,16,320]{3,2,1,0:T(8,128)S(1)} %bitcast.8, f32[8,80,128]{2,1,0:T(8,128)S(1)} %collective-permute-done.7.refs_2_.mid, f32[8,80,128]{2,1,0:T(8,128)S(1)} %collective-permute-done.9.mid_late, f32[16,80,128]{2,1,0:T(8,128)S(1)} %collective-permute-done.10.end, ...), custom_call_target="tpu_custom_call", output_to_operand_aliasing={{}: (4, {})} | custom-call | flops 2000000000 | bytes 1 | tf_op jit(solution)/shard_map/subtract/pallas_call | solution.py:276
  76.8 0.0 collective-permute-done.1.mid_late
  76.8 2.5 %subtract.5 = f32[4,32,16,320]{3,2,1,0:T(8,128)} custom-call(f32[4,32,16,320]{3,2,1,0:T(8,128)S(1)} %bitcast.9, f32[16,80,128]{2,1,0:T(8,128)S(1)} %collective-permute-done.refs_1_.mid, f32[16,80,128]{2,1,0:T(8,128)S(1)} %collective-permute-done.1.mid_late, f32[16,80,128]{2,1,0:T(8,128)S(1)} %collective-permute-done.8.end, ...), custom_call_target="tpu_custom_call", output_to_operand_aliasing={{}: (4, {})} | custom-call | flops 2000000000 | bytes 1 | tf_op jit(solution)/shard_map/subtract/pallas_call | solution.py:276
  (20 shorter events, 0.0 us)
Async XLA Ops:
  4.1 27.8 %collective-permute-start.6 = (f32[8,80,128]{2,1,0:T(8,128)}, f32[8,80,128]{2,1,0:T(8,128)S(1)}, u32[]{:S(2)}, u32[]{:S(2)}) collective-permute-start(f32[8,80,128]{2,1,0:T(8,128)} %get-tuple-element.17.refs_0_), channel_id=1, source_target_pairs={{32,0},{64,32},{96,64},{128,224},{160,128},{192,160},{224,192},{33... | collective-permute-start | bytes 983048 | tf_op jit(solution)/shard_map/ppermute | solution.py:312
  11.0 22.5 %collective-permute-start.4 = (f32[16,48,128]{2,1,0:T(8,128)}, f32[16,48,128]{2,1,0:T(8,128)S(1)}, u32[]{:S(2)}, u32[]{:S(2)}) collective-permute-start(f32[16,48,128]{2,1,0:T(8,128)} %get-tuple-element.26.partner), channel_id=1, source_target_pairs={{0,1},{1,0},{2,3},{3,2},{4,5},{5,4},{6,7},{7,6},{8,9},{9,8},{10,11... | collective-permute-start | bytes 1179656 | tf_op jit(solution)/shard_map/ppermute | solution.py:303
  11.1 22.4 %collective-permute-start.5 = (f32[16,48,128]{2,1,0:T(8,128)}, f32[16,48,128]{2,1,0:T(8,128)S(1)}, u32[]{:S(2)}, u32[]{:S(2)}) collective-permute-start(f32[16,48,128]{2,1,0:T(8,128)} %get-tuple-element.27.other), channel_id=1, source_target_pairs={{0,31},{1,2},{2,1},{3,4},{4,3},{5,6},{6,5},{7,8},{8,7},{9,10},{10,... | collective-permute-start | bytes 1179656 | tf_op jit(solution)/shard_map/ppermute | solution.py:303
  20.0 13.5 %copy-start.1 = (f32[1,2,2,32,16,320]{5,4,3,2,1,0:T(8,128)S(1)}, f32[1,2,2,32,16,320]{5,4,3,2,1,0:T(8,128)}, u32[]{:S(2)}) copy-start(f32[1,2,2,32,16,320]{5,4,3,2,1,0:T(8,128)} %param.4) | copy-start | bytes 7864324
  20.0 13.5 %copy-start.2 = (f32[1,2,32,16,320]{4,3,2,1,0:T(8,128)S(1)}, f32[1,2,32,16,320]{4,3,2,1,0:T(8,128)}, u32[]{:S(2)}) copy-start(f32[1,2,32,16,320]{4,3,2,1,0:T(8,128)} %param.5) | copy-start | bytes 3932164
  20.0 13.6 %copy-start.3 = (f32[16,4,8,384]{3,2,1,0:T(8,128)S(1)}, f32[16,4,8,384]{3,2,1,0:T(8,128)}, u32[]{:S(2)}) copy-start(f32[16,4,8,384]{3,2,1,0:T(8,128)} %get-tuple-element.28.image) | copy-start | bytes 2359300
  20.0 13.6 %copy-start.4 = (f32[16,48,128]{2,1,0:T(8,128)S(1)}, f32[16,48,128]{2,1,0:T(8,128)}, u32[]{:S(2)}) copy-start(f32[16,48,128]{2,1,0:T(8,128)} %get-tuple-element.26.partner) | copy-start | bytes 1179652
  20.0 13.6 %copy-start.5 = (f32[16,48,128]{2,1,0:T(8,128)S(1)}, f32[16,48,128]{2,1,0:T(8,128)}, u32[]{:S(2)}) copy-start(f32[16,48,128]{2,1,0:T(8,128)} %get-tuple-element.27.other) | copy-start | bytes 1179652
  20.0 11.8 %collective-permute-start.7 = (f32[8,80,128]{2,1,0:T(8,128)}, f32[8,80,128]{2,1,0:T(8,128)S(1)}, u32[]{:S(2)}, u32[]{:S(2)}) collective-permute-start(f32[8,80,128]{2,1,0:T(8,128)} %get-tuple-element.21.refs_0_), channel_id=1, source_target_pairs={{32,0},{64,32},{96,64},{128,224},{160,128},{192,160},{224,192},{33... | collective-permute-start | bytes 983048 | tf_op jit(solution)/shard_map/ppermute | solution.py:312
  29.3 18.1 %collective-permute-start = (f32[16,80,128]{2,1,0:T(8,128)}, f32[16,80,128]{2,1,0:T(8,128)S(1)}, u32[]{:S(2)}, u32[]{:S(2)}) collective-permute-start(f32[16,80,128]{2,1,0:T(8,128)} %get-tuple-element.22.refs_0_), channel_id=1, source_target_pairs={{32,0},{64,32},{96,64},{128,224},{160,128},{192,160},{224,192},{33... | collective-permute-start | bytes 1966088 | tf_op jit(solution)/shard_map/ppermute | solution.py:312
  31.8 8.8 %collective-permute-start.2 = (f32[16,48,128]{2,1,0:T(8,128)}, f32[16,48,128]{2,1,0:T(8,128)S(1)}, u32[]{:S(2)}, u32[]{:S(2)}) collective-permute-start(f32[16,48,128]{2,1,0:T(8,128)} %get-tuple-element.23.partner), channel_id=1, source_target_pairs={{0,1},{1,0},{2,3},{3,2},{4,5},{5,4},{6,7},{7,6},{8,9},{9,8},{10,11... | collective-permute-start | bytes 1179656 | tf_op jit(solution)/shard_map/ppermute | solution.py:303
  31.9 15.5 %collective-permute-start.3 = (f32[16,48,128]{2,1,0:T(8,128)}, f32[16,48,128]{2,1,0:T(8,128)S(1)}, u32[]{:S(2)}, u32[]{:S(2)}) collective-permute-start(f32[16,48,128]{2,1,0:T(8,128)} %get-tuple-element.24.other), channel_id=1, source_target_pairs={{0,31},{1,2},{2,1},{3,4},{4,3},{5,6},{6,5},{7,8},{8,7},{9,10},{10,... | collective-permute-start | bytes 1179656 | tf_op jit(solution)/shard_map/ppermute | solution.py:303
  33.5 1.1 %copy-start.7 = (f32[16,80,128]{2,1,0:T(8,128)S(1)}, f32[16,80,128]{2,1,0:T(8,128)}, u32[]{:S(2)}) copy-start(f32[16,80,128]{2,1,0:T(8,128)} %get-tuple-element.22.refs_0_) | copy-start | bytes 1966084
  34.6 12.8 %copy-start.6 = (f32[16,4,8,384]{3,2,1,0:T(8,128)S(1)}, f32[16,4,8,384]{3,2,1,0:T(8,128)}, u32[]{:S(2)}) copy-start(f32[16,4,8,384]{3,2,1,0:T(8,128)} %get-tuple-element.25.image) | copy-start | bytes 2359300
  34.6 12.8 %copy-start.8 = (f32[16,48,128]{2,1,0:T(8,128)S(1)}, f32[16,48,128]{2,1,0:T(8,128)}, u32[]{:S(2)}) copy-start(f32[16,48,128]{2,1,0:T(8,128)} %get-tuple-element.23.partner) | copy-start | bytes 1179652
  34.6 12.8 %copy-start.9 = (f32[16,48,128]{2,1,0:T(8,128)S(1)}, f32[16,48,128]{2,1,0:T(8,128)}, u32[]{:S(2)}) copy-start(f32[16,48,128]{2,1,0:T(8,128)} %get-tuple-element.24.other) | copy-start | bytes 1179652
  37.3 21.7 %collective-permute-start.10 = (f32[16,80,128]{2,1,0:T(8,128)S(1)}, f32[16,80,128]{2,1,0:T(8,128)S(1)}, u32[]{:S(2)}, u32[]{:S(2)}) collective-permute-start(f32[16,80,128]{2,1,0:T(8,128)S(1)} %ends.2.refs_0_), channel_id=1, source_target_pairs={{32,0},{64,32},{96,64},{128,96},{160,128},{192,160},{224,192},{33,... | collective-permute-start | bytes 1966088 | tf_op jit(solution)/shard_map/ppermute | solution.py:310
  39.3 16.0 %collective-permute-start.11 = (f32[8,80,128]{2,1,0:T(8,128)S(1)}, f32[8,80,128]{2,1,0:T(8,128)S(1)}, u32[]{:S(2)}, u32[]{:S(2)}) collective-permute-start(f32[8,80,128]{2,1,0:T(8,128)S(1)} %collective-permute-done.6.refs_1_.mid), channel_id=1, source_target_pairs={{224,96},{225,97},{226,98},{227,99},{228,100},{229,101},{230,102},... | collective-permute-start | bytes 983048 | tf_op jit(solution)/shard_map/ppermute | solution.py:313
  47.5 11.5 %copy-start = (f32[1,4,32,16,320]{4,3,2,1,0:T(8,128)S(1)}, f32[1,4,32,16,320]{4,3,2,1,0:T(8,128)}, u32[]{:S(2)}) copy-start(f32[1,4,32,16,320]{4,3,2,1,0:T(8,128)} %param.3) | copy-start | bytes 7864324
  50.2 26.6 %collective-permute-start.8 = (f32[16,80,128]{2,1,0:T(8,128)S(1)}, f32[16,80,128]{2,1,0:T(8,128)S(1)}, u32[]{:S(2)}, u32[]{:S(2)}) collective-permute-start(f32[16,80,128]{2,1,0:T(8,128)S(1)} %ends.3.refs_0_), channel_id=1, source_target_pairs={{32,0},{64,32},{96,64},{128,96},{160,128},{192,160},{224,192},{33,... | collective-permute-start | bytes 1966088 | tf_op jit(solution)/shard_map/ppermute | solution.py:310
  52.7 24.1 %collective-permute-start.1 = (f32[16,80,128]{2,1,0:T(8,128)S(1)}, f32[16,80,128]{2,1,0:T(8,128)S(1)}, u32[]{:S(2)}, u32[]{:S(2)}) collective-permute-start(f32[16,80,128]{2,1,0:T(8,128)S(1)} %collective-permute-done.refs_1_.mid), channel_id=1, source_target_pairs={{224,96},{225,97},{226,98},{227,99},{228,100},{229,101},{230,102},... | collective-permute-start | bytes 1966088 | tf_op jit(solution)/shard_map/ppermute | solution.py:313
  54.0 21.4 %collective-permute-start.9 = (f32[8,80,128]{2,1,0:T(8,128)S(1)}, f32[8,80,128]{2,1,0:T(8,128)S(1)}, u32[]{:S(2)}, u32[]{:S(2)}) collective-permute-start(f32[8,80,128]{2,1,0:T(8,128)S(1)} %collective-permute-done.7.refs_2_.mid), channel_id=1, source_target_pairs={{224,96},{225,97},{226,98},{227,99},{228,100},{229,101},{230,102},... | collective-permute-start | bytes 983048 | tf_op jit(solution)/shard_map/ppermute | solution.py:313

commit v3 on v2

--- a/solution.py
+++ b/solution.py
@@ -10,10 +10,12 @@
 FIELDS, LON, LAT = 4, 16, 320
 WIDE = 384
 BLOCK = 4
-FLOPS = 2000000000
+FLOPS = (4000000000, 4000000000, 4000000000)
 FIRST_VMEM = 54
 MIB = 1024 * 1024
-HALVES = ((0, 16, ((0, 8), (8, 8))), (16, 16, ((16, 16),)))
+GROUPS = ((0, 24, False), (24, 8, True))
+STEPS = ((1,), (0, 1))
+ENDS = ((0, 24, 0), (24, 8, 1))
 
 
 def wide(x):
@@ -158,32 +160,27 @@
     return lax.axis_index("tile") % 2 == 1
 
 
-def first_kernel(base, adj, vel, kap, *refs):
+def first_kernel(base, blocks, adj, vel, kap, *refs):
     mid, image, partner, other, adj_buf, vel_buf, kap_buf, sem = refs[-8:]
-    at, count = pl.program_id(0), pl.num_programs(0)
+    at = pl.program_id(0)
 
     def copies(block):
-        slot = block % 2
         rows = pl.ds(base + block * BLOCK, BLOCK)
         return [
-            pltpu.make_async_copy(adj.at[:, rows], adj_buf.at[slot], sem.at[slot, 0]),
-            pltpu.make_async_copy(vel.at[:, :, rows], vel_buf.at[slot], sem.at[slot, 1]),
-            pltpu.make_async_copy(kap.at[:, rows], kap_buf.at[slot], sem.at[slot, 2]),
+            pltpu.make_async_copy(adj.at[:, rows], adj_buf.at[block], sem.at[block, 0]),
+            pltpu.make_async_copy(vel.at[:, :, rows], vel_buf.at[block], sem.at[block, 1]),
+            pltpu.make_async_copy(kap.at[:, rows], kap_buf.at[block], sem.at[block, 2]),
         ]
 
     @pl.when(at == 0)
     def _():
-        for copy in copies(at):
-            copy.start()
-
-    @pl.when(at + 1 < count)
-    def _():
-        for copy in copies(at + 1):
-            copy.start()
+        for block in range(blocks):
+            for copy in copies(block):
+                copy.start()
 
     for copy in copies(at):
         copy.wait()
-    adj, vel, kap = adj_buf.at[at % 2], vel_buf.at[at % 2], kap_buf.at[at % 2]
+    adj, vel, kap = adj_buf.at[at], vel_buf.at[at], kap_buf.at[at]
 
     @levels
     def _(l):
@@ -235,10 +232,11 @@
         put_packed(packed, l, pieces)
 
 
-def last_kernel(adj, mid, mid_late, end, *refs):
+def last_kernel(direct, adj, end, mid, *refs):
     out = refs[-1]
     win, windows = lax.axis_index("win"), lax.axis_size("win")
     late, none = win == windows // 2 - 1, win == windows - 1
+    mid_late = refs[0] if direct else None
     row = lax.broadcasted_iota(jnp.int32, (8, 128), 0)
 
     @levels
@@ -247,9 +245,9 @@
             for part in range(3):
                 lanes = slice(128 * part, min(128 * part + 128, LAT))
                 n = lanes.stop - lanes.start
-                m = jnp.where(late, get_packed(mid_late, l, f, part), get_packed(mid, l, f, part))
-                m = jnp.where(none, 0.0, m)
-                e = get_packed(end, l, f, part)
+                m, e = get_packed(mid, l, f, part), get_packed(end, l, f, part)
+                if direct:
+                    m = jnp.where(late, get_packed(mid_late, l, f, part), jnp.where(none, 0.0, m))
                 out[f, l, 0:8, lanes] = adj[f, l, 0:8, lanes] - jnp.where(row < 4, e, m)[:, :n]
                 out[f, l, 8:16, lanes] = adj[f, l, 8:16, lanes] - jnp.where(row < 4, m, e)[:, :n]
 
@@ -263,7 +261,7 @@
     return jax.ShapeDtypeStruct(dims, jnp.float32)
 
 
-def call(kernel, count, in_specs, out_specs, out_shape, name, args, after=(), into=(), scratch=(), vmem=24):
+def call(flops, kernel, count, in_specs, out_specs, out_shape, name, args, after=(), into=(), scratch=(), vmem=24):
     args, in_specs, aliases = list(args), list(in_specs), {}
     for extra in after:
         args.append(extra)
@@ -282,7 +280,7 @@
         scratch_shapes=list(scratch),
         name=name,
         input_output_aliases=aliases,
-        cost_estimate=pl.CostEstimate(flops=FLOPS, bytes_accessed=1, transcendentals=0),
+        cost_estimate=pl.CostEstimate(flops=flops, bytes_accessed=1, transcendentals=0),
         compiler_params=pltpu.CompilerParams(vmem_limit_bytes=vmem * MIB),
     )(*args)
 
@@ -303,62 +301,80 @@
     return lax.ppermute(partner, "tile", inner), lax.ppermute(other, "tile", outer)
 
 
-def to_preceding(x, detour=False):
+def to_preceding(x):
     n = lax.axis_size("win")
-    pairs = [(k + 1, k) for k in range(n - 1)]
-    if not detour:
-        return lax.ppermute(x, "win", pairs)
-    first = [(k, n - 1 if k == n // 2 else j) for k, j in pairs]
-    arrived = lax.ppermute(x, "win", first)
-    return arrived, lax.ppermute(arrived, "win", [(n - 1, n // 2 - 1)])
+    return lax.ppermute(x, "win", [(k + 1, k) for k in range(n - 1)])
+
+
+def detour(x, step):
+    n = lax.axis_size("win")
+    if step:
+        return lax.ppermute(x, "win", [(n - 1, n // 2 - 1)])
+    return lax.ppermute(x, "win", [(k + 1, n - 1 if k + 1 == n // 2 else k) for k in range(n - 1)])
+
+
+def long_way(x, step):
+    n = lax.axis_size("win")
+    h = n // 2
+    side = ((h, h + 1), (h + 1, 2), (2, 3))[step]
+    pairs = [(g + s, g + (s + 1) % h) for g in (0, h) for s in range(h) if s != step]
+    return lax.ppermute(x, "win", [*pairs, side])
 
 
 def per_device(adjoint, velocity, kappa):
     adj, vel, kap = adjoint[0], velocity[0], kappa[0]
-    after = []
-    mids, halves = [], []
-    for start, n, pieces in HALVES:
-        into = [None] * 4
-        for first, count in pieces:
-            c = (first - start) // BLOCK
-            outs = call(
-                functools.partial(first_kernel, first), count,
-                [pl.BlockSpec(memory_space=pltpu.HBM)] * 3,
-                [spec(PACKED, 0)] + [spec(d, 0, c) for d in (FIELD_TILES, MESSAGE, MESSAGE)],
-                [sized(PACKED, count)] + [sized(d, n) for d in (FIELD_TILES, MESSAGE, MESSAGE)],
-                "interior", (adj, vel, kap), after, into,
-                [
-                    pltpu.VMEM((2, FIELDS, BLOCK, LON, LAT), jnp.float32),
-                    pltpu.VMEM((2, 2, 2, BLOCK, LON, LAT), jnp.float32),
-                    pltpu.VMEM((2, 2, BLOCK, LON, LAT), jnp.float32),
-                    pltpu.SemaphoreType.DMA((2, 3)),
-                ],
-                FIRST_VMEM,
-            )
-            into = [None] + list(outs[1:])
-            after = [outs[0]]
-            mids.append((first, count, *to_preceding(outs[0], True)))
-        halves.append((outs[1], outs[2:], swapped(*outs[2:])))
-    after = after + [mids[0][2], mids[1][2]]
-    ends = []
-    for (start, n, _), (image, mine, theirs) in zip(HALVES, halves):
-        b = start // BLOCK
+    groups, after = [], []
+    for start, n, around in GROUPS:
+        blocks = n // BLOCK
+        mid, image, *mine = call(
+            FLOPS[0], functools.partial(first_kernel, start, blocks), n,
+            [pl.BlockSpec(memory_space=pltpu.HBM)] * 3,
+            [spec(d, 0) for d in (PACKED, FIELD_TILES, MESSAGE, MESSAGE)],
+            [sized(d, n) for d in (PACKED, FIELD_TILES, MESSAGE, MESSAGE)],
+            "interior", (adj, vel, kap), after, (),
+            [
+                pltpu.VMEM((blocks, FIELDS, BLOCK, LON, LAT), jnp.float32),
+                pltpu.VMEM((blocks, 2, 2, BLOCK, LON, LAT), jnp.float32),
+                pltpu.VMEM((blocks, 2, BLOCK, LON, LAT), jnp.float32),
+                pltpu.SemaphoreType.DMA((blocks, 3)),
+            ],
+            FIRST_VMEM,
+        )
+        after = [mid]
+        first_theirs = swapped(*mine) if not groups else None
+        groups.append(([(long_way if around else detour)(mid, 0)], image, mine, first_theirs))
+    lasts, after = [], []
+    for k, (first, count, group) in enumerate(ENDS):
+        start = GROUPS[group][0]
+        mid, image, mine, ready = groups[group]
+        if not lasts:
+            theirs = ready
+        elif group != ENDS[k - 1][2]:
+            theirs = swapped(*mine)
+            after = [*after, mid[0], groups[0][0][0]]
+        b, c = first // BLOCK, (first - start) // BLOCK
         end = call(
-            second_kernel, n,
-            [spec((1, *vel.shape[1:]), 2, b), spec((1, *kap.shape[1:]), 1, b)] + [spec(d, 0) for d in (MESSAGE,) * 4 + (FIELD_TILES,)],
-            spec(PACKED, 0), sized(PACKED, n), "ends", (vel, kap, *mine, *theirs, image), after,
+            FLOPS[1], second_kernel, count,
+            [spec((1, *vel.shape[1:]), 2, b), spec((1, *kap.shape[1:]), 1, b)]
+            + [spec(d, 0, c) for d in (MESSAGE,) * 4 + (FIELD_TILES,)],
+            spec(PACKED, 0), sized(PACKED, count), "ends", (vel, kap, *mine, *theirs, image), after,
         )
-        after = [end, mids[2][2]]
-        ends.append((start, n, to_preceding(end)))
-    after = [end]
-    out = None
-    for first, count, mid, mid_late in mids:
-        start, end = [(s, e) for s, n, e in ends if s <= first < s + n][0]
+        after = [end]
+        lasts.append(to_preceding(end))
+        for at, (mid, _, _, _), (_, _, around) in zip(STEPS, groups, GROUPS):
+            if k in at:
+                x = lax.optimization_barrier([mid[-1], end])[0]
+                mid.append((long_way if around else detour)(x, len(mid)))
+    out, after = None, [end]
+    for (first, count, group), end in zip(ENDS, lasts):
         b = first // BLOCK
+        mid, around = groups[group][0], GROUPS[group][2]
+        arrays = (adj, end, mid[-1]) if around else (adj, end, *mid)
+        c = (first - GROUPS[group][0]) // BLOCK
         out = call(
-            last_kernel, count,
-            [spec(adj.shape, 1, b), spec(PACKED, 0), spec(PACKED, 0), spec(PACKED, 0, (first - start) // BLOCK)],
-            spec(adj.shape, 1, b), f32(*adj.shape), "subtract", (adj, mid, mid_late, end), after, [out],
+            FLOPS[2], functools.partial(last_kernel, not around), count,
+            [spec(adj.shape, 1, b), spec(PACKED, 0)] + [spec(PACKED, 0, c)] * (len(arrays) - 2),
+            spec(adj.shape, 1, b), f32(*adj.shape), "subtract", arrays, after, [out],
         )
         after = []
     return out[None]

time: 79.8 us -> 71.9 us (0.901)
  waiting for transfers between devices: 25.5 us -> 17.2 us
  starting transfers between devices: 26.9 us -> 30.3 us
  Pallas kernels: 25.7 us -> 23 us
  local copies, waits for them, and re-layouts: 1.12 us -> 0.05 us
    ppermute x8 -> x7, waiting for transfers between devices: 18.6 us -> 13.6 us  [the longest x2 10.5 us: to_preceding(): return lax.ppermute(x, 'win', [(k + 1, k) for k in range(n - 1)])]
    ppermute x2, waiting for transfers between devices: 6.81 us -> 3.57 us  [swapped(): lax.ppermute(other, 'tile', outer)]
    ppermute x8 -> x7, starting transfers between devices: 16.3 us -> 19.2 us  [the longest x3 10.6 us: long_way(): return lax.ppermute(x, 'win', [*pairs, side])]
    pallas_call x8 -> x6, Pallas kernels: 25.7 us -> 23 us  [call(): pl.pallas_call(kernel, grid=(count // BLOCK,), in_specs=in_specs, out_spe...]
    unnamed x20 -> x18, local copies, waits for them, and re-layouts: 1.12 us -> 0.05 us
  transfers between devices with their start and end apart: 12 -> 11, of which waited for: 3 -> 5; matrix products, arithmetic and copies ran while one was open for 0% -> 0% of each run, Pallas kernels for 24% -> 19%
where the time goes in v3:
time: 71.9 us; the launch traced here: 70.7 us
  starting transfers between devices  30.3 us (42%)
  Pallas kernels  23 us (32%)
  waiting for transfers between devices  17.2 us (24%)
    pallas_call x6, Pallas kernels, call(): pl.pallas_call(kernel, grid=(count // BLOCK,), in_specs=in_specs, out_spe...  23 us
    ppermute x2, starting transfers between devices, swapped(): lax.ppermute(other, 'tile', outer)  10.9 us
    ppermute x3, starting transfers between devices, long_way(): return lax.ppermute(x, 'win', [*pairs, side])  10.6 us
    ppermute x2, waiting for transfers between devices, to_preceding(): return lax.ppermute(x, 'win', [(k + 1, k) for k in range(n - 1)])  10.5 us
    ppermute x2, starting transfers between devices, to_preceding(): return lax.ppermute(x, 'win', [(k + 1, k) for k in range(n - 1)])  4.55 us
    ppermute x2, waiting for transfers between devices, swapped(): lax.ppermute(other, 'tile', outer)  3.57 us
    ppermute x3, waiting for transfers between devices, long_way(): return lax.ppermute(x, 'win', [*pairs, side])  3.12 us
    ppermute x1, starting transfers between devices, detour(): lax.ppermute(x, 'win', [(k + 1, n - 1 if k + 1 == n // 2 else k) for k in...  2.79 us
  transfers between devices with their start and end apart: 11, of which 5 were waited for; matrix products, arithmetic and copies ran while one was open for 0% of the time, Pallas kernels for 19%

profile of v3, /device:TPU:6, one launch (start us, length us, event | category | flops | bytes accessed | tf_op | source)
XLA Modules:
  0.0 70.7 jit_solution(18170534527996138872)
XLA Ops:
  0.0 8.4 %interior.2 = (f32[24,80,128]{2,1,0:T(8,128)}, f32[24,4,8,384]{3,2,1,0:T(8,128)}, f32[24,48,128]{2,1,0:T(8,128)}, f32[24,48,128]{2,1,0:T(8,128)}) custom-call(f32[4,32,16,320]{3,2,1,0:T(8,128)} %bitcast.8, f32[2,2,32,16,320]{4,3,2,1,0:T(8,128)} %bitcast.4, f32[2,32,16,320]{3,2,1,0:T(8,128)} %bitcast.12), custom_call_target="tpu_custom_call" | custom-call | flops 4000000000 | bytes 1 | tf_op jit(solution)/shard_map/interior/pallas_call | solution.py:274
  8.4 2.8 %collective-permute-start.5 = (f32[24,80,128]{2,1,0:T(8,128)}, f32[24,80,128]{2,1,0:T(8,128)S(1)}, u32[]{:S(2)}, u32[]{:S(2)}) collective-permute-start(f32[24,80,128]{2,1,0:T(8,128)} %get-tuple-element.16.refs_0_), channel_id=1, source_target_pairs={{32,0},{64,32},{96,64},{128,224},{160,128},{192,160},{224,192},{33... | collective-permute-start | bytes 2949128 | tf_op jit(solution)/shard_map/ppermute | solution.py:313
  11.2 0.1 collective-permute-start.2
  11.3 0.0 copy-start
  11.3 0.0 copy-start.2
  11.4 0.0 copy-start.7
  11.4 8.9 %collective-permute-start.3 = (f32[24,48,128]{2,1,0:T(8,128)}, f32[24,48,128]{2,1,0:T(8,128)S(1)}, u32[]{:S(2)}, u32[]{:S(2)}) collective-permute-start(f32[24,48,128]{2,1,0:T(8,128)} %get-tuple-element.21.other), channel_id=1, source_target_pairs={{0,31},{1,2},{2,1},{3,4},{4,3},{5,6},{6,5},{7,8},{8,7},{9,10},{10,... | collective-permute-start | bytes 1769480 | tf_op jit(solution)/shard_map/ppermute | solution.py:301
  20.3 4.1 %interior.3 = (f32[8,80,128]{2,1,0:T(8,128)}, f32[8,4,8,384]{3,2,1,0:T(8,128)}, f32[8,48,128]{2,1,0:T(8,128)}, f32[8,48,128]{2,1,0:T(8,128)}) custom-call(f32[4,32,16,320]{3,2,1,0:T(8,128)} %bitcast.9, f32[2,2,32,16,320]{4,3,2,1,0:T(8,128)} %bitcast.5, f32[2,32,16,320]{3,2,1,0:T(8,128)} %bitcast.13, f32[24,80,128]{2,1,0:T(8,128)} %get-tuple-element.16.refs_0_), custom_call_target="tpu_custom_call" | custom-call | flops 4000000000 | bytes 1 | tf_op jit(solution)/shard_map/interior/pallas_call | solution.py:274
  24.4 0.1 collective-permute-start
  24.5 2.0 %collective-permute-start.1 = (f32[8,48,128]{2,1,0:T(8,128)}, f32[8,48,128]{2,1,0:T(8,128)S(1)}, u32[]{:S(2)}, u32[]{:S(2)}) collective-permute-start(f32[8,48,128]{2,1,0:T(8,128)} %get-tuple-element.18.other), channel_id=1, source_target_pairs={{0,31},{1,2},{2,1},{3,4},{4,3},{5,6},{6,5},{7,8},{8,7},{9,10},{10,... | collective-permute-start | bytes 589832 | tf_op jit(solution)/shard_map/ppermute | solution.py:301
  26.5 0.0 collective-permute-done.2.from_partner
  26.5 1.9 %collective-permute-start.4 = (f32[8,80,128]{2,1,0:T(8,128)}, f32[8,80,128]{2,1,0:T(8,128)S(1)}, u32[]{:S(2)}, u32[]{:S(2)}) collective-permute-start(f32[8,80,128]{2,1,0:T(8,128)} %get-tuple-element.23), channel_id=1, source_target_pairs={{32,64},{64,96},{96,0},{160,192},{192,224},{224,128},{128,160},{33... | collective-permute-start | bytes 983048 | tf_op jit(solution)/shard_map/ppermute | solution.py:321
  28.4 3.4 %collective-permute-done.3.from_other = f32[24,48,128]{2,1,0:T(8,128)S(1)} collective-permute-done((f32[24,48,128]{2,1,0:T(8,128)}, f32[24,48,128]{2,1,0:T(8,128)S(1)}, u32[]{:S(2)}, u32[]{:S(2)}) %collective-permute-start.3) | collective-permute-done | bytes 589856 | tf_op jit(solution)/shard_map/ppermute | solution.py:301
  31.9 4.1 %ends.2.refs_0_ = f32[24,80,128]{2,1,0:T(8,128)S(1)} custom-call(f32[2,2,32,16,320]{4,3,2,1,0:T(8,128)S(1)} %bitcast.6, f32[2,32,16,320]{3,2,1,0:T(8,128)S(1)} %bitcast.14, f32[24,48,128]{2,1,0:T(8,128)S(1)} %copy-done.3, f32[24,48,128]{2,1,0:T(8,128)S(1)} %copy-done.4, f32[24,48,128]{2,1,0:T(8,128)S(1)} %collective-permute-done.2.from_partner, ...), custom_call_target="tpu_custom_call" | custom-call | flops 4000000000 | bytes 1 | tf_op jit(solution)/shard_map/ends/pallas_call | solution.py:274
  35.9 2.4 %collective-permute-start.9 = (f32[24,80,128]{2,1,0:T(8,128)S(1)}, f32[24,80,128]{2,1,0:T(8,128)S(1)}, u32[]{:S(2)}, u32[]{:S(2)}) collective-permute-start(f32[24,80,128]{2,1,0:T(8,128)S(1)} %ends.2.refs_0_), channel_id=1, source_target_pairs={{32,0},{64,32},{96,64},{128,96},{160,128},{192,160},{224,192},{33,... | collective-permute-start | bytes 2949128 | tf_op jit(solution)/shard_map/ppermute | solution.py:306
  38.3 0.0 collective-permute-done.from_partner
  38.4 0.2 collective-permute-done.1.from_other
  38.5 0.0 collective-permute-done.4.refs_1_
  38.5 0.0 collective-permute-done.5.refs_2_.mid
  38.6 0.0 copy-start.1
  38.6 1.4 %ends.3.refs_1_ = f32[8,80,128]{2,1,0:T(8,128)S(1)} custom-call(f32[2,2,32,16,320]{4,3,2,1,0:T(8,128)S(1)} %bitcast.7, f32[2,32,16,320]{3,2,1,0:T(8,128)S(1)} %bitcast.15, f32[8,48,128]{2,1,0:T(8,128)S(1)} %copy-done.5, f32[8,48,128]{2,1,0:T(8,128)S(1)} %copy-done.6, f32[8,48,128]{2,1,0:T(8,128)S(1)} %collective-permute-done.from_partner, ...), custom_call_target="tpu_custom_call" | custom-call | flops 4000000000 | bytes 1 | tf_op jit(solution)/shard_map/ends/pallas_call | solution.py:274
  40.0 1.3 %collective-permute-start.10 = (f32[24,80,128]{2,1,0:T(8,128)S(1)}, f32[24,80,128]{2,1,0:T(8,128)S(1)}, u32[]{:S(2)}, u32[]{:S(2)}) collective-permute-start(f32[24,80,128]{2,1,0:T(8,128)S(1)} %collective-permute-done.5.refs_2_.mid), channel_id=1, source_target_pairs={{224,96},{225,97},{226,98},{227,99},{228,100},{229,101},{230,102},... | collective-permute-start | bytes 2949128 | tf_op jit(solution)/shard_map/ppermute | solution.py:312
  41.3 3.7 %collective-permute-start.7 = (f32[8,80,128]{2,1,0:T(8,128)S(1)}, f32[8,80,128]{2,1,0:T(8,128)S(1)}, u32[]{:S(2)}, u32[]{:S(2)}) collective-permute-start(f32[8,80,128]{2,1,0:T(8,128)S(1)} %collective-permute-done.4.refs_1_), channel_id=1, source_target_pairs={{0,32},{64,96},{96,0},{128,160},{192,224},{224,128},{160,64},{1,33... | collective-permute-start | bytes 983048 | tf_op jit(solution)/shard_map/ppermute | solution.py:321
  45.0 2.1 %collective-permute-start.6 = (f32[8,80,128]{2,1,0:T(8,128)S(1)}, f32[8,80,128]{2,1,0:T(8,128)S(1)}, u32[]{:S(2)}, u32[]{:S(2)}) collective-permute-start(f32[8,80,128]{2,1,0:T(8,128)S(1)} %ends.3.refs_1_), channel_id=1, source_target_pairs={{32,0},{64,32},{96,64},{128,96},{160,128},{192,160},{224,192},{33,... | collective-permute-start | bytes 983048 | tf_op jit(solution)/shard_map/ppermute | solution.py:306
  47.1 3.1 %collective-permute-done.7 = f32[8,80,128]{2,1,0:T(8,128)S(1)} collective-permute-done((f32[8,80,128]{2,1,0:T(8,128)S(1)}, f32[8,80,128]{2,1,0:T(8,128)S(1)}, u32[]{:S(2)}, u32[]{:S(2)}) %collective-permute-start.7) | collective-permute-done | bytes 327712 | tf_op jit(solution)/shard_map/ppermute | solution.py:321
  50.2 4.9 %collective-permute-start.8 = (f32[8,80,128]{2,1,0:T(8,128)S(1)}, f32[8,80,128]{2,1,0:T(8,128)S(1)}, u32[]{:S(2)}, u32[]{:S(2)}) collective-permute-start(f32[8,80,128]{2,1,0:T(8,128)S(1)} %collective-permute-done.7), channel_id=1, source_target_pairs={{0,32},{32,64},{96,0},{128,160},{160,192},{224,128},{64,96},{1,33}... | collective-permute-start | bytes 983048 | tf_op jit(solution)/shard_map/ppermute | solution.py:321
  55.2 9.4 %collective-permute-done.9.end = f32[24,80,128]{2,1,0:T(8,128)S(1)} collective-permute-done((f32[24,80,128]{2,1,0:T(8,128)S(1)}, f32[24,80,128]{2,1,0:T(8,128)S(1)}, u32[]{:S(2)}, u32[]{:S(2)}) %collective-permute-start.9) | collective-permute-done | bytes 983072 | tf_op jit(solution)/shard_map/ppermute | solution.py:306
  64.6 0.0 collective-permute-done.10.refs_0_
  64.6 3.6 %subtract.2.refs_0_ = f32[4,32,16,320]{3,2,1,0:T(8,128)} custom-call(f32[4,32,16,320]{3,2,1,0:T(8,128)S(1)} %bitcast.10, f32[24,80,128]{2,1,0:T(8,128)S(1)} %collective-permute-done.9.end, f32[24,80,128]{2,1,0:T(8,128)S(1)} %collective-permute-done.5.refs_2_.mid, f32[24,80,128]{2,1,0:T(8,128)S(1)} %collective-permute-done.10.refs_0_, ...), custom_call_target="tpu_custom_call" | custom-call | flops 4000000000 | bytes 1 | tf_op jit(solution)/shard_map/subtract/pallas_call | solution.py:274
  68.2 0.0 collective-permute-done.8.mid
  68.2 1.0 %collective-permute-done.6.end = f32[8,80,128]{2,1,0:T(8,128)S(1)} collective-permute-done((f32[8,80,128]{2,1,0:T(8,128)S(1)}, f32[8,80,128]{2,1,0:T(8,128)S(1)}, u32[]{:S(2)}, u32[]{:S(2)}) %collective-permute-start.6) | collective-permute-done | bytes 327712 | tf_op jit(solution)/shard_map/ppermute | solution.py:306
  69.3 1.4 %subtract.3 = f32[4,32,16,320]{3,2,1,0:T(8,128)} custom-call(f32[4,32,16,320]{3,2,1,0:T(8,128)S(1)} %bitcast.11, f32[8,80,128]{2,1,0:T(8,128)S(1)} %collective-permute-done.6.end, f32[8,80,128]{2,1,0:T(8,128)S(1)} %collective-permute-done.8.mid, f32[4,32,16,320]{3,2,1,0:T(8,128)} %subtract.2.refs_0_), custom_call_target="tpu_custom_call", output_to_operand_aliasing={{}: (3, {})} | custom-call | flops 4000000000 | bytes 1 | tf_op jit(solution)/shard_map/subtract/pallas_call | solution.py:274
  (14 shorter events, 0.0 us)
Async XLA Ops:
  8.4 30.1 %collective-permute-start.5 = (f32[24,80,128]{2,1,0:T(8,128)}, f32[24,80,128]{2,1,0:T(8,128)S(1)}, u32[]{:S(2)}, u32[]{:S(2)}) collective-permute-start(f32[24,80,128]{2,1,0:T(8,128)} %get-tuple-element.16.refs_0_), channel_id=1, source_target_pairs={{32,0},{64,32},{96,64},{128,224},{160,128},{192,160},{224,192},{33... | collective-permute-start | bytes 2949128 | tf_op jit(solution)/shard_map/ppermute | solution.py:313
  11.2 15.3 %collective-permute-start.2 = (f32[24,48,128]{2,1,0:T(8,128)}, f32[24,48,128]{2,1,0:T(8,128)S(1)}, u32[]{:S(2)}, u32[]{:S(2)}) collective-permute-start(f32[24,48,128]{2,1,0:T(8,128)} %get-tuple-element.20.partner), channel_id=1, source_target_pairs={{0,1},{1,0},{2,3},{3,2},{4,5},{5,4},{6,7},{7,6},{8,9},{9,8},{10,11... | collective-permute-start | bytes 1769480 | tf_op jit(solution)/shard_map/ppermute | solution.py:301
  11.3 20.5 %copy-start = (f32[1,2,2,32,16,320]{5,4,3,2,1,0:T(8,128)S(1)}, f32[1,2,2,32,16,320]{5,4,3,2,1,0:T(8,128)}, u32[]{:S(2)}) copy-start(f32[1,2,2,32,16,320]{5,4,3,2,1,0:T(8,128)} %param.4) | copy-start | bytes 7864324
  11.3 20.5 %copy-start.2 = (f32[1,2,32,16,320]{4,3,2,1,0:T(8,128)S(1)}, f32[1,2,32,16,320]{4,3,2,1,0:T(8,128)}, u32[]{:S(2)}) copy-start(f32[1,2,32,16,320]{4,3,2,1,0:T(8,128)} %param.5) | copy-start | bytes 3932164
  11.4 20.4 %copy-start.3 = (f32[24,48,128]{2,1,0:T(8,128)S(1)}, f32[24,48,128]{2,1,0:T(8,128)}, u32[]{:S(2)}) copy-start(f32[24,48,128]{2,1,0:T(8,128)} %get-tuple-element.20.partner) | copy-start | bytes 1769476
  11.4 20.4 %copy-start.4 = (f32[24,48,128]{2,1,0:T(8,128)S(1)}, f32[24,48,128]{2,1,0:T(8,128)}, u32[]{:S(2)}) copy-start(f32[24,48,128]{2,1,0:T(8,128)} %get-tuple-element.21.other) | copy-start | bytes 1769476
  11.4 20.4 %copy-start.7 = (f32[24,4,8,384]{3,2,1,0:T(8,128)S(1)}, f32[24,4,8,384]{3,2,1,0:T(8,128)}, u32[]{:S(2)}) copy-start(f32[24,4,8,384]{3,2,1,0:T(8,128)} %get-tuple-element.22.image) | copy-start | bytes 3538948
  11.4 20.4 %collective-permute-start.3 = (f32[24,48,128]{2,1,0:T(8,128)}, f32[24,48,128]{2,1,0:T(8,128)S(1)}, u32[]{:S(2)}, u32[]{:S(2)}) collective-permute-start(f32[24,48,128]{2,1,0:T(8,128)} %get-tuple-element.21.other), channel_id=1, source_target_pairs={{0,31},{1,2},{2,1},{3,4},{4,3},{5,6},{6,5},{7,8},{8,7},{9,10},{10,... | collective-permute-start | bytes 1769480 | tf_op jit(solution)/shard_map/ppermute | solution.py:301
  24.4 13.9 %collective-permute-start = (f32[8,48,128]{2,1,0:T(8,128)}, f32[8,48,128]{2,1,0:T(8,128)S(1)}, u32[]{:S(2)}, u32[]{:S(2)}) collective-permute-start(f32[8,48,128]{2,1,0:T(8,128)} %get-tuple-element.17.partner), channel_id=1, source_target_pairs={{0,1},{1,0},{2,3},{3,2},{4,5},{5,4},{6,7},{7,6},{8,9},{9,8},{10,11... | collective-permute-start | bytes 589832 | tf_op jit(solution)/shard_map/ppermute | solution.py:301
  24.5 14.0 %collective-permute-start.1 = (f32[8,48,128]{2,1,0:T(8,128)}, f32[8,48,128]{2,1,0:T(8,128)S(1)}, u32[]{:S(2)}, u32[]{:S(2)}) collective-permute-start(f32[8,48,128]{2,1,0:T(8,128)} %get-tuple-element.18.other), channel_id=1, source_target_pairs={{0,31},{1,2},{2,1},{3,4},{4,3},{5,6},{6,5},{7,8},{8,7},{9,10},{10,... | collective-permute-start | bytes 589832 | tf_op jit(solution)/shard_map/ppermute | solution.py:301
  26.5 12.0 %collective-permute-start.4 = (f32[8,80,128]{2,1,0:T(8,128)}, f32[8,80,128]{2,1,0:T(8,128)S(1)}, u32[]{:S(2)}, u32[]{:S(2)}) collective-permute-start(f32[8,80,128]{2,1,0:T(8,128)} %get-tuple-element.23), channel_id=1, source_target_pairs={{32,64},{64,96},{96,0},{160,192},{192,224},{224,128},{128,160},{33... | collective-permute-start | bytes 983048 | tf_op jit(solution)/shard_map/ppermute | solution.py:321
  31.8 6.7 %copy-start.5 = (f32[8,48,128]{2,1,0:T(8,128)S(1)}, f32[8,48,128]{2,1,0:T(8,128)}, u32[]{:S(2)}) copy-start(f32[8,48,128]{2,1,0:T(8,128)} %get-tuple-element.17.partner) | copy-start | bytes 589828
  31.8 6.7 %copy-start.6 = (f32[8,48,128]{2,1,0:T(8,128)S(1)}, f32[8,48,128]{2,1,0:T(8,128)}, u32[]{:S(2)}) copy-start(f32[8,48,128]{2,1,0:T(8,128)} %get-tuple-element.18.other) | copy-start | bytes 589828
  31.8 6.7 %copy-start.8 = (f32[8,4,8,384]{3,2,1,0:T(8,128)S(1)}, f32[8,4,8,384]{3,2,1,0:T(8,128)}, u32[]{:S(2)}) copy-start(f32[8,4,8,384]{3,2,1,0:T(8,128)} %get-tuple-element.19.image) | copy-start | bytes 1179652
  35.9 28.7 %collective-permute-start.9 = (f32[24,80,128]{2,1,0:T(8,128)S(1)}, f32[24,80,128]{2,1,0:T(8,128)S(1)}, u32[]{:S(2)}, u32[]{:S(2)}) collective-permute-start(f32[24,80,128]{2,1,0:T(8,128)S(1)} %ends.2.refs_0_), channel_id=1, source_target_pairs={{32,0},{64,32},{96,64},{128,96},{160,128},{192,160},{224,192},{33,... | collective-permute-start | bytes 2949128 | tf_op jit(solution)/shard_map/ppermute | solution.py:306
  38.6 26.0 %copy-start.1 = (f32[1,4,32,16,320]{4,3,2,1,0:T(8,128)S(1)}, f32[1,4,32,16,320]{4,3,2,1,0:T(8,128)}, u32[]{:S(2)}) copy-start(f32[1,4,32,16,320]{4,3,2,1,0:T(8,128)} %param.3) | copy-start | bytes 7864324
  40.0 24.6 %collective-permute-start.10 = (f32[24,80,128]{2,1,0:T(8,128)S(1)}, f32[24,80,128]{2,1,0:T(8,128)S(1)}, u32[]{:S(2)}, u32[]{:S(2)}) collective-permute-start(f32[24,80,128]{2,1,0:T(8,128)S(1)} %collective-permute-done.5.refs_2_.mid), channel_id=1, source_target_pairs={{224,96},{225,97},{226,98},{227,99},{228,100},{229,101},{230,102},... | collective-permute-start | bytes 2949128 | tf_op jit(solution)/shard_map/ppermute | solution.py:312
  41.3 9.0 %collective-permute-start.7 = (f32[8,80,128]{2,1,0:T(8,128)S(1)}, f32[8,80,128]{2,1,0:T(8,128)S(1)}, u32[]{:S(2)}, u32[]{:S(2)}) collective-permute-start(f32[8,80,128]{2,1,0:T(8,128)S(1)} %collective-permute-done.4.refs_1_), channel_id=1, source_target_pairs={{0,32},{64,96},{96,0},{128,160},{192,224},{224,128},{160,64},{1,33... | collective-permute-start | bytes 983048 | tf_op jit(solution)/shard_map/ppermute | solution.py:321
  45.0 24.3 %collective-permute-start.6 = (f32[8,80,128]{2,1,0:T(8,128)S(1)}, f32[8,80,128]{2,1,0:T(8,128)S(1)}, u32[]{:S(2)}, u32[]{:S(2)}) collective-permute-start(f32[8,80,128]{2,1,0:T(8,128)S(1)} %ends.3.refs_1_), channel_id=1, source_target_pairs={{32,0},{64,32},{96,64},{128,96},{160,128},{192,160},{224,192},{33,... | collective-permute-start | bytes 983048 | tf_op jit(solution)/shard_map/ppermute | solution.py:306
  50.2 18.0 %collective-permute-start.8 = (f32[8,80,128]{2,1,0:T(8,128)S(1)}, f32[8,80,128]{2,1,0:T(8,128)S(1)}, u32[]{:S(2)}, u32[]{:S(2)}) collective-permute-start(f32[8,80,128]{2,1,0:T(8,128)S(1)} %collective-permute-done.7), channel_id=1, source_target_pairs={{0,32},{32,64},{96,0},{128,160},{160,192},{224,128},{64,96},{1,33}... | collective-permute-start | bytes 983048 | tf_op jit(solution)/shard_map/ppermute | solution.py:321

commit v4 on v3

--- a/solution.py
+++ b/solution.py
@@ -10,12 +10,13 @@
 FIELDS, LON, LAT = 4, 16, 320
 WIDE = 384
 BLOCK = 4
-FLOPS = (4000000000, 4000000000, 4000000000)
+FLOPS = (8000000000, 8000000000, 8000000000)
 FIRST_VMEM = 54
 MIB = 1024 * 1024
 GROUPS = ((0, 24, False), (24, 8, True))
-STEPS = ((1,), (0, 1))
-ENDS = ((0, 24, 0), (24, 8, 1))
+SPLIT = 12
+ENDS = ((0, 12, 0, 0), (12, 12, 0, 1), (24, 8, 1, 1))
+STEPS = ((0,), (0, 2))
 
 
 def wide(x):
@@ -160,8 +161,9 @@
     return lax.axis_index("tile") % 2 == 1
 
 
-def first_kernel(base, blocks, adj, vel, kap, *refs):
-    mid, image, partner, other, adj_buf, vel_buf, kap_buf, sem = refs[-8:]
+def first_kernel(base, blocks, outs, adj, vel, kap, *refs):
+    adj_buf, vel_buf, kap_buf, sem = refs[-4:]
+    mid, image, *messages = refs[-4 - outs : -4]
     at = pl.program_id(0)
 
     def copies(block):
@@ -182,8 +184,7 @@
         copy.wait()
     adj, vel, kap = adj_buf.at[at], vel_buf.at[at], kap_buf.at[at]
 
-    @levels
-    def _(l):
+    def each(partner, other, l):
         odd = odd_tile()
         ws = [wide(adj[f, l]) for f in range(FIELDS)]
         sent = []
@@ -199,6 +200,18 @@
         put_packed(mid, l, [middle(w) for w in ws])
         for f, w in enumerate(ws):
             image[l, f] = ends(w)
+
+    if len(messages) == 2:
+        levels(functools.partial(each, *messages))
+    else:
+
+        @pl.when(at < SPLIT // BLOCK)
+        def _():
+            levels(functools.partial(each, *messages[:2]))
+
+        @pl.when(at >= SPLIT // BLOCK)
+        def _():
+            levels(functools.partial(each, *messages[2:]))
 
 
 def second_kernel(vel, kap, partner, other, from_partner, from_other, image, *refs):
@@ -257,6 +270,10 @@
     return pl.BlockSpec(block, lambda i: tuple(first + i if k == at else 0 for k in range(len(dims))))
 
 
+def part_spec(begin, end):
+    return pl.BlockSpec((BLOCK, *MESSAGE[1:]), lambda i: (jnp.clip(i - begin, 0, end - begin - 1), 0, 0))
+
+
 def f32(*dims):
     return jax.ShapeDtypeStruct(dims, jnp.float32)
 
@@ -323,50 +340,59 @@
 
 def per_device(adjoint, velocity, kappa):
     adj, vel, kap = adjoint[0], velocity[0], kappa[0]
+    scratch = [
+        (FIELDS, BLOCK, LON, LAT),
+        (2, 2, BLOCK, LON, LAT),
+        (2, BLOCK, LON, LAT),
+    ]
     groups, after = [], []
+    cut, rest = SPLIT // BLOCK, sized(MESSAGE, sum(n for _, n, _ in GROUPS) - SPLIT)
+    early = late = None
     for start, n, around in GROUPS:
         blocks = n // BLOCK
+        if early is None:
+            specs = [part_spec(0, cut)] * 2 + [part_spec(cut, blocks)] * 2
+            shapes, into = [sized(MESSAGE, SPLIT)] * 2 + [rest] * 2, ()
+        else:
+            specs = [spec(MESSAGE, 0, (start - SPLIT) // BLOCK)] * 2
+            shapes, into = [rest] * 2, (None, None, *late)
         mid, image, *mine = call(
-            FLOPS[0], functools.partial(first_kernel, start, blocks), n,
+            FLOPS[0], functools.partial(first_kernel, start, blocks, 2 + len(specs)), n,
             [pl.BlockSpec(memory_space=pltpu.HBM)] * 3,
-            [spec(d, 0) for d in (PACKED, FIELD_TILES, MESSAGE, MESSAGE)],
-            [sized(d, n) for d in (PACKED, FIELD_TILES, MESSAGE, MESSAGE)],
-            "interior", (adj, vel, kap), after, (),
-            [
-                pltpu.VMEM((blocks, FIELDS, BLOCK, LON, LAT), jnp.float32),
-                pltpu.VMEM((blocks, 2, 2, BLOCK, LON, LAT), jnp.float32),
-                pltpu.VMEM((blocks, 2, BLOCK, LON, LAT), jnp.float32),
-                pltpu.SemaphoreType.DMA((blocks, 3)),
-            ],
+            [spec(d, 0) for d in (PACKED, FIELD_TILES)] + specs,
+            [sized(d, n) for d in (PACKED, FIELD_TILES)] + shapes,
+            "interior", (adj, vel, kap), after, into,
+            [pltpu.VMEM((blocks, *d), jnp.float32) for d in scratch] + [pltpu.SemaphoreType.DMA((blocks, 3))],
             FIRST_VMEM,
         )
         after = [mid]
-        first_theirs = swapped(*mine) if not groups else None
-        groups.append(([(long_way if around else detour)(mid, 0)], image, mine, first_theirs))
+        if early is None:
+            early = mine[:2]
+            early_theirs = swapped(*early)
+        late = mine[-2:]
+        groups.append(([(long_way if around else detour)(mid, 0)], image))
+    exchanges = ((early, early_theirs), (late, swapped(*late)))
     lasts, after = [], []
-    for k, (first, count, group) in enumerate(ENDS):
-        start = GROUPS[group][0]
-        mid, image, mine, ready = groups[group]
-        if not lasts:
-            theirs = ready
-        elif group != ENDS[k - 1][2]:
-            theirs = swapped(*mine)
-            after = [*after, mid[0], groups[0][0][0]]
-        b, c = first // BLOCK, (first - start) // BLOCK
+    for k, (first, count, group, exchange) in enumerate(ENDS):
+        mine, theirs = exchanges[exchange]
+        b = first // BLOCK
+        c, m = (first - GROUPS[group][0]) // BLOCK, (first - SPLIT * exchange) // BLOCK
+        if k == 1:
+            after = [*after, groups[1][0][0]]
         end = call(
             FLOPS[1], second_kernel, count,
             [spec((1, *vel.shape[1:]), 2, b), spec((1, *kap.shape[1:]), 1, b)]
-            + [spec(d, 0, c) for d in (MESSAGE,) * 4 + (FIELD_TILES,)],
-            spec(PACKED, 0), sized(PACKED, count), "ends", (vel, kap, *mine, *theirs, image), after,
+            + [spec(MESSAGE, 0, m)] * 4 + [spec(FIELD_TILES, 0, c)],
+            spec(PACKED, 0), sized(PACKED, count), "ends", (vel, kap, *mine, *theirs, groups[group][1]), after,
         )
         after = [end]
         lasts.append(to_preceding(end))
-        for at, (mid, _, _, _), (_, _, around) in zip(STEPS, groups, GROUPS):
+        for at, (mid, _), (_, _, around) in zip(STEPS, groups, GROUPS):
             if k in at:
                 x = lax.optimization_barrier([mid[-1], end])[0]
                 mid.append((long_way if around else detour)(x, len(mid)))
     out, after = None, [end]
-    for (first, count, group), end in zip(ENDS, lasts):
+    for (first, count, group, _), end in zip(ENDS, lasts):
         b = first // BLOCK
         mid, around = groups[group][0], GROUPS[group][2]
         arrays = (adj, end, mid[-1]) if around else (adj, end, *mid)

time: 71.9 us -> 69.7 us (0.969); the launches traced: 70.7 us -> 69.5 us
  waiting for transfers between devices: 17.2 us -> 14.8 us
  Pallas kernels: 23 us -> 24.2 us
    ppermute x2 -> x3, waiting for transfers between devices: 10.5 us -> 0.4 us  [to_preceding(): return lax.ppermute(x, 'win', [(k + 1, k) for k in range(n - 1)])]
    ppermute x1, waiting for transfers between devices: 0.01 us -> 7.86 us  [detour(): return lax.ppermute(x, 'win', [(n - 1, n // 2 - 1)])]
    ppermute x2 -> x3, starting transfers between devices: 4.55 us -> 9.12 us  [to_preceding(): return lax.ppermute(x, 'win', [(k + 1, k) for k in range(n - 1)])]
    ppermute x3, starting transfers between devices: 10.6 us -> 6.39 us  [long_way(): return lax.ppermute(x, 'win', [*pairs, side])]
    ppermute x3, waiting for transfers between devices: 3.12 us -> 0.01 us  [long_way(): return lax.ppermute(x, 'win', [*pairs, side])]
    ppermute x1, waiting for transfers between devices: 0.01 us -> 2.11 us  [detour(): lax.ppermute(x, 'win', [(k + 1, n - 1 if k + 1 == n // 2 else k) for k in...]
    pallas_call x6 -> x8, Pallas kernels: 23 us -> 24.2 us  [call(): pl.pallas_call(kernel, grid=(count // BLOCK,), in_specs=in_specs, out_spe...]
    ppermute x2, waiting for transfers between devices: 3.57 us -> 4.41 us  [swapped(): lax.ppermute(other, 'tile', outer)]
  transfers between devices with their start and end apart: 11 -> 12, of which waited for: 5 -> 4; matrix products, arithmetic and copies ran while one was open for 0% -> 0% of each run, Pallas kernels for 19% -> 20%
where the time goes in v4:
time: 69.7 us; the launch traced here: 69.5 us
  starting transfers between devices  30.2 us (43%)
  Pallas kernels  24.2 us (35%)
  waiting for transfers between devices  14.8 us (21%)
    pallas_call x8, Pallas kernels, call(): pl.pallas_call(kernel, grid=(count // BLOCK,), in_specs=in_specs, out_spe...  24.2 us
    ppermute x2, starting transfers between devices, swapped(): lax.ppermute(other, 'tile', outer)  10.4 us
    ppermute x3, starting transfers between devices, to_preceding(): return lax.ppermute(x, 'win', [(k + 1, k) for k in range(n - 1)])  9.12 us
    ppermute x1, waiting for transfers between devices, detour(): return lax.ppermute(x, 'win', [(n - 1, n // 2 - 1)])  7.86 us
    ppermute x3, starting transfers between devices, long_way(): return lax.ppermute(x, 'win', [*pairs, side])  6.39 us
    ppermute x2, waiting for transfers between devices, swapped(): lax.ppermute(other, 'tile', outer)  4.41 us
    ppermute x1, starting transfers between devices, detour(): lax.ppermute(x, 'win', [(k + 1, n - 1 if k + 1 == n // 2 else k) for k in...  2.78 us
    ppermute x1, waiting for transfers between devices, detour(): lax.ppermute(x, 'win', [(k + 1, n - 1 if k + 1 == n // 2 else k) for k in...  2.11 us
  transfers between devices with their start and end apart: 12, of which 4 were waited for; matrix products, arithmetic and copies ran while one was open for 0% of the time, Pallas kernels for 20%

profile of v4, /device:TPU:6, one launch (start us, length us, event | category | flops | bytes accessed | tf_op | source)
XLA Modules:
  0.0 69.5 jit_solution(7843392579954423899)
XLA Ops:
  0.0 8.7 %interior.2 = (f32[24,80,128]{2,1,0:T(8,128)}, f32[24,4,8,384]{3,2,1,0:T(8,128)}, f32[12,48,128]{2,1,0:T(8,128)}, f32[12,48,128]{2,1,0:T(8,128)}, f32[20,48,128]{2,1,0:T(8,128)}, /*index=5*/f32[20,48,128]{2,1,0:T(8,128)}) custom-call(f32[4,32,16,320]{3,2,1,0:T(8,128)} %bitcast.9, f32[2,2,32,16,320]{4,3,2,1,0:T(8,128)} %bitcast.4, f32[2,32,16,320]{3,2,1,0:T(8,128)} %bitcast.14), custom_call_target="tpu_custom_call" | custom-call | flops 8000000000 | bytes 1 | tf_op jit(solution)/shard_map/interior/pallas_call | solution.py:291
  8.7 0.1 collective-permute-start.2
  8.8 8.9 %collective-permute-start.3 = (f32[12,48,128]{2,1,0:T(8,128)}, f32[12,48,128]{2,1,0:T(8,128)S(1)}, u32[]{:S(2)}, u32[]{:S(2)}) collective-permute-start(f32[12,48,128]{2,1,0:T(8,128)} %get-tuple-element.26.other), channel_id=1, source_target_pairs={{0,31},{1,2},{2,1},{3,4},{4,3},{5,6},{6,5},{7,8},{8,7},{9,10},{10,... | collective-permute-start | bytes 884744 | tf_op jit(solution)/shard_map/ppermute | solution.py:318
  17.7 2.8 %collective-permute-start.9 = (f32[24,80,128]{2,1,0:T(8,128)}, f32[24,80,128]{2,1,0:T(8,128)S(1)}, u32[]{:S(2)}, u32[]{:S(2)}) collective-permute-start(f32[24,80,128]{2,1,0:T(8,128)} %get-tuple-element.18.refs_0_), channel_id=1, source_target_pairs={{32,0},{64,32},{96,64},{128,224},{160,128},{192,160},{224,192},{33... | collective-permute-start | bytes 2949128 | tf_op jit(solution)/shard_map/ppermute | solution.py:330
  20.4 0.0 copy-start
  20.5 0.0 copy-start.2
  20.5 0.0 copy-start.7
  20.5 4.3 %interior.3 = (f32[8,80,128]{2,1,0:T(8,128)}, f32[8,4,8,384]{3,2,1,0:T(8,128)}, f32[20,48,128]{2,1,0:T(8,128)}, f32[20,48,128]{2,1,0:T(8,128)}) custom-call(f32[4,32,16,320]{3,2,1,0:T(8,128)} %bitcast.10, f32[2,2,32,16,320]{4,3,2,1,0:T(8,128)} %bitcast.5, f32[2,32,16,320]{3,2,1,0:T(8,128)} %bitcast.15, ...), custom_call_target="tpu_custom_call", output_to_operand_aliasing={{2}: (4, {}), {3}: (5, {})} | custom-call | flops 8000000000 | bytes 1 | tf_op jit(solution)/shard_map/interior/pallas_call | solution.py:291
  24.8 1.9 %collective-permute-start.4 = (f32[8,80,128]{2,1,0:T(8,128)}, f32[8,80,128]{2,1,0:T(8,128)S(1)}, u32[]{:S(2)}, u32[]{:S(2)}) collective-permute-start(f32[8,80,128]{2,1,0:T(8,128)} %get-tuple-element.27), channel_id=1, source_target_pairs={{32,64},{64,96},{96,0},{160,192},{192,224},{224,128},{128,160},{33... | collective-permute-start | bytes 983048 | tf_op jit(solution)/shard_map/ppermute | solution.py:338
  26.7 0.1 collective-permute-start
  26.8 0.0 collective-permute-done.2.from_partner
  26.8 1.5 %collective-permute-start.1 = (f32[20,48,128]{2,1,0:T(8,128)}, f32[20,48,128]{2,1,0:T(8,128)S(1)}, u32[]{:S(2)}, u32[]{:S(2)}) collective-permute-start(f32[20,48,128]{2,1,0:T(8,128)} %get-tuple-element.22.other), channel_id=1, source_target_pairs={{0,31},{1,2},{2,1},{3,4},{4,3},{5,6},{6,5},{7,8},{8,7},{9,10},{10,... | collective-permute-start | bytes 1474568 | tf_op jit(solution)/shard_map/ppermute | solution.py:318
  28.4 0.0 collective-permute-done.3.from_other
  28.4 2.0 %ends.3.refs_0_ = f32[12,80,128]{2,1,0:T(8,128)S(1)} custom-call(f32[2,2,32,16,320]{4,3,2,1,0:T(8,128)S(1)} %bitcast.6, f32[2,32,16,320]{3,2,1,0:T(8,128)S(1)} %bitcast.16, f32[12,48,128]{2,1,0:T(8,128)S(1)} %copy-done.5, f32[12,48,128]{2,1,0:T(8,128)S(1)} %copy-done.6, f32[12,48,128]{2,1,0:T(8,128)S(1)} %collective-permute-done.2.from_partner, ...), custom_call_target="tpu_custom_call" | custom-call | flops 8000000000 | bytes 1 | tf_op jit(solution)/shard_map/ends/pallas_call | solution.py:291
  30.5 4.0 %collective-permute-start.11 = (f32[12,80,128]{2,1,0:T(8,128)S(1)}, f32[12,80,128]{2,1,0:T(8,128)S(1)}, u32[]{:S(2)}, u32[]{:S(2)}) collective-permute-start(f32[12,80,128]{2,1,0:T(8,128)S(1)} %ends.3.refs_0_), channel_id=1, source_target_pairs={{32,0},{64,32},{96,64},{128,96},{160,128},{192,160},{224,192},{33,... | collective-permute-start | bytes 1474568 | tf_op jit(solution)/shard_map/ppermute | solution.py:323
  34.5 0.0 collective-permute-done.4.refs_1_
  34.5 2.5 %collective-permute-start.6 = (f32[8,80,128]{2,1,0:T(8,128)S(1)}, f32[8,80,128]{2,1,0:T(8,128)S(1)}, u32[]{:S(2)}, u32[]{:S(2)}) collective-permute-start(f32[8,80,128]{2,1,0:T(8,128)S(1)} %collective-permute-done.4.refs_1_), channel_id=1, source_target_pairs={{0,32},{64,96},{96,0},{128,160},{192,224},{224,128},{160,64},{1,33... | collective-permute-start | bytes 983048 | tf_op jit(solution)/shard_map/ppermute | solution.py:338
  37.1 2.1 %collective-permute-done.9.mid = f32[24,80,128]{2,1,0:T(8,128)S(1)} collective-permute-done((f32[24,80,128]{2,1,0:T(8,128)}, f32[24,80,128]{2,1,0:T(8,128)S(1)}, u32[]{:S(2)}, u32[]{:S(2)}) %collective-permute-start.9) | collective-permute-done | bytes 983072 | tf_op jit(solution)/shard_map/ppermute | solution.py:330
  39.2 1.3 %collective-permute-start.10 = (f32[24,80,128]{2,1,0:T(8,128)S(1)}, f32[24,80,128]{2,1,0:T(8,128)S(1)}, u32[]{:S(2)}, u32[]{:S(2)}) collective-permute-start(f32[24,80,128]{2,1,0:T(8,128)S(1)} %collective-permute-done.9.mid), channel_id=1, source_target_pairs={{224,96},{225,97},{226,98},{227,99},{228,100},{229,101},{230,102},... | collective-permute-start | bytes 2949128 | tf_op jit(solution)/shard_map/ppermute | solution.py:329
  40.5 4.4 %collective-permute-done.1.from_other = f32[20,48,128]{2,1,0:T(8,128)S(1)} collective-permute-done((f32[20,48,128]{2,1,0:T(8,128)}, f32[20,48,128]{2,1,0:T(8,128)S(1)}, u32[]{:S(2)}, u32[]{:S(2)}) %collective-permute-start.1) | collective-permute-done | bytes 491552 | tf_op jit(solution)/shard_map/ppermute | solution.py:318
  44.9 2.0 %ends.4.refs_0_ = f32[12,80,128]{2,1,0:T(8,128)S(1)} custom-call(f32[2,2,32,16,320]{4,3,2,1,0:T(8,128)S(1)} %bitcast.7, f32[2,32,16,320]{3,2,1,0:T(8,128)S(1)} %bitcast.17, f32[20,48,128]{2,1,0:T(8,128)S(1)} %copy-done.3, f32[20,48,128]{2,1,0:T(8,128)S(1)} %copy-done.4, f32[20,48,128]{2,1,0:T(8,128)S(1)} %collective-permute-done.from_partner, ...), custom_call_target="tpu_custom_call" | custom-call | flops 8000000000 | bytes 1 | tf_op jit(solution)/shard_map/ends/pallas_call | solution.py:291
  47.0 2.6 %collective-permute-start.8 = (f32[12,80,128]{2,1,0:T(8,128)S(1)}, f32[12,80,128]{2,1,0:T(8,128)S(1)}, u32[]{:S(2)}, u32[]{:S(2)}) collective-permute-start(f32[12,80,128]{2,1,0:T(8,128)S(1)} %ends.4.refs_0_), channel_id=1, source_target_pairs={{32,0},{64,32},{96,64},{128,96},{160,128},{192,160},{224,192},{33,... | collective-permute-start | bytes 1474568 | tf_op jit(solution)/shard_map/ppermute | solution.py:323
  49.5 0.0 copy-start.1
  49.6 1.4 %ends.5.refs_1_ = f32[8,80,128]{2,1,0:T(8,128)S(1)} custom-call(f32[2,2,32,16,320]{4,3,2,1,0:T(8,128)S(1)} %bitcast.8, f32[2,32,16,320]{3,2,1,0:T(8,128)S(1)} %bitcast.18, f32[20,48,128]{2,1,0:T(8,128)S(1)} %copy-done.3, f32[20,48,128]{2,1,0:T(8,128)S(1)} %copy-done.4, f32[20,48,128]{2,1,0:T(8,128)S(1)} %collective-permute-done.from_partner, ...), custom_call_target="tpu_custom_call" | custom-call | flops 8000000000 | bytes 1 | tf_op jit(solution)/shard_map/ends/pallas_call | solution.py:291
  50.9 2.5 %collective-permute-start.5 = (f32[8,80,128]{2,1,0:T(8,128)S(1)}, f32[8,80,128]{2,1,0:T(8,128)S(1)}, u32[]{:S(2)}, u32[]{:S(2)}) collective-permute-start(f32[8,80,128]{2,1,0:T(8,128)S(1)} %ends.5.refs_1_), channel_id=1, source_target_pairs={{32,0},{64,32},{96,64},{128,96},{160,128},{192,160},{224,192},{33,... | collective-permute-start | bytes 983048 | tf_op jit(solution)/shard_map/ppermute | solution.py:323
  53.4 1.9 %collective-permute-start.7 = (f32[8,80,128]{2,1,0:T(8,128)S(1)}, f32[8,80,128]{2,1,0:T(8,128)S(1)}, u32[]{:S(2)}, u32[]{:S(2)}) collective-permute-start(f32[8,80,128]{2,1,0:T(8,128)S(1)} %collective-permute-done.6), channel_id=1, source_target_pairs={{0,32},{32,64},{96,0},{128,160},{160,192},{224,128},{64,96},{1,33}... | collective-permute-start | bytes 983048 | tf_op jit(solution)/shard_map/ppermute | solution.py:338
  55.4 7.9 %collective-permute-done.10.refs_0_ = f32[24,80,128]{2,1,0:T(8,128)S(1)} collective-permute-done((f32[24,80,128]{2,1,0:T(8,128)S(1)}, f32[24,80,128]{2,1,0:T(8,128)S(1)}, u32[]{:S(2)}, u32[]{:S(2)}) %collective-permute-start.10) | collective-permute-done | bytes 983072 | tf_op jit(solution)/shard_map/ppermute | solution.py:329
  63.2 2.2 %subtract.3.refs_1_ = f32[4,32,16,320]{3,2,1,0:T(8,128)} custom-call(f32[4,32,16,320]{3,2,1,0:T(8,128)S(1)} %bitcast.11, f32[12,80,128]{2,1,0:T(8,128)S(1)} %collective-permute-done.11.end, f32[24,80,128]{2,1,0:T(8,128)S(1)} %collective-permute-done.9.mid, f32[24,80,128]{2,1,0:T(8,128)S(1)} %collective-permute-done.10.refs_0_, f32[8,80,128]{2,1,0:T(8,128)S(1)} %ends.5.refs_1_), custom_call_target="tpu_custom_call" | custom-call | flops 8000000000 | bytes 1 | tf_op jit(solution)/shard_map/subtract/pallas_call | solution.py:291
  65.4 2.2 %subtract.4.refs_0_ = f32[4,32,16,320]{3,2,1,0:T(8,128)} custom-call(f32[4,32,16,320]{3,2,1,0:T(8,128)S(1)} %bitcast.12, f32[12,80,128]{2,1,0:T(8,128)S(1)} %collective-permute-done.8.end, f32[24,80,128]{2,1,0:T(8,128)S(1)} %collective-permute-done.9.mid, f32[24,80,128]{2,1,0:T(8,128)S(1)} %collective-permute-done.10.refs_0_, ...), custom_call_target="tpu_custom_call", output_to_operand_aliasing={{}: (4, {})} | custom-call | flops 8000000000 | bytes 1 | tf_op jit(solution)/shard_map/subtract/pallas_call | solution.py:291
  67.6 0.4 collective-permute-done.5.end
  68.0 0.0 collective-permute-done.7.mid
  68.0 1.4 %subtract.5 = f32[4,32,16,320]{3,2,1,0:T(8,128)} custom-call(f32[4,32,16,320]{3,2,1,0:T(8,128)S(1)} %bitcast.13, f32[8,80,128]{2,1,0:T(8,128)S(1)} %collective-permute-done.5.end, f32[8,80,128]{2,1,0:T(8,128)S(1)} %collective-permute-done.7.mid, f32[4,32,16,320]{3,2,1,0:T(8,128)} %subtract.4.refs_0_), custom_call_target="tpu_custom_call", output_to_operand_aliasing={{}: (3, {})} | custom-call | flops 8000000000 | bytes 1 | tf_op jit(solution)/shard_map/subtract/pallas_call | solution.py:291
  (18 shorter events, 0.0 us)
Async XLA Ops:
  8.7 18.1 %collective-permute-start.2 = (f32[12,48,128]{2,1,0:T(8,128)}, f32[12,48,128]{2,1,0:T(8,128)S(1)}, u32[]{:S(2)}, u32[]{:S(2)}) collective-permute-start(f32[12,48,128]{2,1,0:T(8,128)} %get-tuple-element.25.partner), channel_id=1, source_target_pairs={{0,1},{1,0},{2,3},{3,2},{4,5},{5,4},{6,7},{7,6},{8,9},{9,8},{10,11... | collective-permute-start | bytes 884744 | tf_op jit(solution)/shard_map/ppermute | solution.py:318
  8.8 19.6 %collective-permute-start.3 = (f32[12,48,128]{2,1,0:T(8,128)}, f32[12,48,128]{2,1,0:T(8,128)S(1)}, u32[]{:S(2)}, u32[]{:S(2)}) collective-permute-start(f32[12,48,128]{2,1,0:T(8,128)} %get-tuple-element.26.other), channel_id=1, source_target_pairs={{0,31},{1,2},{2,1},{3,4},{4,3},{5,6},{6,5},{7,8},{8,7},{9,10},{10,... | collective-permute-start | bytes 884744 | tf_op jit(solution)/shard_map/ppermute | solution.py:318
  17.7 21.6 %collective-permute-start.9 = (f32[24,80,128]{2,1,0:T(8,128)}, f32[24,80,128]{2,1,0:T(8,128)S(1)}, u32[]{:S(2)}, u32[]{:S(2)}) collective-permute-start(f32[24,80,128]{2,1,0:T(8,128)} %get-tuple-element.18.refs_0_), channel_id=1, source_target_pairs={{32,0},{64,32},{96,64},{128,224},{160,128},{192,160},{224,192},{33... | collective-permute-start | bytes 2949128 | tf_op jit(solution)/shard_map/ppermute | solution.py:330
  20.4 7.9 %copy-start = (f32[1,2,2,32,16,320]{5,4,3,2,1,0:T(8,128)S(1)}, f32[1,2,2,32,16,320]{5,4,3,2,1,0:T(8,128)}, u32[]{:S(2)}) copy-start(f32[1,2,2,32,16,320]{5,4,3,2,1,0:T(8,128)} %param.4) | copy-start | bytes 7864324
  20.5 7.9 %copy-start.2 = (f32[1,2,32,16,320]{4,3,2,1,0:T(8,128)S(1)}, f32[1,2,32,16,320]{4,3,2,1,0:T(8,128)}, u32[]{:S(2)}) copy-start(f32[1,2,32,16,320]{4,3,2,1,0:T(8,128)} %param.5) | copy-start | bytes 3932164
  20.5 7.9 %copy-start.5 = (f32[12,48,128]{2,1,0:T(8,128)S(1)}, f32[12,48,128]{2,1,0:T(8,128)}, u32[]{:S(2)}) copy-start(f32[12,48,128]{2,1,0:T(8,128)} %get-tuple-element.25.partner) | copy-start | bytes 884740
  20.5 7.9 %copy-start.6 = (f32[12,48,128]{2,1,0:T(8,128)S(1)}, f32[12,48,128]{2,1,0:T(8,128)}, u32[]{:S(2)}) copy-start(f32[12,48,128]{2,1,0:T(8,128)} %get-tuple-element.26.other) | copy-start | bytes 884740
  20.5 7.9 %copy-start.7 = (f32[24,4,8,384]{3,2,1,0:T(8,128)S(1)}, f32[24,4,8,384]{3,2,1,0:T(8,128)}, u32[]{:S(2)}) copy-start(f32[24,4,8,384]{3,2,1,0:T(8,128)} %get-tuple-element.24.image) | copy-start | bytes 3538948
  24.8 9.7 %collective-permute-start.4 = (f32[8,80,128]{2,1,0:T(8,128)}, f32[8,80,128]{2,1,0:T(8,128)S(1)}, u32[]{:S(2)}, u32[]{:S(2)}) collective-permute-start(f32[8,80,128]{2,1,0:T(8,128)} %get-tuple-element.27), channel_id=1, source_target_pairs={{32,64},{64,96},{96,0},{160,192},{192,224},{224,128},{128,160},{33... | collective-permute-start | bytes 983048 | tf_op jit(solution)/shard_map/ppermute | solution.py:338
  26.7 13.8 %collective-permute-start = (f32[20,48,128]{2,1,0:T(8,128)}, f32[20,48,128]{2,1,0:T(8,128)S(1)}, u32[]{:S(2)}, u32[]{:S(2)}) collective-permute-start(f32[20,48,128]{2,1,0:T(8,128)} %get-tuple-element.21.partner), channel_id=1, source_target_pairs={{0,1},{1,0},{2,3},{3,2},{4,5},{5,4},{6,7},{7,6},{8,9},{9,8},{10,11... | collective-permute-start | bytes 1474568 | tf_op jit(solution)/shard_map/ppermute | solution.py:318
  26.8 18.1 %collective-permute-start.1 = (f32[20,48,128]{2,1,0:T(8,128)}, f32[20,48,128]{2,1,0:T(8,128)S(1)}, u32[]{:S(2)}, u32[]{:S(2)}) collective-permute-start(f32[20,48,128]{2,1,0:T(8,128)} %get-tuple-element.22.other), channel_id=1, source_target_pairs={{0,31},{1,2},{2,1},{3,4},{4,3},{5,6},{6,5},{7,8},{8,7},{9,10},{10,... | collective-permute-start | bytes 1474568 | tf_op jit(solution)/shard_map/ppermute | solution.py:318
  28.4 16.5 %copy-start.3 = (f32[20,48,128]{2,1,0:T(8,128)S(1)}, f32[20,48,128]{2,1,0:T(8,128)}, u32[]{:S(2)}) copy-start(f32[20,48,128]{2,1,0:T(8,128)} %get-tuple-element.21.partner) | copy-start | bytes 1474564
  28.4 16.5 %copy-start.4 = (f32[20,48,128]{2,1,0:T(8,128)S(1)}, f32[20,48,128]{2,1,0:T(8,128)}, u32[]{:S(2)}) copy-start(f32[20,48,128]{2,1,0:T(8,128)} %get-tuple-element.22.other) | copy-start | bytes 1474564
  30.5 19.0 %copy-start.8 = (f32[8,4,8,384]{3,2,1,0:T(8,128)S(1)}, f32[8,4,8,384]{3,2,1,0:T(8,128)}, u32[]{:S(2)}) copy-start(f32[8,4,8,384]{3,2,1,0:T(8,128)} %get-tuple-element.23.image) | copy-start | bytes 1179652
  30.5 24.9 %collective-permute-start.11 = (f32[12,80,128]{2,1,0:T(8,128)S(1)}, f32[12,80,128]{2,1,0:T(8,128)S(1)}, u32[]{:S(2)}, u32[]{:S(2)}) collective-permute-start(f32[12,80,128]{2,1,0:T(8,128)S(1)} %ends.3.refs_0_), channel_id=1, source_target_pairs={{32,0},{64,32},{96,64},{128,96},{160,128},{192,160},{224,192},{33,... | collective-permute-start | bytes 1474568 | tf_op jit(solution)/shard_map/ppermute | solution.py:323
  34.5 18.9 %collective-permute-start.6 = (f32[8,80,128]{2,1,0:T(8,128)S(1)}, f32[8,80,128]{2,1,0:T(8,128)S(1)}, u32[]{:S(2)}, u32[]{:S(2)}) collective-permute-start(f32[8,80,128]{2,1,0:T(8,128)S(1)} %collective-permute-done.4.refs_1_), channel_id=1, source_target_pairs={{0,32},{64,96},{96,0},{128,160},{192,224},{224,128},{160,64},{1,33... | collective-permute-start | bytes 983048 | tf_op jit(solution)/shard_map/ppermute | solution.py:338
  39.2 24.0 %collective-permute-start.10 = (f32[24,80,128]{2,1,0:T(8,128)S(1)}, f32[24,80,128]{2,1,0:T(8,128)S(1)}, u32[]{:S(2)}, u32[]{:S(2)}) collective-permute-start(f32[24,80,128]{2,1,0:T(8,128)S(1)} %collective-permute-done.9.mid), channel_id=1, source_target_pairs={{224,96},{225,97},{226,98},{227,99},{228,100},{229,101},{230,102},... | collective-permute-start | bytes 2949128 | tf_op jit(solution)/shard_map/ppermute | solution.py:329
  47.0 18.5 %collective-permute-start.8 = (f32[12,80,128]{2,1,0:T(8,128)S(1)}, f32[12,80,128]{2,1,0:T(8,128)S(1)}, u32[]{:S(2)}, u32[]{:S(2)}) collective-permute-start(f32[12,80,128]{2,1,0:T(8,128)S(1)} %ends.4.refs_0_), channel_id=1, source_target_pairs={{32,0},{64,32},{96,64},{128,96},{160,128},{192,160},{224,192},{33,... | collective-permute-start | bytes 1474568 | tf_op jit(solution)/shard_map/ppermute | solution.py:323
  49.5 13.7 %copy-start.1 = (f32[1,4,32,16,320]{4,3,2,1,0:T(8,128)S(1)}, f32[1,4,32,16,320]{4,3,2,1,0:T(8,128)}, u32[]{:S(2)}) copy-start(f32[1,4,32,16,320]{4,3,2,1,0:T(8,128)} %param.3) | copy-start | bytes 7864324
  50.9 17.1 %collective-permute-start.5 = (f32[8,80,128]{2,1,0:T(8,128)S(1)}, f32[8,80,128]{2,1,0:T(8,128)S(1)}, u32[]{:S(2)}, u32[]{:S(2)}) collective-permute-start(f32[8,80,128]{2,1,0:T(8,128)S(1)} %ends.5.refs_1_), channel_id=1, source_target_pairs={{32,0},{64,32},{96,64},{128,96},{160,128},{192,160},{224,192},{33,... | collective-permute-start | bytes 983048 | tf_op jit(solution)/shard_map/ppermute | solution.py:323
  53.4 14.6 %collective-permute-start.7 = (f32[8,80,128]{2,1,0:T(8,128)S(1)}, f32[8,80,128]{2,1,0:T(8,128)S(1)}, u32[]{:S(2)}, u32[]{:S(2)}) collective-permute-start(f32[8,80,128]{2,1,0:T(8,128)S(1)} %collective-permute-done.6), channel_id=1, source_target_pairs={{0,32},{32,64},{96,0},{128,160},{160,192},{224,128},{64,96},{1,33}... | collective-permute-start | bytes 983048 | tf_op jit(solution)/shard_map/ppermute | solution.py:338

commit v5 on v4

--- a/solution.py
+++ b/solution.py
@@ -10,7 +10,7 @@
 FIELDS, LON, LAT = 4, 16, 320
 WIDE = 384
 BLOCK = 4
-FLOPS = (8000000000, 8000000000, 8000000000)
+FLOPS = (4000000000, 6000000000, 4000000000)
 FIRST_VMEM = 54
 MIB = 1024 * 1024
 GROUPS = ((0, 24, False), (24, 8, True))

time: 69.7 us -> 70.1 us (level)
    ppermute x1, waiting for transfers between devices: 2.11 us -> 0.01 us  [detour(): lax.ppermute(x, 'win', [(k + 1, n - 1 if k + 1 == n // 2 else k) for k in...]
    ppermute x2, waiting for transfers between devices: 4.41 us -> 6.5 us  [swapped(): lax.ppermute(other, 'tile', outer)]
  transfers between devices with their start and end apart: 12 -> 12, of which waited for: 4 -> 3; matrix products, arithmetic and copies ran while one was open for 0% -> 0% of each run, Pallas kernels for 20% -> 20%
where the time goes in v5:
time: 70.1 us; the launch traced here: 69.8 us
  starting transfers between devices  30.3 us (43%)
  Pallas kernels  24.2 us (35%)
  waiting for transfers between devices  15.1 us (22%)
    pallas_call x8, Pallas kernels, call(): pl.pallas_call(kernel, grid=(count // BLOCK,), in_specs=in_specs, out_spe...  24.2 us
    ppermute x2, starting transfers between devices, swapped(): lax.ppermute(other, 'tile', outer)  10.4 us
    ppermute x3, starting transfers between devices, to_preceding(): return lax.ppermute(x, 'win', [(k + 1, k) for k in range(n - 1)])  9.22 us
    ppermute x1, waiting for transfers between devices, detour(): return lax.ppermute(x, 'win', [(n - 1, n // 2 - 1)])  7.75 us
    ppermute x2, waiting for transfers between devices, swapped(): lax.ppermute(other, 'tile', outer)  6.5 us
    ppermute x3, starting transfers between devices, long_way(): return lax.ppermute(x, 'win', [*pairs, side])  6.39 us
    ppermute x1, starting transfers between devices, detour(): lax.ppermute(x, 'win', [(k + 1, n - 1 if k + 1 == n // 2 else k) for k in...  2.79 us
  transfers between devices with their start and end apart: 12, of which 3 were waited for; matrix products, arithmetic and copies ran while one was open for 0% of the time, Pallas kernels for 20%

profile of v5, /device:TPU:6, one launch (start us, length us, event | category | flops | bytes accessed | tf_op | source)
XLA Modules:
  0.0 69.8 jit_solution(4205696228372869251)
XLA Ops:
  0.0 8.7 %interior.2 = (f32[24,80,128]{2,1,0:T(8,128)}, f32[24,4,8,384]{3,2,1,0:T(8,128)}, f32[12,48,128]{2,1,0:T(8,128)}, f32[12,48,128]{2,1,0:T(8,128)}, f32[20,48,128]{2,1,0:T(8,128)}, /*index=5*/f32[20,48,128]{2,1,0:T(8,128)}) custom-call(f32[4,32,16,320]{3,2,1,0:T(8,128)} %bitcast.9, f32[2,2,32,16,320]{4,3,2,1,0:T(8,128)} %bitcast.4, f32[2,32,16,320]{3,2,1,0:T(8,128)} %bitcast.14), custom_call_target="tpu_custom_call" | custom-call | flops 4000000000 | bytes 1 | tf_op jit(solution)/shard_map/interior/pallas_call | solution.py:291
  8.7 2.8 %collective-permute-start.9 = (f32[24,80,128]{2,1,0:T(8,128)}, f32[24,80,128]{2,1,0:T(8,128)S(1)}, u32[]{:S(2)}, u32[]{:S(2)}) collective-permute-start(f32[24,80,128]{2,1,0:T(8,128)} %get-tuple-element.18.refs_0_), channel_id=1, source_target_pairs={{32,0},{64,32},{96,64},{128,224},{160,128},{192,160},{224,192},{33... | collective-permute-start | bytes 2949128 | tf_op jit(solution)/shard_map/ppermute | solution.py:330
  11.5 0.1 collective-permute-start.2
  11.6 8.9 %collective-permute-start.3 = (f32[12,48,128]{2,1,0:T(8,128)}, f32[12,48,128]{2,1,0:T(8,128)S(1)}, u32[]{:S(2)}, u32[]{:S(2)}) collective-permute-start(f32[12,48,128]{2,1,0:T(8,128)} %get-tuple-element.26.other), channel_id=1, source_target_pairs={{0,31},{1,2},{2,1},{3,4},{4,3},{5,6},{6,5},{7,8},{8,7},{9,10},{10,... | collective-permute-start | bytes 884744 | tf_op jit(solution)/shard_map/ppermute | solution.py:318
  20.5 0.0 copy-start.7
  20.5 4.3 %interior.3 = (f32[8,80,128]{2,1,0:T(8,128)}, f32[8,4,8,384]{3,2,1,0:T(8,128)}, f32[20,48,128]{2,1,0:T(8,128)}, f32[20,48,128]{2,1,0:T(8,128)}) custom-call(f32[4,32,16,320]{3,2,1,0:T(8,128)} %bitcast.10, f32[2,2,32,16,320]{4,3,2,1,0:T(8,128)} %bitcast.5, f32[2,32,16,320]{3,2,1,0:T(8,128)} %bitcast.15, ...), custom_call_target="tpu_custom_call", output_to_operand_aliasing={{2}: (4, {}), {3}: (5, {})} | custom-call | flops 4000000000 | bytes 1 | tf_op jit(solution)/shard_map/interior/pallas_call | solution.py:291
  24.8 1.9 %collective-permute-start.4 = (f32[8,80,128]{2,1,0:T(8,128)}, f32[8,80,128]{2,1,0:T(8,128)S(1)}, u32[]{:S(2)}, u32[]{:S(2)}) collective-permute-start(f32[8,80,128]{2,1,0:T(8,128)} %get-tuple-element.27), channel_id=1, source_target_pairs={{32,64},{64,96},{96,0},{160,192},{192,224},{224,128},{128,160},{33... | collective-permute-start | bytes 983048 | tf_op jit(solution)/shard_map/ppermute | solution.py:338
  26.7 0.1 collective-permute-start
  26.8 0.0 collective-permute-done.2.from_partner
  26.8 1.5 %collective-permute-start.1 = (f32[20,48,128]{2,1,0:T(8,128)}, f32[20,48,128]{2,1,0:T(8,128)S(1)}, u32[]{:S(2)}, u32[]{:S(2)}) collective-permute-start(f32[20,48,128]{2,1,0:T(8,128)} %get-tuple-element.22.other), channel_id=1, source_target_pairs={{0,31},{1,2},{2,1},{3,4},{4,3},{5,6},{6,5},{7,8},{8,7},{9,10},{10,... | collective-permute-start | bytes 1474568 | tf_op jit(solution)/shard_map/ppermute | solution.py:318
  28.4 2.0 %ends.3.refs_0_ = f32[12,80,128]{2,1,0:T(8,128)S(1)} custom-call(f32[2,2,32,16,320]{4,3,2,1,0:T(8,128)S(1)} %bitcast.6, f32[2,32,16,320]{3,2,1,0:T(8,128)S(1)} %bitcast.16, f32[12,48,128]{2,1,0:T(8,128)S(1)} %copy-done.5, f32[12,48,128]{2,1,0:T(8,128)S(1)} %copy-done.6, f32[12,48,128]{2,1,0:T(8,128)S(1)} %collective-permute-done.2.from_partner, ...), custom_call_target="tpu_custom_call" | custom-call | flops 6000000000 | bytes 1 | tf_op jit(solution)/shard_map/ends/pallas_call | solution.py:291
  30.5 4.0 %collective-permute-start.11 = (f32[12,80,128]{2,1,0:T(8,128)S(1)}, f32[12,80,128]{2,1,0:T(8,128)S(1)}, u32[]{:S(2)}, u32[]{:S(2)}) collective-permute-start(f32[12,80,128]{2,1,0:T(8,128)S(1)} %ends.3.refs_0_), channel_id=1, source_target_pairs={{32,0},{64,32},{96,64},{128,96},{160,128},{192,160},{224,192},{33,... | collective-permute-start | bytes 1474568 | tf_op jit(solution)/shard_map/ppermute | solution.py:323
  34.5 0.0 collective-permute-done.4.refs_1_
  34.5 2.5 %collective-permute-start.6 = (f32[8,80,128]{2,1,0:T(8,128)S(1)}, f32[8,80,128]{2,1,0:T(8,128)S(1)}, u32[]{:S(2)}, u32[]{:S(2)}) collective-permute-start(f32[8,80,128]{2,1,0:T(8,128)S(1)} %collective-permute-done.4.refs_1_), channel_id=1, source_target_pairs={{0,32},{64,96},{96,0},{128,160},{192,224},{224,128},{160,64},{1,33... | collective-permute-start | bytes 983048 | tf_op jit(solution)/shard_map/ppermute | solution.py:338
  37.1 1.3 %collective-permute-start.10 = (f32[24,80,128]{2,1,0:T(8,128)S(1)}, f32[24,80,128]{2,1,0:T(8,128)S(1)}, u32[]{:S(2)}, u32[]{:S(2)}) collective-permute-start(f32[24,80,128]{2,1,0:T(8,128)S(1)} %collective-permute-done.9.mid), channel_id=1, source_target_pairs={{224,96},{225,97},{226,98},{227,99},{228,100},{229,101},{230,102},... | collective-permute-start | bytes 2949128 | tf_op jit(solution)/shard_map/ppermute | solution.py:329
  38.4 0.0 collective-permute-done.from_partner
  38.4 6.5 %collective-permute-done.1.from_other = f32[20,48,128]{2,1,0:T(8,128)S(1)} collective-permute-done((f32[20,48,128]{2,1,0:T(8,128)}, f32[20,48,128]{2,1,0:T(8,128)S(1)}, u32[]{:S(2)}, u32[]{:S(2)}) %collective-permute-start.1) | collective-permute-done | bytes 491552 | tf_op jit(solution)/shard_map/ppermute | solution.py:318
  44.9 2.0 %ends.4.refs_0_ = f32[12,80,128]{2,1,0:T(8,128)S(1)} custom-call(f32[2,2,32,16,320]{4,3,2,1,0:T(8,128)S(1)} %bitcast.7, f32[2,32,16,320]{3,2,1,0:T(8,128)S(1)} %bitcast.17, f32[20,48,128]{2,1,0:T(8,128)S(1)} %copy-done.3, f32[20,48,128]{2,1,0:T(8,128)S(1)} %copy-done.4, f32[20,48,128]{2,1,0:T(8,128)S(1)} %collective-permute-done.from_partner, ...), custom_call_target="tpu_custom_call" | custom-call | flops 6000000000 | bytes 1 | tf_op jit(solution)/shard_map/ends/pallas_call | solution.py:291
  46.9 2.7 %collective-permute-start.8 = (f32[12,80,128]{2,1,0:T(8,128)S(1)}, f32[12,80,128]{2,1,0:T(8,128)S(1)}, u32[]{:S(2)}, u32[]{:S(2)}) collective-permute-start(f32[12,80,128]{2,1,0:T(8,128)S(1)} %ends.4.refs_0_), channel_id=1, source_target_pairs={{32,0},{64,32},{96,64},{128,96},{160,128},{192,160},{224,192},{33,... | collective-permute-start | bytes 1474568 | tf_op jit(solution)/shard_map/ppermute | solution.py:323
  49.7 0.0 copy-start.1
  49.7 1.4 %ends.5.refs_1_ = f32[8,80,128]{2,1,0:T(8,128)S(1)} custom-call(f32[2,2,32,16,320]{4,3,2,1,0:T(8,128)S(1)} %bitcast.8, f32[2,32,16,320]{3,2,1,0:T(8,128)S(1)} %bitcast.18, f32[20,48,128]{2,1,0:T(8,128)S(1)} %copy-done.3, f32[20,48,128]{2,1,0:T(8,128)S(1)} %copy-done.4, f32[20,48,128]{2,1,0:T(8,128)S(1)} %collective-permute-done.from_partner, ...), custom_call_target="tpu_custom_call" | custom-call | flops 6000000000 | bytes 1 | tf_op jit(solution)/shard_map/ends/pallas_call | solution.py:291
  51.0 2.5 %collective-permute-start.5 = (f32[8,80,128]{2,1,0:T(8,128)S(1)}, f32[8,80,128]{2,1,0:T(8,128)S(1)}, u32[]{:S(2)}, u32[]{:S(2)}) collective-permute-start(f32[8,80,128]{2,1,0:T(8,128)S(1)} %ends.5.refs_1_), channel_id=1, source_target_pairs={{32,0},{64,32},{96,64},{128,96},{160,128},{192,160},{224,192},{33,... | collective-permute-start | bytes 983048 | tf_op jit(solution)/shard_map/ppermute | solution.py:323
  53.5 0.0 collective-permute-done.6
  53.5 1.9 %collective-permute-start.7 = (f32[8,80,128]{2,1,0:T(8,128)S(1)}, f32[8,80,128]{2,1,0:T(8,128)S(1)}, u32[]{:S(2)}, u32[]{:S(2)}) collective-permute-start(f32[8,80,128]{2,1,0:T(8,128)S(1)} %collective-permute-done.6), channel_id=1, source_target_pairs={{0,32},{32,64},{96,0},{128,160},{160,192},{224,128},{64,96},{1,33}... | collective-permute-start | bytes 983048 | tf_op jit(solution)/shard_map/ppermute | solution.py:338
  55.5 0.0 collective-permute-done.11.end
  55.5 7.8 %collective-permute-done.10.refs_0_ = f32[24,80,128]{2,1,0:T(8,128)S(1)} collective-permute-done((f32[24,80,128]{2,1,0:T(8,128)S(1)}, f32[24,80,128]{2,1,0:T(8,128)S(1)}, u32[]{:S(2)}, u32[]{:S(2)}) %collective-permute-start.10) | collective-permute-done | bytes 983072 | tf_op jit(solution)/shard_map/ppermute | solution.py:329
  63.2 2.2 %subtract.3.refs_1_ = f32[4,32,16,320]{3,2,1,0:T(8,128)} custom-call(f32[4,32,16,320]{3,2,1,0:T(8,128)S(1)} %bitcast.11, f32[12,80,128]{2,1,0:T(8,128)S(1)} %collective-permute-done.11.end, f32[24,80,128]{2,1,0:T(8,128)S(1)} %collective-permute-done.9.mid, f32[24,80,128]{2,1,0:T(8,128)S(1)} %collective-permute-done.10.refs_0_, f32[8,80,128]{2,1,0:T(8,128)S(1)} %ends.5.refs_1_), custom_call_target="tpu_custom_call" | custom-call | flops 4000000000 | bytes 1 | tf_op jit(solution)/shard_map/subtract/pallas_call | solution.py:291
  65.4 0.0 collective-permute-done.8.end
  65.4 2.2 %subtract.4.refs_0_ = f32[4,32,16,320]{3,2,1,0:T(8,128)} custom-call(f32[4,32,16,320]{3,2,1,0:T(8,128)S(1)} %bitcast.12, f32[12,80,128]{2,1,0:T(8,128)S(1)} %collective-permute-done.8.end, f32[24,80,128]{2,1,0:T(8,128)S(1)} %collective-permute-done.9.mid, f32[24,80,128]{2,1,0:T(8,128)S(1)} %collective-permute-done.10.refs_0_, ...), custom_call_target="tpu_custom_call", output_to_operand_aliasing={{}: (4, {})} | custom-call | flops 4000000000 | bytes 1 | tf_op jit(solution)/shard_map/subtract/pallas_call | solution.py:291
  67.6 0.8 %collective-permute-done.5.end = f32[8,80,128]{2,1,0:T(8,128)S(1)} collective-permute-done((f32[8,80,128]{2,1,0:T(8,128)S(1)}, f32[8,80,128]{2,1,0:T(8,128)S(1)}, u32[]{:S(2)}, u32[]{:S(2)}) %collective-permute-start.5) | collective-permute-done | bytes 327712 | tf_op jit(solution)/shard_map/ppermute | solution.py:323
  68.4 0.0 collective-permute-done.7.mid
  68.4 1.4 %subtract.5 = f32[4,32,16,320]{3,2,1,0:T(8,128)} custom-call(f32[4,32,16,320]{3,2,1,0:T(8,128)S(1)} %bitcast.13, f32[8,80,128]{2,1,0:T(8,128)S(1)} %collective-permute-done.5.end, f32[8,80,128]{2,1,0:T(8,128)S(1)} %collective-permute-done.7.mid, f32[4,32,16,320]{3,2,1,0:T(8,128)} %subtract.4.refs_0_), custom_call_target="tpu_custom_call", output_to_operand_aliasing={{}: (3, {})} | custom-call | flops 4000000000 | bytes 1 | tf_op jit(solution)/shard_map/subtract/pallas_call | solution.py:291
  (18 shorter events, 0.0 us)
Async XLA Ops:
  8.7 28.4 %collective-permute-start.9 = (f32[24,80,128]{2,1,0:T(8,128)}, f32[24,80,128]{2,1,0:T(8,128)S(1)}, u32[]{:S(2)}, u32[]{:S(2)}) collective-permute-start(f32[24,80,128]{2,1,0:T(8,128)} %get-tuple-element.18.refs_0_), channel_id=1, source_target_pairs={{32,0},{64,32},{96,64},{128,224},{160,128},{192,160},{224,192},{33... | collective-permute-start | bytes 2949128 | tf_op jit(solution)/shard_map/ppermute | solution.py:330
  11.5 15.3 %collective-permute-start.2 = (f32[12,48,128]{2,1,0:T(8,128)}, f32[12,48,128]{2,1,0:T(8,128)S(1)}, u32[]{:S(2)}, u32[]{:S(2)}) collective-permute-start(f32[12,48,128]{2,1,0:T(8,128)} %get-tuple-element.25.partner), channel_id=1, source_target_pairs={{0,1},{1,0},{2,3},{3,2},{4,5},{5,4},{6,7},{7,6},{8,9},{9,8},{10,11... | collective-permute-start | bytes 884744 | tf_op jit(solution)/shard_map/ppermute | solution.py:318
  11.6 16.8 %collective-permute-start.3 = (f32[12,48,128]{2,1,0:T(8,128)}, f32[12,48,128]{2,1,0:T(8,128)S(1)}, u32[]{:S(2)}, u32[]{:S(2)}) collective-permute-start(f32[12,48,128]{2,1,0:T(8,128)} %get-tuple-element.26.other), channel_id=1, source_target_pairs={{0,31},{1,2},{2,1},{3,4},{4,3},{5,6},{6,5},{7,8},{8,7},{9,10},{10,... | collective-permute-start | bytes 884744 | tf_op jit(solution)/shard_map/ppermute | solution.py:318
  20.5 7.9 %copy-start = (f32[1,2,2,32,16,320]{5,4,3,2,1,0:T(8,128)S(1)}, f32[1,2,2,32,16,320]{5,4,3,2,1,0:T(8,128)}, u32[]{:S(2)}) copy-start(f32[1,2,2,32,16,320]{5,4,3,2,1,0:T(8,128)} %param.4) | copy-start | bytes 7864324
  20.5 7.9 %copy-start.2 = (f32[1,2,32,16,320]{4,3,2,1,0:T(8,128)S(1)}, f32[1,2,32,16,320]{4,3,2,1,0:T(8,128)}, u32[]{:S(2)}) copy-start(f32[1,2,32,16,320]{4,3,2,1,0:T(8,128)} %param.5) | copy-start | bytes 3932164
  20.5 7.9 %copy-start.5 = (f32[12,48,128]{2,1,0:T(8,128)S(1)}, f32[12,48,128]{2,1,0:T(8,128)}, u32[]{:S(2)}) copy-start(f32[12,48,128]{2,1,0:T(8,128)} %get-tuple-element.25.partner) | copy-start | bytes 884740
  20.5 7.9 %copy-start.6 = (f32[12,48,128]{2,1,0:T(8,128)S(1)}, f32[12,48,128]{2,1,0:T(8,128)}, u32[]{:S(2)}) copy-start(f32[12,48,128]{2,1,0:T(8,128)} %get-tuple-element.26.other) | copy-start | bytes 884740
  20.5 7.9 %copy-start.7 = (f32[24,4,8,384]{3,2,1,0:T(8,128)S(1)}, f32[24,4,8,384]{3,2,1,0:T(8,128)}, u32[]{:S(2)}) copy-start(f32[24,4,8,384]{3,2,1,0:T(8,128)} %get-tuple-element.24.image) | copy-start | bytes 3538948
  24.8 9.7 %collective-permute-start.4 = (f32[8,80,128]{2,1,0:T(8,128)}, f32[8,80,128]{2,1,0:T(8,128)S(1)}, u32[]{:S(2)}, u32[]{:S(2)}) collective-permute-start(f32[8,80,128]{2,1,0:T(8,128)} %get-tuple-element.27), channel_id=1, source_target_pairs={{32,64},{64,96},{96,0},{160,192},{192,224},{224,128},{128,160},{33... | collective-permute-start | bytes 983048 | tf_op jit(solution)/shard_map/ppermute | solution.py:338
  26.7 11.7 %collective-permute-start = (f32[20,48,128]{2,1,0:T(8,128)}, f32[20,48,128]{2,1,0:T(8,128)S(1)}, u32[]{:S(2)}, u32[]{:S(2)}) collective-permute-start(f32[20,48,128]{2,1,0:T(8,128)} %get-tuple-element.21.partner), channel_id=1, source_target_pairs={{0,1},{1,0},{2,3},{3,2},{4,5},{5,4},{6,7},{7,6},{8,9},{9,8},{10,11... | collective-permute-start | bytes 1474568 | tf_op jit(solution)/shard_map/ppermute | solution.py:318
  26.8 18.1 %collective-permute-start.1 = (f32[20,48,128]{2,1,0:T(8,128)}, f32[20,48,128]{2,1,0:T(8,128)S(1)}, u32[]{:S(2)}, u32[]{:S(2)}) collective-permute-start(f32[20,48,128]{2,1,0:T(8,128)} %get-tuple-element.22.other), channel_id=1, source_target_pairs={{0,31},{1,2},{2,1},{3,4},{4,3},{5,6},{6,5},{7,8},{8,7},{9,10},{10,... | collective-permute-start | bytes 1474568 | tf_op jit(solution)/shard_map/ppermute | solution.py:318
  28.4 16.5 %copy-start.3 = (f32[20,48,128]{2,1,0:T(8,128)S(1)}, f32[20,48,128]{2,1,0:T(8,128)}, u32[]{:S(2)}) copy-start(f32[20,48,128]{2,1,0:T(8,128)} %get-tuple-element.21.partner) | copy-start | bytes 1474564
  28.4 16.5 %copy-start.4 = (f32[20,48,128]{2,1,0:T(8,128)S(1)}, f32[20,48,128]{2,1,0:T(8,128)}, u32[]{:S(2)}) copy-start(f32[20,48,128]{2,1,0:T(8,128)} %get-tuple-element.22.other) | copy-start | bytes 1474564
  30.5 19.2 %copy-start.8 = (f32[8,4,8,384]{3,2,1,0:T(8,128)S(1)}, f32[8,4,8,384]{3,2,1,0:T(8,128)}, u32[]{:S(2)}) copy-start(f32[8,4,8,384]{3,2,1,0:T(8,128)} %get-tuple-element.23.image) | copy-start | bytes 1179652
  30.5 25.0 %collective-permute-start.11 = (f32[12,80,128]{2,1,0:T(8,128)S(1)}, f32[12,80,128]{2,1,0:T(8,128)S(1)}, u32[]{:S(2)}, u32[]{:S(2)}) collective-permute-start(f32[12,80,128]{2,1,0:T(8,128)S(1)} %ends.3.refs_0_), channel_id=1, source_target_pairs={{32,0},{64,32},{96,64},{128,96},{160,128},{192,160},{224,192},{33,... | collective-permute-start | bytes 1474568 | tf_op jit(solution)/shard_map/ppermute | solution.py:323
  34.5 19.0 %collective-permute-start.6 = (f32[8,80,128]{2,1,0:T(8,128)S(1)}, f32[8,80,128]{2,1,0:T(8,128)S(1)}, u32[]{:S(2)}, u32[]{:S(2)}) collective-permute-start(f32[8,80,128]{2,1,0:T(8,128)S(1)} %collective-permute-done.4.refs_1_), channel_id=1, source_target_pairs={{0,32},{64,96},{96,0},{128,160},{192,224},{224,128},{160,64},{1,33... | collective-permute-start | bytes 983048 | tf_op jit(solution)/shard_map/ppermute | solution.py:338
  37.1 26.1 %collective-permute-start.10 = (f32[24,80,128]{2,1,0:T(8,128)S(1)}, f32[24,80,128]{2,1,0:T(8,128)S(1)}, u32[]{:S(2)}, u32[]{:S(2)}) collective-permute-start(f32[24,80,128]{2,1,0:T(8,128)S(1)} %collective-permute-done.9.mid), channel_id=1, source_target_pairs={{224,96},{225,97},{226,98},{227,99},{228,100},{229,101},{230,102},... | collective-permute-start | bytes 2949128 | tf_op jit(solution)/shard_map/ppermute | solution.py:329
  46.9 18.5 %collective-permute-start.8 = (f32[12,80,128]{2,1,0:T(8,128)S(1)}, f32[12,80,128]{2,1,0:T(8,128)S(1)}, u32[]{:S(2)}, u32[]{:S(2)}) collective-permute-start(f32[12,80,128]{2,1,0:T(8,128)S(1)} %ends.4.refs_0_), channel_id=1, source_target_pairs={{32,0},{64,32},{96,64},{128,96},{160,128},{192,160},{224,192},{33,... | collective-permute-start | bytes 1474568 | tf_op jit(solution)/shard_map/ppermute | solution.py:323
  49.7 13.6 %copy-start.1 = (f32[1,4,32,16,320]{4,3,2,1,0:T(8,128)S(1)}, f32[1,4,32,16,320]{4,3,2,1,0:T(8,128)}, u32[]{:S(2)}) copy-start(f32[1,4,32,16,320]{4,3,2,1,0:T(8,128)} %param.3) | copy-start | bytes 7864324
  51.0 17.3 %collective-permute-start.5 = (f32[8,80,128]{2,1,0:T(8,128)S(1)}, f32[8,80,128]{2,1,0:T(8,128)S(1)}, u32[]{:S(2)}, u32[]{:S(2)}) collective-permute-start(f32[8,80,128]{2,1,0:T(8,128)S(1)} %ends.5.refs_1_), channel_id=1, source_target_pairs={{32,0},{64,32},{96,64},{128,96},{160,128},{192,160},{224,192},{33,... | collective-permute-start | bytes 983048 | tf_op jit(solution)/shard_map/ppermute | solution.py:323
  53.5 14.9 %collective-permute-start.7 = (f32[8,80,128]{2,1,0:T(8,128)S(1)}, f32[8,80,128]{2,1,0:T(8,128)S(1)}, u32[]{:S(2)}, u32[]{:S(2)}) collective-permute-start(f32[8,80,128]{2,1,0:T(8,128)S(1)} %collective-permute-done.6), channel_id=1, source_target_pairs={{0,32},{32,64},{96,0},{128,160},{160,192},{224,128},{64,96},{1,33}... | collective-permute-start | bytes 983048 | tf_op jit(solution)/shard_map/ppermute | solution.py:338

commit v6 on v4

--- a/solution.py
+++ b/solution.py
@@ -14,8 +14,8 @@
 FIRST_VMEM = 54
 MIB = 1024 * 1024
 GROUPS = ((0, 24, False), (24, 8, True))
-SPLIT = 12
-ENDS = ((0, 12, 0, 0), (12, 12, 0, 1), (24, 8, 1, 1))
+SPLIT = 16
+ENDS = ((0, 16, 0, 0), (16, 8, 0, 1), (24, 8, 1, 1))
 STEPS = ((0,), (0, 2))
 
 

time: 69.7 us -> 67.8 us (0.973)
  waiting for transfers between devices: 14.8 us -> 13.7 us
  starting transfers between devices: 30.2 us -> 29.5 us
    ppermute x2, waiting for transfers between devices: 4.41 us -> 3.01 us  [swapped(): lax.ppermute(other, 'tile', outer)]
    ppermute x1, waiting for transfers between devices: 2.11 us -> 1.37 us  [detour(): lax.ppermute(x, 'win', [(k + 1, n - 1 if k + 1 == n // 2 else k) for k in...]
  transfers between devices with their start and end apart: 12 -> 12, of which waited for: 4 -> 5; matrix products, arithmetic and copies ran while one was open for 0% -> 0% of each run, Pallas kernels for 20% -> 20%
where the time goes in v6:
time: 67.8 us; the launch traced here: 67.4 us
  starting transfers between devices  29.5 us (44%)
  Pallas kernels  23.8 us (35%)
  waiting for transfers between devices  13.7 us (20%)
    pallas_call x8, Pallas kernels, call(): pl.pallas_call(kernel, grid=(count // BLOCK,), in_specs=in_specs, out_spe...  23.8 us
    ppermute x2, starting transfers between devices, swapped(): lax.ppermute(other, 'tile', outer)  10.4 us
    ppermute x3, starting transfers between devices, to_preceding(): return lax.ppermute(x, 'win', [(k + 1, k) for k in range(n - 1)])  9.11 us
    ppermute x1, waiting for transfers between devices, detour(): return lax.ppermute(x, 'win', [(n - 1, n // 2 - 1)])  8.47 us
    ppermute x3, starting transfers between devices, long_way(): return lax.ppermute(x, 'win', [*pairs, side])  5.76 us
    ppermute x2, waiting for transfers between devices, swapped(): lax.ppermute(other, 'tile', outer)  3.01 us
    ppermute x1, starting transfers between devices, detour(): lax.ppermute(x, 'win', [(k + 1, n - 1 if k + 1 == n // 2 else k) for k in...  2.78 us
    ppermute x1, waiting for transfers between devices, detour(): lax.ppermute(x, 'win', [(k + 1, n - 1 if k + 1 == n // 2 else k) for k in...  1.37 us
  transfers between devices with their start and end apart: 12, of which 5 were waited for; matrix products, arithmetic and copies ran while one was open for 0% of the time, Pallas kernels for 20%

profile of v6, /device:TPU:6, one launch (start us, length us, event | category | flops | bytes accessed | tf_op | source)
XLA Modules:
  0.0 67.4 jit_solution(1807518124125621143)
XLA Ops:
  0.0 8.7 %interior.2 = (f32[24,80,128]{2,1,0:T(8,128)}, f32[24,4,8,384]{3,2,1,0:T(8,128)}, f32[16,48,128]{2,1,0:T(8,128)}, f32[16,48,128]{2,1,0:T(8,128)}, f32[16,48,128]{2,1,0:T(8,128)}, /*index=5*/f32[16,48,128]{2,1,0:T(8,128)}) custom-call(f32[4,32,16,320]{3,2,1,0:T(8,128)} %bitcast.9, f32[2,2,32,16,320]{4,3,2,1,0:T(8,128)} %bitcast.4, f32[2,32,16,320]{3,2,1,0:T(8,128)} %bitcast.14), custom_call_target="tpu_custom_call" | custom-call | flops 8000000000 | bytes 1 | tf_op jit(solution)/shard_map/interior/pallas_call | solution.py:291
  8.7 0.1 collective-permute-start.2
  8.8 8.9 %collective-permute-start.3 = (f32[16,48,128]{2,1,0:T(8,128)}, f32[16,48,128]{2,1,0:T(8,128)S(1)}, u32[]{:S(2)}, u32[]{:S(2)}) collective-permute-start(f32[16,48,128]{2,1,0:T(8,128)} %get-tuple-element.26.other), channel_id=1, source_target_pairs={{0,31},{1,2},{2,1},{3,4},{4,3},{5,6},{6,5},{7,8},{8,7},{9,10},{10,... | collective-permute-start | bytes 1179656 | tf_op jit(solution)/shard_map/ppermute | solution.py:318
  17.7 2.8 %collective-permute-start.9 = (f32[24,80,128]{2,1,0:T(8,128)}, f32[24,80,128]{2,1,0:T(8,128)S(1)}, u32[]{:S(2)}, u32[]{:S(2)}) collective-permute-start(f32[24,80,128]{2,1,0:T(8,128)} %get-tuple-element.18.refs_0_), channel_id=1, source_target_pairs={{32,0},{64,32},{96,64},{128,224},{160,128},{192,160},{224,192},{33... | collective-permute-start | bytes 2949128 | tf_op jit(solution)/shard_map/ppermute | solution.py:330
  20.4 0.0 copy-start
  20.5 0.0 copy-start.2
  20.5 0.0 copy-start.7
  20.5 4.3 %interior.3 = (f32[8,80,128]{2,1,0:T(8,128)}, f32[8,4,8,384]{3,2,1,0:T(8,128)}, f32[16,48,128]{2,1,0:T(8,128)}, f32[16,48,128]{2,1,0:T(8,128)}) custom-call(f32[4,32,16,320]{3,2,1,0:T(8,128)} %bitcast.10, f32[2,2,32,16,320]{4,3,2,1,0:T(8,128)} %bitcast.5, f32[2,32,16,320]{3,2,1,0:T(8,128)} %bitcast.15, ...), custom_call_target="tpu_custom_call", output_to_operand_aliasing={{2}: (4, {}), {3}: (5, {})} | custom-call | flops 8000000000 | bytes 1 | tf_op jit(solution)/shard_map/interior/pallas_call | solution.py:291
  24.8 1.9 %collective-permute-start.4 = (f32[8,80,128]{2,1,0:T(8,128)}, f32[8,80,128]{2,1,0:T(8,128)S(1)}, u32[]{:S(2)}, u32[]{:S(2)}) collective-permute-start(f32[8,80,128]{2,1,0:T(8,128)} %get-tuple-element.27), channel_id=1, source_target_pairs={{32,64},{64,96},{96,0},{160,192},{192,224},{224,128},{128,160},{33... | collective-permute-start | bytes 983048 | tf_op jit(solution)/shard_map/ppermute | solution.py:338
  26.7 0.1 collective-permute-start
  26.8 0.0 collective-permute-done.2.from_partner
  26.8 1.5 %collective-permute-start.1 = (f32[16,48,128]{2,1,0:T(8,128)}, f32[16,48,128]{2,1,0:T(8,128)S(1)}, u32[]{:S(2)}, u32[]{:S(2)}) collective-permute-start(f32[16,48,128]{2,1,0:T(8,128)} %get-tuple-element.22.other), channel_id=1, source_target_pairs={{0,31},{1,2},{2,1},{3,4},{4,3},{5,6},{6,5},{7,8},{8,7},{9,10},{10,... | collective-permute-start | bytes 1179656 | tf_op jit(solution)/shard_map/ppermute | solution.py:318
  28.4 0.0 collective-permute-done.3.from_other
  28.4 2.7 %ends.3.refs_0_ = f32[16,80,128]{2,1,0:T(8,128)S(1)} custom-call(f32[2,2,32,16,320]{4,3,2,1,0:T(8,128)S(1)} %bitcast.6, f32[2,32,16,320]{3,2,1,0:T(8,128)S(1)} %bitcast.16, f32[16,48,128]{2,1,0:T(8,128)S(1)} %copy-done.3, f32[16,48,128]{2,1,0:T(8,128)S(1)} %copy-done.4, f32[16,48,128]{2,1,0:T(8,128)S(1)} %collective-permute-done.2.from_partner, ...), custom_call_target="tpu_custom_call" | custom-call | flops 8000000000 | bytes 1 | tf_op jit(solution)/shard_map/ends/pallas_call | solution.py:291
  31.2 4.0 %collective-permute-start.11 = (f32[16,80,128]{2,1,0:T(8,128)S(1)}, f32[16,80,128]{2,1,0:T(8,128)S(1)}, u32[]{:S(2)}, u32[]{:S(2)}) collective-permute-start(f32[16,80,128]{2,1,0:T(8,128)S(1)} %ends.3.refs_0_), channel_id=1, source_target_pairs={{32,0},{64,32},{96,64},{128,96},{160,128},{192,160},{224,192},{33,... | collective-permute-start | bytes 1966088 | tf_op jit(solution)/shard_map/ppermute | solution.py:323
  35.2 1.9 %collective-permute-start.6 = (f32[8,80,128]{2,1,0:T(8,128)S(1)}, f32[8,80,128]{2,1,0:T(8,128)S(1)}, u32[]{:S(2)}, u32[]{:S(2)}) collective-permute-start(f32[8,80,128]{2,1,0:T(8,128)S(1)} %collective-permute-done.4.refs_1_), channel_id=1, source_target_pairs={{0,32},{64,96},{96,0},{128,160},{192,224},{224,128},{160,64},{1,33... | collective-permute-start | bytes 983048 | tf_op jit(solution)/shard_map/ppermute | solution.py:338
  37.2 1.4 %collective-permute-done.9.mid = f32[24,80,128]{2,1,0:T(8,128)S(1)} collective-permute-done((f32[24,80,128]{2,1,0:T(8,128)}, f32[24,80,128]{2,1,0:T(8,128)S(1)}, u32[]{:S(2)}, u32[]{:S(2)}) %collective-permute-start.9) | collective-permute-done | bytes 983072 | tf_op jit(solution)/shard_map/ppermute | solution.py:330
  38.5 1.3 %collective-permute-start.10 = (f32[24,80,128]{2,1,0:T(8,128)S(1)}, f32[24,80,128]{2,1,0:T(8,128)S(1)}, u32[]{:S(2)}, u32[]{:S(2)}) collective-permute-start(f32[24,80,128]{2,1,0:T(8,128)S(1)} %collective-permute-done.9.mid), channel_id=1, source_target_pairs={{224,96},{225,97},{226,98},{227,99},{228,100},{229,101},{230,102},... | collective-permute-start | bytes 2949128 | tf_op jit(solution)/shard_map/ppermute | solution.py:329
  39.8 0.0 collective-permute-done.from_partner
  39.8 3.0 %collective-permute-done.1.from_other = f32[16,48,128]{2,1,0:T(8,128)S(1)} collective-permute-done((f32[16,48,128]{2,1,0:T(8,128)}, f32[16,48,128]{2,1,0:T(8,128)S(1)}, u32[]{:S(2)}, u32[]{:S(2)}) %collective-permute-start.1) | collective-permute-done | bytes 393248 | tf_op jit(solution)/shard_map/ppermute | solution.py:318
  42.8 1.4 %ends.4.refs_0_ = f32[8,80,128]{2,1,0:T(8,128)S(1)} custom-call(f32[2,2,32,16,320]{4,3,2,1,0:T(8,128)S(1)} %bitcast.7, f32[2,32,16,320]{3,2,1,0:T(8,128)S(1)} %bitcast.17, f32[16,48,128]{2,1,0:T(8,128)S(1)} %copy-done.5, f32[16,48,128]{2,1,0:T(8,128)S(1)} %copy-done.6, f32[16,48,128]{2,1,0:T(8,128)S(1)} %collective-permute-done.from_partner, ...), custom_call_target="tpu_custom_call" | custom-call | flops 8000000000 | bytes 1 | tf_op jit(solution)/shard_map/ends/pallas_call | solution.py:291
  44.2 2.6 %collective-permute-start.8 = (f32[8,80,128]{2,1,0:T(8,128)S(1)}, f32[8,80,128]{2,1,0:T(8,128)S(1)}, u32[]{:S(2)}, u32[]{:S(2)}) collective-permute-start(f32[8,80,128]{2,1,0:T(8,128)S(1)} %ends.4.refs_0_), channel_id=1, source_target_pairs={{32,0},{64,32},{96,64},{128,96},{160,128},{192,160},{224,192},{33,... | collective-permute-start | bytes 983048 | tf_op jit(solution)/shard_map/ppermute | solution.py:323
  46.8 0.0 copy-start.1
  46.8 1.4 %ends.5.refs_1_ = f32[8,80,128]{2,1,0:T(8,128)S(1)} custom-call(f32[2,2,32,16,320]{4,3,2,1,0:T(8,128)S(1)} %bitcast.8, f32[2,32,16,320]{3,2,1,0:T(8,128)S(1)} %bitcast.18, f32[16,48,128]{2,1,0:T(8,128)S(1)} %copy-done.5, f32[16,48,128]{2,1,0:T(8,128)S(1)} %copy-done.6, f32[16,48,128]{2,1,0:T(8,128)S(1)} %collective-permute-done.from_partner, ...), custom_call_target="tpu_custom_call" | custom-call | flops 8000000000 | bytes 1 | tf_op jit(solution)/shard_map/ends/pallas_call | solution.py:291
  48.1 2.5 %collective-permute-start.5 = (f32[8,80,128]{2,1,0:T(8,128)S(1)}, f32[8,80,128]{2,1,0:T(8,128)S(1)}, u32[]{:S(2)}, u32[]{:S(2)}) collective-permute-start(f32[8,80,128]{2,1,0:T(8,128)S(1)} %ends.5.refs_1_), channel_id=1, source_target_pairs={{32,0},{64,32},{96,64},{128,96},{160,128},{192,160},{224,192},{33,... | collective-permute-start | bytes 983048 | tf_op jit(solution)/shard_map/ppermute | solution.py:323
  50.7 1.9 %collective-permute-start.7 = (f32[8,80,128]{2,1,0:T(8,128)S(1)}, f32[8,80,128]{2,1,0:T(8,128)S(1)}, u32[]{:S(2)}, u32[]{:S(2)}) collective-permute-start(f32[8,80,128]{2,1,0:T(8,128)S(1)} %collective-permute-done.6), channel_id=1, source_target_pairs={{0,32},{32,64},{96,0},{128,160},{160,192},{224,128},{64,96},{1,33}... | collective-permute-start | bytes 983048 | tf_op jit(solution)/shard_map/ppermute | solution.py:338
  52.6 0.4 collective-permute-done.11.end
  53.0 8.5 %collective-permute-done.10.refs_0_ = f32[24,80,128]{2,1,0:T(8,128)S(1)} collective-permute-done((f32[24,80,128]{2,1,0:T(8,128)S(1)}, f32[24,80,128]{2,1,0:T(8,128)S(1)}, u32[]{:S(2)}, u32[]{:S(2)}) %collective-permute-start.10) | collective-permute-done | bytes 983072 | tf_op jit(solution)/shard_map/ppermute | solution.py:329
  61.4 2.5 %subtract.3.refs_1_ = f32[4,32,16,320]{3,2,1,0:T(8,128)} custom-call(f32[4,32,16,320]{3,2,1,0:T(8,128)S(1)} %bitcast.11, f32[16,80,128]{2,1,0:T(8,128)S(1)} %collective-permute-done.11.end, f32[24,80,128]{2,1,0:T(8,128)S(1)} %collective-permute-done.9.mid, f32[24,80,128]{2,1,0:T(8,128)S(1)} %collective-permute-done.10.refs_0_, f32[8,80,128]{2,1,0:T(8,128)S(1)} %ends.5.refs_1_), custom_call_target="tpu_custom_call" | custom-call | flops 8000000000 | bytes 1 | tf_op jit(solution)/shard_map/subtract/pallas_call | solution.py:291
  64.0 1.4 %subtract.4.refs_0_ = f32[4,32,16,320]{3,2,1,0:T(8,128)} custom-call(f32[4,32,16,320]{3,2,1,0:T(8,128)S(1)} %bitcast.12, f32[8,80,128]{2,1,0:T(8,128)S(1)} %collective-permute-done.8.end, f32[24,80,128]{2,1,0:T(8,128)S(1)} %collective-permute-done.9.mid, f32[24,80,128]{2,1,0:T(8,128)S(1)} %collective-permute-done.10.refs_0_, ...), custom_call_target="tpu_custom_call", output_to_operand_aliasing={{}: (4, {})} | custom-call | flops 8000000000 | bytes 1 | tf_op jit(solution)/shard_map/subtract/pallas_call | solution.py:291
  65.4 0.5 collective-permute-done.5.end
  65.9 1.4 %subtract.5 = f32[4,32,16,320]{3,2,1,0:T(8,128)} custom-call(f32[4,32,16,320]{3,2,1,0:T(8,128)S(1)} %bitcast.13, f32[8,80,128]{2,1,0:T(8,128)S(1)} %collective-permute-done.5.end, f32[8,80,128]{2,1,0:T(8,128)S(1)} %collective-permute-done.7.mid, f32[4,32,16,320]{3,2,1,0:T(8,128)} %subtract.4.refs_0_), custom_call_target="tpu_custom_call", output_to_operand_aliasing={{}: (3, {})} | custom-call | flops 8000000000 | bytes 1 | tf_op jit(solution)/shard_map/subtract/pallas_call | solution.py:291
  (18 shorter events, 0.0 us)
Async XLA Ops:
  8.7 18.1 %collective-permute-start.2 = (f32[16,48,128]{2,1,0:T(8,128)}, f32[16,48,128]{2,1,0:T(8,128)S(1)}, u32[]{:S(2)}, u32[]{:S(2)}) collective-permute-start(f32[16,48,128]{2,1,0:T(8,128)} %get-tuple-element.25.partner), channel_id=1, source_target_pairs={{0,1},{1,0},{2,3},{3,2},{4,5},{5,4},{6,7},{7,6},{8,9},{9,8},{10,11... | collective-permute-start | bytes 1179656 | tf_op jit(solution)/shard_map/ppermute | solution.py:318
  8.8 19.6 %collective-permute-start.3 = (f32[16,48,128]{2,1,0:T(8,128)}, f32[16,48,128]{2,1,0:T(8,128)S(1)}, u32[]{:S(2)}, u32[]{:S(2)}) collective-permute-start(f32[16,48,128]{2,1,0:T(8,128)} %get-tuple-element.26.other), channel_id=1, source_target_pairs={{0,31},{1,2},{2,1},{3,4},{4,3},{5,6},{6,5},{7,8},{8,7},{9,10},{10,... | collective-permute-start | bytes 1179656 | tf_op jit(solution)/shard_map/ppermute | solution.py:318
  17.7 20.9 %collective-permute-start.9 = (f32[24,80,128]{2,1,0:T(8,128)}, f32[24,80,128]{2,1,0:T(8,128)S(1)}, u32[]{:S(2)}, u32[]{:S(2)}) collective-permute-start(f32[24,80,128]{2,1,0:T(8,128)} %get-tuple-element.18.refs_0_), channel_id=1, source_target_pairs={{32,0},{64,32},{96,64},{128,224},{160,128},{192,160},{224,192},{33... | collective-permute-start | bytes 2949128 | tf_op jit(solution)/shard_map/ppermute | solution.py:330
  20.4 7.9 %copy-start = (f32[1,2,2,32,16,320]{5,4,3,2,1,0:T(8,128)S(1)}, f32[1,2,2,32,16,320]{5,4,3,2,1,0:T(8,128)}, u32[]{:S(2)}) copy-start(f32[1,2,2,32,16,320]{5,4,3,2,1,0:T(8,128)} %param.4) | copy-start | bytes 7864324
  20.5 7.9 %copy-start.2 = (f32[1,2,32,16,320]{4,3,2,1,0:T(8,128)S(1)}, f32[1,2,32,16,320]{4,3,2,1,0:T(8,128)}, u32[]{:S(2)}) copy-start(f32[1,2,32,16,320]{4,3,2,1,0:T(8,128)} %param.5) | copy-start | bytes 3932164
  20.5 7.9 %copy-start.3 = (f32[16,48,128]{2,1,0:T(8,128)S(1)}, f32[16,48,128]{2,1,0:T(8,128)}, u32[]{:S(2)}) copy-start(f32[16,48,128]{2,1,0:T(8,128)} %get-tuple-element.25.partner) | copy-start | bytes 1179652
  20.5 7.9 %copy-start.4 = (f32[16,48,128]{2,1,0:T(8,128)S(1)}, f32[16,48,128]{2,1,0:T(8,128)}, u32[]{:S(2)}) copy-start(f32[16,48,128]{2,1,0:T(8,128)} %get-tuple-element.26.other) | copy-start | bytes 1179652
  20.5 7.9 %copy-start.7 = (f32[24,4,8,384]{3,2,1,0:T(8,128)S(1)}, f32[24,4,8,384]{3,2,1,0:T(8,128)}, u32[]{:S(2)}) copy-start(f32[24,4,8,384]{3,2,1,0:T(8,128)} %get-tuple-element.24.image) | copy-start | bytes 3538948
  24.8 10.4 %collective-permute-start.4 = (f32[8,80,128]{2,1,0:T(8,128)}, f32[8,80,128]{2,1,0:T(8,128)S(1)}, u32[]{:S(2)}, u32[]{:S(2)}) collective-permute-start(f32[8,80,128]{2,1,0:T(8,128)} %get-tuple-element.27), channel_id=1, source_target_pairs={{32,64},{64,96},{96,0},{160,192},{192,224},{224,128},{128,160},{33... | collective-permute-start | bytes 983048 | tf_op jit(solution)/shard_map/ppermute | solution.py:338
  26.7 13.1 %collective-permute-start = (f32[16,48,128]{2,1,0:T(8,128)}, f32[16,48,128]{2,1,0:T(8,128)S(1)}, u32[]{:S(2)}, u32[]{:S(2)}) collective-permute-start(f32[16,48,128]{2,1,0:T(8,128)} %get-tuple-element.21.partner), channel_id=1, source_target_pairs={{0,1},{1,0},{2,3},{3,2},{4,5},{5,4},{6,7},{7,6},{8,9},{9,8},{10,11... | collective-permute-start | bytes 1179656 | tf_op jit(solution)/shard_map/ppermute | solution.py:318
  26.8 16.0 %collective-permute-start.1 = (f32[16,48,128]{2,1,0:T(8,128)}, f32[16,48,128]{2,1,0:T(8,128)S(1)}, u32[]{:S(2)}, u32[]{:S(2)}) collective-permute-start(f32[16,48,128]{2,1,0:T(8,128)} %get-tuple-element.22.other), channel_id=1, source_target_pairs={{0,31},{1,2},{2,1},{3,4},{4,3},{5,6},{6,5},{7,8},{8,7},{9,10},{10,... | collective-permute-start | bytes 1179656 | tf_op jit(solution)/shard_map/ppermute | solution.py:318
  28.4 14.4 %copy-start.5 = (f32[16,48,128]{2,1,0:T(8,128)S(1)}, f32[16,48,128]{2,1,0:T(8,128)}, u32[]{:S(2)}) copy-start(f32[16,48,128]{2,1,0:T(8,128)} %get-tuple-element.21.partner) | copy-start | bytes 1179652
  28.4 14.4 %copy-start.6 = (f32[16,48,128]{2,1,0:T(8,128)S(1)}, f32[16,48,128]{2,1,0:T(8,128)}, u32[]{:S(2)}) copy-start(f32[16,48,128]{2,1,0:T(8,128)} %get-tuple-element.22.other) | copy-start | bytes 1179652
  31.2 15.6 %copy-start.8 = (f32[8,4,8,384]{3,2,1,0:T(8,128)S(1)}, f32[8,4,8,384]{3,2,1,0:T(8,128)}, u32[]{:S(2)}) copy-start(f32[8,4,8,384]{3,2,1,0:T(8,128)} %get-tuple-element.23.image) | copy-start | bytes 1179652
  31.2 21.8 %collective-permute-start.11 = (f32[16,80,128]{2,1,0:T(8,128)S(1)}, f32[16,80,128]{2,1,0:T(8,128)S(1)}, u32[]{:S(2)}, u32[]{:S(2)}) collective-permute-start(f32[16,80,128]{2,1,0:T(8,128)S(1)} %ends.3.refs_0_), channel_id=1, source_target_pairs={{32,0},{64,32},{96,64},{128,96},{160,128},{192,160},{224,192},{33,... | collective-permute-start | bytes 1966088 | tf_op jit(solution)/shard_map/ppermute | solution.py:323
  35.2 15.4 %collective-permute-start.6 = (f32[8,80,128]{2,1,0:T(8,128)S(1)}, f32[8,80,128]{2,1,0:T(8,128)S(1)}, u32[]{:S(2)}, u32[]{:S(2)}) collective-permute-start(f32[8,80,128]{2,1,0:T(8,128)S(1)} %collective-permute-done.4.refs_1_), channel_id=1, source_target_pairs={{0,32},{64,96},{96,0},{128,160},{192,224},{224,128},{160,64},{1,33... | collective-permute-start | bytes 983048 | tf_op jit(solution)/shard_map/ppermute | solution.py:338
  38.5 22.9 %collective-permute-start.10 = (f32[24,80,128]{2,1,0:T(8,128)S(1)}, f32[24,80,128]{2,1,0:T(8,128)S(1)}, u32[]{:S(2)}, u32[]{:S(2)}) collective-permute-start(f32[24,80,128]{2,1,0:T(8,128)S(1)} %collective-permute-done.9.mid), channel_id=1, source_target_pairs={{224,96},{225,97},{226,98},{227,99},{228,100},{229,101},{230,102},... | collective-permute-start | bytes 2949128 | tf_op jit(solution)/shard_map/ppermute | solution.py:329
  44.2 19.8 %collective-permute-start.8 = (f32[8,80,128]{2,1,0:T(8,128)S(1)}, f32[8,80,128]{2,1,0:T(8,128)S(1)}, u32[]{:S(2)}, u32[]{:S(2)}) collective-permute-start(f32[8,80,128]{2,1,0:T(8,128)S(1)} %ends.4.refs_0_), channel_id=1, source_target_pairs={{32,0},{64,32},{96,64},{128,96},{160,128},{192,160},{224,192},{33,... | collective-permute-start | bytes 983048 | tf_op jit(solution)/shard_map/ppermute | solution.py:323
  46.8 14.7 %copy-start.1 = (f32[1,4,32,16,320]{4,3,2,1,0:T(8,128)S(1)}, f32[1,4,32,16,320]{4,3,2,1,0:T(8,128)}, u32[]{:S(2)}) copy-start(f32[1,4,32,16,320]{4,3,2,1,0:T(8,128)} %param.3) | copy-start | bytes 7864324
  48.1 17.8 %collective-permute-start.5 = (f32[8,80,128]{2,1,0:T(8,128)S(1)}, f32[8,80,128]{2,1,0:T(8,128)S(1)}, u32[]{:S(2)}, u32[]{:S(2)}) collective-permute-start(f32[8,80,128]{2,1,0:T(8,128)S(1)} %ends.5.refs_1_), channel_id=1, source_target_pairs={{32,0},{64,32},{96,64},{128,96},{160,128},{192,160},{224,192},{33,... | collective-permute-start | bytes 983048 | tf_op jit(solution)/shard_map/ppermute | solution.py:323
  50.7 15.2 %collective-permute-start.7 = (f32[8,80,128]{2,1,0:T(8,128)S(1)}, f32[8,80,128]{2,1,0:T(8,128)S(1)}, u32[]{:S(2)}, u32[]{:S(2)}) collective-permute-start(f32[8,80,128]{2,1,0:T(8,128)S(1)} %collective-permute-done.6), channel_id=1, source_target_pairs={{0,32},{32,64},{96,0},{128,160},{160,192},{224,128},{64,96},{1,33}... | collective-permute-start | bytes 983048 | tf_op jit(solution)/shard_map/ppermute | solution.py:338
